TPU v7x, 256 devices: a whole 4x4x8 slice. The times are simulated.
256 devices in a mesh: img: 8 (over y_lo, x), txt: 32 (over z, y_hi, core).
Axes of the slice: x: 4, y: 4 (y_hi: 2, y_lo: 2; y = y_hi * 2 + y_lo), z: 8, core: 2. Of those that a mesh axis runs over, the one named last changes fastest.
Arguments:
- images: bfloat16 [12288, 1024], P('img'), may hold values from -160 to 160
- texts: bfloat16 [12288, 1024], P('txt'), may hold values from -6 to 6
- match: int32 [12288], P('img'), may hold values from 0 to 12287, each once
Outputs:
- image_grad: float32 [12288, 1024], P(('img', 'txt'))
- text_grad: float32 [12288, 1024], P(('txt', 'img'))
Inputs may be any that keep to these rules, and one draw needn't show every extreme that they name: `match`: each text index appears exactly once.
All inputs are finite; a program needn't handle non-finite values.
Results may differ from a plain program's by a relative error of at most 0.0019.
Values may be sent and summed in bfloat16 or wider, within the bound.
No kernel may reach another device: no remote copies, remote signals or barrier semaphores. Data moves between devices by JAX's collectives and lax.ppermute only.
A program may use at most 128 MiB of HBM per device.

v0:
```python
import math

import jax
import jax.numpy as jnp
from jax import lax
from jax.sharding import PartitionSpec as P


def shards(images, texts, match):
    feature_width = images.shape[1]
    scale_factor = 2.0 / math.sqrt(feature_width)
    text_rows = texts.shape[0]
    logits = (
        lax.dot_general(images, texts, (((1,), (1,)), ((), ())), preferred_element_type=jnp.float32)
        * scale_factor
    )
    local_row_max = jnp.max(logits, axis=1)
    local_col_max = jnp.max(logits, axis=0)
    row_top = lax.pmax(local_row_max, "txt")
    col_top = lax.pmax(local_col_max, "img")
    row_sum_all = lax.psum(jnp.sum(jnp.exp(logits - row_top[:, None]), axis=1), "txt")
    col_sum_all = lax.psum(jnp.sum(jnp.exp(logits - col_top[None, :]), axis=0), "img")
    row_lse = row_top + jnp.log(row_sum_all)
    col_lse = col_top + jnp.log(col_sum_all)
    column_ids = lax.axis_index("txt") * text_rows + jnp.arange(text_rows, dtype=jnp.int32)
    paired = (match[:, None] == column_ids[None, :]).astype(jnp.float32)
    weights = (
        0.5 * (jnp.exp(logits - row_lse[:, None]) + jnp.exp(logits - col_lse[None, :])) - paired
    ).astype(jnp.bfloat16)
    image_grad = lax.psum_scatter(
        jnp.dot(weights, texts, preferred_element_type=jnp.float32),
        "txt",
        scatter_dimension=0,
        tiled=True,
    )
    text_grad = lax.psum_scatter(
        lax.dot_general(
            weights, images, (((0,), (0,)), ((), ())), preferred_element_type=jnp.float32
        ),
        "img",
        scatter_dimension=0,
        tiled=True,
    )
    return (image_grad, text_grad)


def solution(mesh):
    in_specs = (P("img", None), P("txt", None), P("img"))
    out_specs = (P(("img", "txt"), None), P(("txt", "img"), None))
    return jax.shard_map(shards, mesh=mesh, in_specs=in_specs, out_specs=out_specs, check_vma=False)
```

profile of v0, /device:TPU:2, one launch (start us, length us, event | category | flops | bytes accessed | tf_op | source)
XLA Modules:
  0.0 381.1 jit_solution(4223665578179730419)
XLA Ops:
  7.2 0.0 copy-start
  7.2 0.0 reduce-scatter.5.cloned.1.call-start
  7.2 1.8 copy-done
  9.1 4.4 %fusion.2 = (f32[1536]{0:T(1024)S(1)}, f32[384]{0:T(512)S(1)}, f32[1536,384]{1,0:T(8,128)}) fusion(bf16[1536,1024]{1,0:T(8,128)(2,1)S(1)} %copy-done, bf16[384,1024]{1,0:T(8,128)(2,1)} %param.4), kind=kOutput, calls=%fused_computation.9 | convolution fusion | flops 1209727104 | bytes 6299136 | tf_op jit(solution)/shard_map/dot_general | solution.py:14
  13.4 0.0 copy-start.1
  13.4 73.9 %pmax.14 = f32[1536]{0:T(1024)S(1)} all-reduce(f32[1536]{0:T(1024)S(1)} %get-tuple-element.4), channel_id=1, replica_groups=mesh['img'=8,'txt'=32] {'txt'}, use_global_device_ids=true, to_apply=%region_1.0 | all-reduce | flops 1536 | bytes 12288 | tf_op jit(solution)/shard_map/pmax | solution.py:19
  87.4 16.5 %pmax.15 = f32[384]{0:T(512)S(1)} all-reduce(f32[384]{0:T(512)S(1)} %get-tuple-element.5), channel_id=1, replica_groups=mesh['img'=8,'txt'=32] {'img'}, use_global_device_ids=true, to_apply=%region_5.0 | all-reduce | flops 384 | bytes 3072 | tf_op jit(solution)/shard_map/pmax | solution.py:20
  103.9 2.9 exponential_reduce_fusion.1
  106.7 66.0 %psum.14 = f32[1536]{0:T(1024)S(1)} all-reduce(f32[1536]{0:T(1024)S(1)} %get-tuple-element.2), channel_id=1, replica_groups=mesh['img'=8,'txt'=32] {'txt'}, use_global_device_ids=true, to_apply=%region_3.0 | all-reduce | flops 1536 | bytes 12288 | tf_op jit(solution)/shard_map/psum | solution.py:21
  172.8 18.9 %psum.15 = f32[384]{0:T(512)S(1)} all-reduce(f32[384]{0:T(512)S(1)} %get-tuple-element.3), channel_id=1, replica_groups=mesh['img'=8,'txt'=32] {'img'}, use_global_device_ids=true, to_apply=%region_7.0 | all-reduce | flops 384 | bytes 3072 | tf_op jit(solution)/shard_map/psum | solution.py:22
  191.7 0.0 copy-done.1
  191.7 4.6 %fusion = f32[384,1024]{1,0:T(8,128)} fusion(bf16[1536,1024]{1,0:T(8,128)(2,1)S(1)} %copy-done, f32[1536,384]{1,0:T(8,128)} %get-tuple-element.6, s32[384]{0:T(512)S(1)} %iota_add_fusion, f32[384]{0:T(512)S(1)} %log_add_fusion.1, f32[1536]{0:T(1024)S(1)} %log_add_fusion, s32[1536]{0:T(1024)S(1)} %copy-done.1), kind=kOutput, calls=%fused_computation.7 | convolution fusion | flops 1212678144 | bytes 7093248 | tf_op jit(solution)/shard_map/dot_general | solution.py:37
  196.3 0.0 reduce-scatter.5.cloned.1.call-update
  196.3 0.0 reduce-scatter.3.cloned.1.call-start
  196.4 6.6 %fusion.1 = f32[1536,1024]{1,0:T(8,128)} fusion(bf16[384,1024]{1,0:T(8,128)(2,1)} %param.4, f32[1536,384]{1,0:T(8,128)} %get-tuple-element.6, s32[384]{0:T(512)S(1)} %iota_add_fusion, f32[384]{0:T(512)S(1)} %log_add_fusion.1, f32[1536]{0:T(1024)S(1)} %log_add_fusion, s32[1536]{0:T(1024)S(1)} %copy-done.1), kind=kOutput, calls=%fused_computation.8 | convolution fusion | flops 1212678144 | bytes 9452544 | tf_op jit(solution)/shard_map/dot_general | solution.py:31
  202.9 0.0 reduce-scatter.3.cloned.1.call-update
  203.0 27.8 %reduce-scatter.5.cloned.1.call-done = f32[48,1024]{1,0:T(8,128)} async-done(((f32[384,1024]{1,0:T(8,128)}), f32[48,1024]{1,0:T(8,128)}) %reduce-scatter.5.cloned.1.call-update) | async-done | bytes 196624 | tf_op jit(solution)/shard_map/reduce_scatter | solution.py:36
  230.7 143.6 %reduce-scatter.3.cloned.1.call-done = f32[48,1024]{1,0:T(8,128)} async-done(((f32[1536,1024]{1,0:T(8,128)}), f32[48,1024]{1,0:T(8,128)}) %reduce-scatter.3.cloned.1.call-update) | async-done | bytes 196624 | tf_op jit(solution)/shard_map/reduce_scatter | solution.py:30
  (3 shorter events, 0.0 us)
Async XLA Ops:
  7.2 1.9 copy-start
  7.2 223.5 %reduce-scatter.5.cloned.1.call-start = ((), (), s32[]{:S(2)}) async-start(), calls=%async_computation.3 | async-start | bytes 1769472 | tf_op jit(solution)/shard_map/reduce_scatter | solution.py:36
  13.4 178.2 %copy-start.1 = (s32[1536]{0:T(1024)S(1)}, s32[1536]{0:T(1024)}, u32[]{:S(2)}) copy-start(s32[1536]{0:T(1024)} %param.5) | copy-start | bytes 18436
  196.3 178.0 %reduce-scatter.3.cloned.1.call-start = ((), (), s32[]{:S(2)}) async-start(), calls=%async_computation.2 | async-start | bytes 6488064 | tf_op jit(solution)/shard_map/reduce_scatter | solution.py:30
Sparse Core Ops, SparseCore 0:
  196.4 34.2 reduce-scatter.4
  235.6 138.6 reduce-scatter.2
where the time goes:
time: 381 us
  blocking collectives  175 us (46%)
  waiting for transfers between devices  171 us (45%)
  matrix products  15.6 us (4%)
  between operations  14.1 us (4%)
    reduce_scatter x1, waiting for transfers between devices, shards(): lax.psum_scatter(jnp.dot(weights, texts, preferred_element_type=jnp.float...  144 us
    pmax x1, blocking collectives, shards(): row_top = lax.pmax(local_row_max, 'txt')  73.9 us
    psum x1, blocking collectives, shards(): lax.psum(jnp.sum(jnp.exp(logits - row_top[:, None]), axis=1), 'txt')  66 us
    reduce_scatter x1, waiting for transfers between devices, shards(): lax.psum_scatter(lax.dot_general(weights, images, (((0,), (0,)), ((), ())...  27.8 us
    psum x1, blocking collectives, shards(): lax.psum(jnp.sum(jnp.exp(logits - col_top[None, :]), axis=0), 'img')  18.9 us
    pmax x1, blocking collectives, shards(): col_top = lax.pmax(local_col_max, 'img')  16.5 us
  transfers between devices with their start and end apart: 2, of which 2 were waited for; matrix products, arithmetic and copies ran while one was open for 2% of the time, Pallas kernels for 0%

commit v1 on v0

v1 whole, which is shorter than its diff:
```python
import math

import jax
import jax.numpy as jnp
from jax import lax
from jax.sharding import Mesh, PartitionSpec as P

AXES = ("ylo", "x", "z", "yhi", "core")
IMG = ("ylo", "x")
TXT = ("z", "yhi", "core")
F32 = jnp.float32


def swap(value, axis):
    return lax.ppermute(value, axis, [(0, 1), (1, 0)])


def spread(value, axes, n):
    copies = jnp.broadcast_to(value[None], (n,) + value.shape)
    return lax.all_to_all(copies, axes, 0, 0, tiled=True)


def combine(values):
    top = jnp.max(values, axis=0)
    return top + jnp.log(jnp.sum(jnp.exp(values - top[None]), axis=0))


def lse(logits, axis):
    top = jnp.max(logits, axis=axis, keepdims=True)
    return jnp.squeeze(top, axis) + jnp.log(jnp.sum(jnp.exp(logits - top), axis=axis))


def shards(images, texts, match):
    width = images.shape[1]
    scale = 2.0 / math.sqrt(width)
    rows, cols = images.shape[0], texts.shape[0]
    z, yhi, core = (lax.axis_index(a) for a in TXT)
    place = yhi * 2 + core

    other_yhi = swap(texts, "yhi")
    other_core = swap(texts, "core")

    logits = scale * lax.dot_general(
        images, texts, (((1,), (1,)), ((), ())), preferred_element_type=F32
    )
    row_part, col_part = lse(logits, 1), lse(logits, 0)
    row_part = combine(jnp.stack([row_part, swap(row_part, "core")]))
    col_lse = combine(spread(col_part, IMG, 8))
    row_lse = combine(spread(row_part, ("z", "yhi"), 16))

    other_both = swap(other_yhi, "core")
    col_pair = jnp.stack([col_lse, swap(col_lse, "core")])
    col_four = jnp.concatenate([col_pair, swap(col_pair, "yhi")])

    def weigh(logits, row_lse, col_lse, match, ids):
        paired = (match[:, None] == ids[None, :]).astype(F32)
        total = jnp.exp(logits - row_lse[:, None]) + jnp.exp(logits - col_lse[None, :])
        return (0.5 * total - paired).astype(jnp.bfloat16)

    ids = jnp.arange(cols, dtype=jnp.int32)
    weights = weigh(logits, row_lse, col_lse, match, (z * 4 + place) * cols + ids)
    text_part = lax.dot_general(
        weights, images, (((0,), (0,)), ((), ())), preferred_element_type=F32
    ).astype(jnp.bfloat16)
    text_parts = lax.all_to_all(text_part, IMG, 0, 0, tiled=True)
    text_grad = jnp.sum(text_parts.astype(F32).reshape(8, cols // 8, width), axis=0)

    def own(value):
        split = value.reshape((8, 4, rows // 32) + value.shape[1:])
        picked = lax.dynamic_index_in_dim(split, place, 1, keepdims=False)
        return picked.reshape((rows // 4,) + value.shape[1:])

    four = jnp.concatenate([texts, other_core, other_yhi, other_both])
    own_images = own(images)
    own_logits = scale * lax.dot_general(
        own_images, four, (((1,), (1,)), ((), ())), preferred_element_type=F32
    )
    four_ids = jnp.concatenate([(z * 4 + (place ^ k)) * cols + ids for k in range(4)])
    own_weights = weigh(own_logits, own(row_lse), col_four.reshape(-1), own(match), four_ids)
    image_part = jnp.dot(own_weights, four, preferred_element_type=F32).astype(jnp.bfloat16)
    image_parts = lax.all_to_all(image_part, "z", 0, 0, tiled=True)
    image_grad = jnp.sum(image_parts.astype(F32).reshape(8, rows // 32, width), axis=0)
    return image_grad, text_grad


def solution(mesh):
    fine = Mesh(mesh.devices.reshape(2, 4, 8, 2, 2), AXES)
    in_specs = (P(IMG, None), P(TXT, None), P(IMG))
    out_specs = (P(IMG + TXT, None), P(TXT + IMG, None))
    return jax.shard_map(shards, mesh=fine, in_specs=in_specs, out_specs=out_specs, check_vma=False)
```

time: 381 us -> 98.3 us (0.26)
  blocking collectives: 175 us -> 0 us
  waiting for transfers between devices: 171 us -> 33.4 us
  starting transfers between devices: 0.08 us -> 31 us
  between operations: 14.1 us -> 0.86 us
  local copies, waits for them, and re-layouts: 1.83 us -> 12.4 us
    reduce_scatter x2 -> x0, waiting for transfers between devices: 171 us -> none  [the longest x1 144 us: shards(): lax.psum_scatter(jnp.dot(weights, texts, preferred_element_type=jnp.float...]
    pmax x2 -> x0, blocking collectives: 90.4 us -> none  [the longest x1 73.9 us: shards(): row_top = lax.pmax(local_row_max, 'txt')]
    psum x2 -> x0, blocking collectives: 84.9 us -> none  [the longest x1 66 us: shards(): lax.psum(jnp.sum(jnp.exp(logits - row_top[:, None]), axis=1), 'txt')]
    all_to_all x0 -> x4, waiting for transfers between devices: none -> 31.8 us  [the longest x1 21.7 us: shards(): image_parts = lax.all_to_all(image_part, 'z', 0, 0, tiled=True)]
    all_to_all x0 -> x4, starting transfers between devices: none -> 23.8 us  [the longest x2 14.8 us: spread(): return lax.all_to_all(copies, axes, 0, 0, tiled=True)]
    ppermute x0 -> x6, starting transfers between devices: none -> 7.17 us  [swap(): return lax.ppermute(value, axis, [(0, 1), (1, 0)])]
    unnamed x4 -> x9, local copies, waits for them, and re-layouts: 1.83 us -> 7.68 us
  transfers between devices with their start and end apart: 2 -> 10, of which waited for: 2 -> 4; matrix products, arithmetic and copies ran while one was open for 2% -> 30% of each run, Pallas kernels for 0% -> 0%
where the time goes in v1:
time: 98.3 us; the launch traced here: 97.4 us
  waiting for transfers between devices  33.4 us (34%)
  starting transfers between devices  31 us (32%)
  matrix products  14.5 us (15%)
  local copies, waits for them, and re-layouts  12.4 us (13%)
  other arithmetic  5.29 us (5%)
    all_to_all x1, waiting for transfers between devices, shards(): image_parts = lax.all_to_all(image_part, 'z', 0, 0, tiled=True)  21.7 us
    all_to_all x2, starting transfers between devices, spread(): return lax.all_to_all(copies, axes, 0, 0, tiled=True)  14.8 us
    all_to_all x2, waiting for transfers between devices, spread(): return lax.all_to_all(copies, axes, 0, 0, tiled=True)  10.2 us
    unnamed x9, local copies, waits for them, and re-layouts  7.68 us
    ppermute x6, starting transfers between devices, swap(): return lax.ppermute(value, axis, [(0, 1), (1, 0)])  7.17 us
    dot_general x1, matrix products, shards(): jnp.dot(own_weights, four, preferred_element_type=F32).astype(jnp.bfloat16)  7.06 us
    all_to_all x1, starting transfers between devices, shards(): text_parts = lax.all_to_all(text_part, IMG, 0, 0, tiled=True)  4.83 us
    dot_general x1, matrix products, shards(): lax.dot_general(weights, images, (((0,), (0,)), ((), ())), preferred_elem...  4.32 us
  transfers between devices with their start and end apart: 10, of which 4 were waited for; matrix products, arithmetic and copies ran while one was open for 30% of the time, Pallas kernels for 0%

profile of v1, /device:TPU:2, one launch (start us, length us, event | category | flops | bytes accessed | tf_op | source)
XLA Modules:
  0.0 97.4 jit_solution(4437380469842783161)
XLA Ops:
  0.6 0.1 collective-permute-start
  0.7 3.3 %collective-permute-start.1 = (bf16[384,1024]{1,0:T(8,128)(2,1)}, bf16[384,1024]{1,0:T(8,128)(2,1)}, u32[]{:S(2)}, u32[]{:S(2)}) collective-permute-start(bf16[384,1024]{1,0:T(8,128)(2,1)} %param.4), channel_id=1, source_target_pairs={{0,2},{2,0},{1,3},{3,1},{4,6},{6,4},{5,7},{7,5},{8,10},{10,8},{9,1... | collective-permute-start | bytes 2359304 | tf_op jit(solution)/shard_map/ppermute | solution.py:15
  4.0 3.1 %fusion.14 = (f32[1536]{0:T(1024)S(1)}, f32[384]{0:T(512)S(1)}, f32[1536,384]{1,0:T(8,128)S(1)}) fusion(bf16[1536,1024]{1,0:T(8,128)(2,1)S(1)} %copy-done, bf16[384,1024]{1,0:T(8,128)(2,1)} %param.4), kind=kOutput, calls=%fused_computation.46 | convolution fusion | flops 1209727104 | bytes 6299136 | tf_op jit(solution)/shard_map/dot_general | solution.py:43
  7.1 1.4 %copy-done.1 = f32[1536,384]{1,0:T(8,128)} copy-done((f32[1536,384]{1,0:T(8,128)}, f32[1536,384]{1,0:T(8,128)S(1)}, u32[]{:S(2)}) %copy-start.1) | copy-done | bytes 2359320
  8.6 1.1 %exponential_reduce_fusion.1 = (f32[1536]{0:T(1024)S(1)}, f32[384]{0:T(512)S(1)}) fusion(f32[1536,384]{1,0:T(8,128)S(1)} %get-tuple-element.6, f32[1536]{0:T(1024)S(1)} %get-tuple-element.4, f32[384]{0:T(512)S(1)} %get-tuple-element.5), kind=kLoop, calls=%fused_computation.5 | loop fusion | flops 2357376 | bytes 2374656 | tf_op jit(solution)/shard_map/reduce_sum | solution.py:30
  9.7 0.6 broadcast_in_dim.5
  10.4 4.9 %all-to-all-start.1 = ((f32[8,1,384]{2,1,0:T(1,128)}), f32[8,1,384]{2,1,0:T(1,128)S(1)}, u32[]{:S(2)}, u32[]{:S(2)}) async-start(f32[8,1,384]{2,1,0:T(1,128)} %broadcast_in_dim.5), calls=%async_computation.1 | async-start | bytes 24576 | tf_op jit(solution)/shard_map/all_to_all | solution.py:20
  15.3 0.1 collective-permute-start.3
  15.4 2.1 %constant_dynamic-update-slice_fusion.3 = bf16[1536,1024]{1,0:T(8,128)(2,1)} fusion(bf16[384,1024]{1,0:T(8,128)(2,1)} %param.4), kind=kLoop, calls=%fused_computation.27 | loop fusion | bytes 1572864
  17.5 1.0 %constant_dynamic-slice_fusion = bf16[8,1,48,1024]{3,2,1,0:T(8,128)(2,1)} fusion(bf16[8,4,48,1024]{3,2,1,0:T(8,128)(2,1)S(1)} %bitcast.22, s32[]{:T(128)S(6)} %select_n.8), kind=kLoop, calls=%fused_computation.42 | loop fusion | bytes 1572868 | tf_op jit(solution)/shard_map/jit(dynamic_index_in_dim)/dynamic_slice | solution.py:70
  18.6 4.3 %all-to-all-done.1 = f32[8,1,384]{2,1,0:T(1,128)S(1)} async-done(((f32[8,1,384]{2,1,0:T(1,128)}), f32[8,1,384]{2,1,0:T(1,128)S(1)}, u32[]{:S(2)}, u32[]{:S(2)}) %all-to-all-start.1) | async-done | bytes 12320 | tf_op jit(solution)/shard_map/all_to_all | solution.py:20
  23.0 0.1 collective-permute-start.4
  23.1 0.7 broadcast_in_dim.4
  23.8 9.8 %all-to-all-start = ((f32[16,1,1536]{2,1,0:T(1,128)}), f32[16,1,1536]{2,1,0:T(1,128)S(1)}, u32[]{:S(2)}, u32[]{:S(2)}) async-start(f32[16,1,1536]{2,1,0:T(1,128)} %broadcast_in_dim.4), calls=%async_computation | async-start | bytes 196608 | tf_op jit(solution)/shard_map/all_to_all | solution.py:20
  33.7 3.5 %collective-permute-start.5 = (f32[2,384]{1,0:T(2,128)S(1)}, f32[2,384]{1,0:T(2,128)S(1)}, u32[]{:S(2)}, u32[]{:S(2)}) collective-permute-start(f32[2,384]{1,0:T(2,128)S(1)} %pad_maximum_fusion.1), channel_id=1, source_target_pairs={{0,2},{2,0},{1,3},{3,1},{4,6},{6,4},{5,7},{7,5},{8,10},{10,8},{9,1... | collective-permute-start | bytes 9224 | tf_op jit(solution)/shard_map/ppermute | solution.py:15
  37.2 0.1 reshape.110
  37.3 0.1 eq.28
  37.4 1.5 %collective-permute-done.5 = f32[2,384]{1,0:T(2,128)S(1)} collective-permute-done((f32[2,384]{1,0:T(2,128)S(1)}, f32[2,384]{1,0:T(2,128)S(1)}, u32[]{:S(2)}, u32[]{:S(2)}) %collective-permute-start.5) | collective-permute-done | bytes 3104 | tf_op jit(solution)/shard_map/ppermute | solution.py:15
  38.9 5.8 %all-to-all-done = f32[16,1,1536]{2,1,0:T(1,128)S(1)} async-done(((f32[16,1,1536]{2,1,0:T(1,128)}), f32[16,1,1536]{2,1,0:T(1,128)S(1)}, u32[]{:S(2)}, u32[]{:S(2)}) %all-to-all-start) | async-done | bytes 98336 | tf_op jit(solution)/shard_map/all_to_all | solution.py:20
  44.9 0.1 add.119
  45.0 0.1 sub.88
  45.1 0.1 collective-permute-start.2
  45.2 4.3 %convolution_convert_fusion = bf16[384,1024]{1,0:T(8,128)(2,1)} fusion(bf16[1536,1024]{1,0:T(8,128)(2,1)S(1)} %copy-done, f32[1536,384]{1,0:T(8,128)} %copy-done.1, s32[384]{0:T(512)S(1)} %get-tuple-element.10, f32[384]{0:T(512)S(1)} %log_add_fusion.3, f32[1536]{0:T(1024)S(1)} %log_add_fusion, s32[1536]{0:T(1024)S(1)} %copy-done.2), kind=kOutput, calls=%fused_computation.8 | convolution fusion | flops 1213071360 | bytes 6306816 | tf_op jit(solution)/shard_map/dot_general | solution.py:62
  49.5 4.8 %all-to-all-start.3 = ((bf16[8,48,1024]{2,1,0:T(8,128)(2,1)}), bf16[8,48,1024]{2,1,0:T(8,128)(2,1)}, u32[]{:S(2)}, u32[]{:S(2)}) async-start(bf16[8,48,1024]{2,1,0:T(8,128)(2,1)} %bitcast.24), calls=%async_computation.3 | async-start | bytes 1572864 | tf_op jit(solution)/shard_map/all_to_all | solution.py:65
  54.3 2.1 %constant_dynamic-update-slice_fusion.2 = bf16[1536,1024]{1,0:T(8,128)(2,1)} fusion(bf16[1536,1024]{1,0:T(8,128)(2,1)} %constant_dynamic-update-slice_fusion.3, bf16[384,1024]{1,0:T(8,128)(2,1)} %collective-permute-done), kind=kLoop, calls=%fused_computation.26 | loop fusion | bytes 1572864
  56.4 2.1 %constant_dynamic-update-slice_fusion.1 = bf16[1536,1024]{1,0:T(8,128)(2,1)} fusion(bf16[1536,1024]{1,0:T(8,128)(2,1)} %constant_dynamic-update-slice_fusion.2, bf16[384,1024]{1,0:T(8,128)(2,1)} %collective-permute-done.1), kind=kLoop, calls=%fused_computation.25 | loop fusion | bytes 1572864
  58.5 2.1 %constant_dynamic-update-slice_fusion = bf16[1536,1024]{1,0:T(8,128)(2,1)} fusion(bf16[1536,1024]{1,0:T(8,128)(2,1)} %constant_dynamic-update-slice_fusion.1, bf16[384,1024]{1,0:T(8,128)(2,1)} %collective-permute-done.2), kind=kLoop, calls=%fused_computation.24 | loop fusion | bytes 1572864 | tf_op jit(solution)/shard_map/concatenate | solution.py:73
  60.6 7.1 %convolution_convert_fusion.1 = bf16[384,1024]{1,0:T(8,128)(2,1)} fusion(bf16[1536,1024]{1,0:T(8,128)(2,1)} %constant_dynamic-update-slice_fusion, bf16[384,1024]{1,0:T(8,128)(2,1)} %bitcast.23, s32[1536]{0:T(1024)S(1)} %pad_add_fusion, f32[1536]{0:T(1024)S(1)} %sub.95, f32[384]{0:T(512)S(1)} %sub.88, s32[384]{0:T(512)S(1)} %eq.28), kind=kOutput, calls=%fused_computation.9 | convolution fusion | flops 2421620736 | bytes 4733952 | tf_op jit(solution)/shard_map/dot_general | solution.py:80
  67.6 4.2 %all-to-all-start.2 = ((bf16[8,48,1024]{2,1,0:T(8,128)(2,1)}), bf16[8,48,1024]{2,1,0:T(8,128)(2,1)}, u32[]{:S(2)}, u32[]{:S(2)}) async-start(bf16[8,48,1024]{2,1,0:T(8,128)(2,1)} %bitcast.25), calls=%async_computation.2 | async-start | bytes 1572864 | tf_op jit(solution)/shard_map/all_to_all | solution.py:81
  71.9 1.9 %convert_reduce_fusion = f32[48,1024]{1,0:T(8,128)} fusion(bf16[8,48,1024]{2,1,0:T(8,128)(2,1)} %all-to-all-done.3), kind=kLoop, calls=%fused_computation.6 | loop fusion | flops 737280 | bytes 983040 | tf_op jit(solution)/shard_map/reduce_sum | solution.py:66
  73.8 21.7 %all-to-all-done.2 = bf16[8,48,1024]{2,1,0:T(8,128)(2,1)} async-done(((bf16[8,48,1024]{2,1,0:T(8,128)(2,1)}), bf16[8,48,1024]{2,1,0:T(8,128)(2,1)}, u32[]{:S(2)}, u32[]{:S(2)}) %all-to-all-start.2) | async-done | bytes 786464 | tf_op jit(solution)/shard_map/all_to_all | solution.py:81
  95.5 1.9 %convert_reduce_fusion.1 = f32[48,1024]{1,0:T(8,128)} fusion(bf16[8,48,1024]{2,1,0:T(8,128)(2,1)} %all-to-all-done.2), kind=kLoop, calls=%fused_computation.7 | loop fusion | flops 737280 | bytes 983040 | tf_op jit(solution)/shard_map/reduce_sum | solution.py:82
  (34 shorter events, 0.4 us)
Async XLA Ops:
  0.6 3.4 %copy-start = (bf16[1536,1024]{1,0:T(8,128)(2,1)S(1)}, bf16[1536,1024]{1,0:T(8,128)(2,1)}, u32[]{:S(2)}) copy-start(bf16[1536,1024]{1,0:T(8,128)(2,1)} %param.3) | copy-start | bytes 9437188
  0.6 53.7 %collective-permute-start = (bf16[384,1024]{1,0:T(8,128)(2,1)}, bf16[384,1024]{1,0:T(8,128)(2,1)}, u32[]{:S(2)}, u32[]{:S(2)}) collective-permute-start(bf16[384,1024]{1,0:T(8,128)(2,1)} %param.4), channel_id=1, source_target_pairs={{0,1},{1,0},{2,3},{3,2},{4,5},{5,4},{6,7},{7,6},{8,9},{9,8},{10,11... | collective-permute-start | bytes 2359304 | tf_op jit(solution)/shard_map/ppermute | solution.py:15
  0.7 44.3 %collective-permute-start.1 = (bf16[384,1024]{1,0:T(8,128)(2,1)}, bf16[384,1024]{1,0:T(8,128)(2,1)}, u32[]{:S(2)}, u32[]{:S(2)}) collective-permute-start(bf16[384,1024]{1,0:T(8,128)(2,1)} %param.4), channel_id=1, source_target_pairs={{0,2},{2,0},{1,3},{3,1},{4,6},{6,4},{5,7},{7,5},{8,10},{10,8},{9,1... | collective-permute-start | bytes 2359304 | tf_op jit(solution)/shard_map/ppermute | solution.py:15
  7.1 1.4 %copy-start.1 = (f32[1536,384]{1,0:T(8,128)}, f32[1536,384]{1,0:T(8,128)S(1)}, u32[]{:S(2)}) copy-start(f32[1536,384]{1,0:T(8,128)S(1)} %get-tuple-element.6) | copy-start | bytes 7077892
  9.7 27.5 %copy-start.2 = (s32[1536]{0:T(1024)S(1)}, s32[1536]{0:T(1024)}, u32[]{:S(2)}) copy-start(s32[1536]{0:T(1024)} %param.5) | copy-start | bytes 18436
  10.4 12.5 %all-to-all-start.1 = ((f32[8,1,384]{2,1,0:T(1,128)}), f32[8,1,384]{2,1,0:T(1,128)S(1)}, u32[]{:S(2)}, u32[]{:S(2)}) async-start(f32[8,1,384]{2,1,0:T(1,128)} %broadcast_in_dim.5), calls=%async_computation.1 | async-start | bytes 24576 | tf_op jit(solution)/shard_map/all_to_all | solution.py:20
  15.3 3.2 %collective-permute-start.3 = (f32[1536]{0:T(1024)S(1)}, f32[1536]{0:T(1024)S(1)}, u32[]{:S(2)}, u32[]{:S(2)}) collective-permute-start(f32[1536]{0:T(1024)S(1)} %log_add_fusion.2), channel_id=1, source_target_pairs={{0,1},{1,0},{2,3},{3,2},{4,5},{5,4},{6,7},{7,6},{8,9},{9,8},{10,11... | collective-permute-start | bytes 18440 | tf_op jit(solution)/shard_map/ppermute | solution.py:15
  23.0 10.7 %collective-permute-start.4 = (f32[384]{0:T(512)S(1)}, f32[384]{0:T(512)S(1)}, u32[]{:S(2)}, u32[]{:S(2)}) collective-permute-start(f32[384]{0:T(512)S(1)} %log_add_fusion.3), channel_id=1, source_target_pairs={{0,1},{1,0},{2,3},{3,2},{4,5},{5,4},{6,7},{7,6},{8,9},{9,8},{10,11... | collective-permute-start | bytes 4616 | tf_op jit(solution)/shard_map/ppermute | solution.py:15
  23.8 21.0 %all-to-all-start = ((f32[16,1,1536]{2,1,0:T(1,128)}), f32[16,1,1536]{2,1,0:T(1,128)S(1)}, u32[]{:S(2)}, u32[]{:S(2)}) async-start(f32[16,1,1536]{2,1,0:T(1,128)} %broadcast_in_dim.4), calls=%async_computation | async-start | bytes 196608 | tf_op jit(solution)/shard_map/all_to_all | solution.py:20
  33.7 5.2 %collective-permute-start.5 = (f32[2,384]{1,0:T(2,128)S(1)}, f32[2,384]{1,0:T(2,128)S(1)}, u32[]{:S(2)}, u32[]{:S(2)}) collective-permute-start(f32[2,384]{1,0:T(2,128)S(1)} %pad_maximum_fusion.1), channel_id=1, source_target_pairs={{0,2},{2,0},{1,3},{3,1},{4,6},{6,4},{5,7},{7,5},{8,10},{10,8},{9,1... | collective-permute-start | bytes 9224 | tf_op jit(solution)/shard_map/ppermute | solution.py:15
  45.1 13.4 %collective-permute-start.2 = (bf16[384,1024]{1,0:T(8,128)(2,1)}, bf16[384,1024]{1,0:T(8,128)(2,1)}, u32[]{:S(2)}, u32[]{:S(2)}) collective-permute-start(bf16[384,1024]{1,0:T(8,128)(2,1)} %collective-permute-done.1), channel_id=1, source_target_pairs={{0,1},{1,0},{2,3},{3,2},{4,5},{5,4},{6,7},{7,6},{8,9},{9,8},{10,11... | collective-permute-start | bytes 2359304 | tf_op jit(solution)/shard_map/ppermute | solution.py:15
  49.5 18.1 %all-to-all-start.3 = ((bf16[8,48,1024]{2,1,0:T(8,128)(2,1)}), bf16[8,48,1024]{2,1,0:T(8,128)(2,1)}, u32[]{:S(2)}, u32[]{:S(2)}) async-start(bf16[8,48,1024]{2,1,0:T(8,128)(2,1)} %bitcast.24), calls=%async_computation.3 | async-start | bytes 1572864 | tf_op jit(solution)/shard_map/all_to_all | solution.py:65
  67.6 27.8 %all-to-all-start.2 = ((bf16[8,48,1024]{2,1,0:T(8,128)(2,1)}), bf16[8,48,1024]{2,1,0:T(8,128)(2,1)}, u32[]{:S(2)}, u32[]{:S(2)}) async-start(bf16[8,48,1024]{2,1,0:T(8,128)(2,1)} %bitcast.25), calls=%async_computation.2 | async-start | bytes 1572864 | tf_op jit(solution)/shard_map/all_to_all | solution.py:81

commit v2 on v1

v2 whole, which is shorter than its diff:
```python
import functools
import math

import jax
import jax.numpy as jnp
from jax import lax
from jax.experimental import pallas as pl
from jax.experimental.pallas import tpu as pltpu
from jax.sharding import Mesh, PartitionSpec as P

AXES = ("ylo", "x", "z", "yhi", "core")
IMG = ("ylo", "x")
TXT = ("z", "yhi", "core")
F32 = jnp.float32
BF16 = jnp.bfloat16
F16 = jnp.float16
VMEM_LIMIT = 48 * 1024 * 1024
HBM = pl.BlockSpec(memory_space=pl.ANY)
SCALARS = pl.BlockSpec(memory_space=pltpu.SMEM)


def swap(value, axis, bit=1):
    n = {"x": 4}.get(axis, 2)
    return lax.ppermute(value, axis, [(i, i ^ bit) for i in range(n)])


def spread(value, axes, n):
    copies = jnp.broadcast_to(value[None], (n,) + value.shape)
    return lax.all_to_all(copies, axes, 0, 0, tiled=True)


def combine(values, axis):
    top = jnp.max(values, axis=axis, keepdims=True)
    return top + jnp.log(jnp.sum(jnp.exp(values - top), axis=axis, keepdims=True))


def params():
    return pltpu.CompilerParams(vmem_limit_bytes=VMEM_LIMIT)


def nt_dot(a, b):
    return lax.dot_general(a, b, (((1,), (1,)), ((), ())), preferred_element_type=F32)


def first_kernel(scale, steps, text_ref, image_ref, logits_ref, row_ref, col_ref, peak_ref, top_ref, sum_ref):
    step = pl.program_id(0)
    block = image_ref[...]
    logits = nt_dot(text_ref[...], block) * scale
    logits_ref[...] = logits
    row_ref[...] = combine(logits, 0)
    peak = jnp.max(jnp.abs(block).astype(F32), axis=0, keepdims=True)
    peak = jnp.max(peak, axis=1, keepdims=True)
    top = jnp.max(logits, axis=1, keepdims=True)

    @pl.when(step == 0)
    def _():
        top_ref[...] = top
        sum_ref[...] = jnp.sum(jnp.exp(logits - top), axis=1, keepdims=True)
        peak_ref[...] = jnp.broadcast_to(peak, peak_ref.shape)

    @pl.when(step > 0)
    def _():
        old = top_ref[...]
        new = jnp.maximum(old, top)
        total = jnp.sum(jnp.exp(logits - new), axis=1, keepdims=True)
        sum_ref[...] = sum_ref[...] * jnp.exp(old - new) + total
        top_ref[...] = new
        peak_ref[...] = jnp.maximum(peak_ref[...], peak)

    @pl.when(step == steps - 1)
    def _():
        share = top_ref[...] + jnp.log(sum_ref[...])
        col_ref[...] = jnp.transpose(jnp.broadcast_to(share, (share.shape[0], 128)))[:1]


def first_call(texts, images, scale):
    cols, width = texts.shape
    rows = images.shape[0]
    steps = 3
    size = rows // steps
    return pl.pallas_call(
        functools.partial(first_kernel, scale, steps),
        grid=(steps,),
        in_specs=[
            pl.BlockSpec((cols, width), lambda i: (0, 0)),
            pl.BlockSpec((size, width), lambda i: (i, 0)),
        ],
        out_specs=[
            pl.BlockSpec((cols, size), lambda i: (0, i)),
            pl.BlockSpec((1, size), lambda i: (0, i)),
            pl.BlockSpec((1, cols), lambda i: (0, 0)),
            pl.BlockSpec((1, 128), lambda i: (0, 0)),
        ],
        out_shape=[
            jax.ShapeDtypeStruct((cols, rows), F32),
            jax.ShapeDtypeStruct((1, rows), F32),
            jax.ShapeDtypeStruct((1, cols), F32),
            jax.ShapeDtypeStruct((1, 128), F32),
        ],
        scratch_shapes=[pltpu.VMEM((cols, 1), F32), pltpu.VMEM((cols, 1), F32)],
        compiler_params=params(),
        cost_estimate=pl.CostEstimate(
            flops=2 * rows * cols * width, bytes_accessed=6_500_000, transcendentals=2 * rows * cols
        ),
        name="logits",
    )(texts, images)


def weigh(logits, row_lse, col_lse, paired):
    total = jnp.exp(logits - row_lse) + jnp.exp(logits - col_lse)
    return (0.5 * total - paired.astype(F32)).astype(BF16)


def text_kernel(steps, at_ref, logits_ref, row_ref, col_ref, match_ref, image_ref, a_ref, b_ref, c_ref, d_ref, total_ref):
    step = pl.program_id(0)
    cols = logits_ref.shape[0]
    col_lse = jnp.transpose(jnp.broadcast_to(col_ref[...], (128, cols)))[:, :1]
    ids = at_ref[0] + lax.broadcasted_iota(jnp.int32, logits_ref.shape, 0)
    weights = weigh(logits_ref[...], row_ref[...], col_lse, match_ref[...] == ids)
    part = jnp.dot(weights, image_ref[...], preferred_element_type=F32).reshape(total_ref.shape)

    @pl.when(step == 0)
    def _():
        total_ref[...] = part

    @pl.when(step > 0)
    def _():
        total_ref[...] += part

    @pl.when(step == steps - 1)
    def _():
        me = at_ref[1]
        d_ref[...] = total_ref[me]
        c_ref[...] = total_ref[me ^ 1]
        for k in range(2):
            b_ref[k] = total_ref[me ^ (2 + k)]
        for k in range(4):
            a_ref[k] = total_ref[me ^ (4 + k)]


def text_call(at, logits, row_lse, col_lse, match, images):
    cols, rows = logits.shape
    width = images.shape[1]
    steps = 3
    size = rows // steps
    per = cols // 8
    whole = lambda *shape: pl.BlockSpec(shape, lambda i: (0,) * len(shape))
    outs = [(4, per, width), (2, per, width), (per, width), (per, width)]
    return pl.pallas_call(
        functools.partial(text_kernel, steps),
        grid=(steps,),
        in_specs=[
            SCALARS,
            pl.BlockSpec((cols, size), lambda i: (0, i)),
            pl.BlockSpec((1, size), lambda i: (0, i)),
            whole(1, cols),
            pl.BlockSpec((1, size), lambda i: (0, i)),
            pl.BlockSpec((size, width), lambda i: (i, 0)),
        ],
        out_specs=[whole(*s) for s in outs],
        out_shape=[jax.ShapeDtypeStruct(s, F32) for s in outs],
        scratch_shapes=[pltpu.VMEM((8, per, width), F32)],
        compiler_params=params(),
        cost_estimate=pl.CostEstimate(
            flops=2 * rows * cols * width, bytes_accessed=7_000_000, transcendentals=2 * rows * cols
        ),
        name="text_part",
    )(at, logits, row_lse, col_lse, match, images)


def image_kernel(scale, at_ref, row_ref, col_ref, match_ref, image_ref, t0, t1, t2, t3, out_ref, own, four, weights, sems):
    texts = (t0, t1, t2, t3)
    blocks, _, per, width = image_ref.shape
    cols = t0.shape[0]
    place = at_ref[0]
    copies = [pltpu.make_async_copy(image_ref.at[:, place], own, sems.at[4])]
    copies += [
        pltpu.make_async_copy(texts[k], four.at[pl.ds(k * cols, cols)], sems.at[k]) for k in range(4)
    ]
    for copy in copies:
        copy.start()
    rows = blocks * per
    lanes = lax.broadcasted_iota(jnp.int32, (rows, row_ref.shape[1]), 1)
    places = lax.broadcasted_iota(jnp.int32, (rows, row_ref.shape[1]), 0)
    wanted = lanes == places + (places // per) * (3 * per) + place * per
    row_lse = jnp.sum(jnp.where(wanted, row_ref[...], 0.0), axis=1, keepdims=True)
    match = jnp.sum(jnp.where(wanted, match_ref[...], 0), axis=1, keepdims=True)
    copies[0].wait()
    mine = own[...].reshape(rows, width)
    for k in range(4):
        copies[1 + k].wait()
        logits = nt_dot(mine, four[k * cols : (k + 1) * cols]) * scale
        ids = at_ref[1 + k] + lax.broadcasted_iota(jnp.int32, logits.shape, 1)
        weights[:, k * cols : (k + 1) * cols] = weigh(
            logits, row_lse, col_ref[k : k + 1], match == ids
        )
    part = jnp.dot(weights[...], four[...], preferred_element_type=F32)
    out_ref[...] = part.astype(BF16)


def image_call(at, row_lse, col_four, match, images, texts, scale):
    rows, width = images.shape
    cols = texts[0].shape[0]
    own = rows // 4
    full = pl.BlockSpec(memory_space=pltpu.VMEM)
    return pl.pallas_call(
        functools.partial(image_kernel, scale),
        in_specs=[SCALARS, full, full, full] + [HBM] * 5,
        out_specs=full,
        out_shape=jax.ShapeDtypeStruct((own, width), BF16),
        scratch_shapes=[
            pltpu.VMEM((8, rows // 32, width), BF16),
            pltpu.VMEM((4 * cols, width), BF16),
            pltpu.VMEM((own, 4 * cols), BF16),
            pltpu.SemaphoreType.DMA((5,)),
        ],
        compiler_params=params(),
        cost_estimate=pl.CostEstimate(
            flops=4 * own * 4 * cols * width, bytes_accessed=5_000_000, transcendentals=2 * own * 4 * cols
        ),
        name="image_part",
    )(at, row_lse, col_four, match, images.reshape(8, 4, rows // 32, width), *texts)


def shards(images, texts, match):
    rows, width = images.shape
    cols = texts.shape[0]
    scale = 2.0 / math.sqrt(width)
    ylo, x, z, yhi, core = (lax.axis_index(a) for a in AXES)
    place = yhi * 2 + core

    other_yhi = swap(texts, "yhi")
    other_core = swap(texts, "core")

    logits, row_part, col_part, peak = first_call(texts, images, scale)

    sent = jnp.concatenate([row_part, col_part, peak], axis=1)
    got = spread(sent, IMG + ("core",), 16).reshape(8, 2, rows + cols + 128)
    both = lax.dynamic_index_in_dim(got, ylo * 4 + x, 0, keepdims=False)
    row_part = combine(both[:, :rows], 0)
    columns = combine(got[:, :, rows : rows + cols], 0)[0]
    col_lse = lax.dynamic_slice_in_dim(columns, core, 1, 0)
    col_other = lax.dynamic_slice_in_dim(columns, 1 - core, 1, 0)
    peak = jnp.maximum(jnp.max(got[:, :, rows + cols]), 1e-30)
    other_both = swap(other_yhi, "core")

    sent = jnp.concatenate([row_part, col_lse, col_other], axis=1)
    got = spread(sent, ("z", "yhi"), 16)[:, 0]
    row_lse = combine(got[:, :rows], 0)
    across = lax.dynamic_slice_in_dim(got, z * 2 + 1 - yhi, 1, 0)[:, rows:].reshape(2, cols)
    col_four = jnp.concatenate([col_lse, col_other, across])

    bases = jnp.stack([(z * 4 + (place ^ k)) * cols for k in range(4)])
    match = match[None]
    a, b, c, d = text_call(
        jnp.stack([bases[0], ylo * 4 + x]), logits, row_lse, col_lse, match, images
    )
    up, down = 8.0 / peak, peak / 8.0
    a = swap((a * up).astype(F16), "ylo")

    image_part = image_call(
        jnp.concatenate([place[None], bases]), row_lse, col_four, match, images,
        (texts, other_core, other_yhi, other_both), scale,
    )
    image_parts = lax.all_to_all(image_part, "z", 0, 0, tiled=True)
    image_grad = jnp.sum(image_parts.astype(F32).reshape(8, rows // 32, width), axis=0)

    b = swap((b * up + a[2:].astype(F32)).astype(F16), "x", 2)
    c = c * up + a[1].astype(F32)
    d = d * up + a[0].astype(F32)
    c = swap((c + b[1].astype(F32)).astype(F16), "x", 1)
    d = d + b[0].astype(F32)
    text_grad = (d + c.astype(F32)) * down
    return image_grad, text_grad


def solution(mesh):
    fine = Mesh(mesh.devices.reshape(2, 4, 8, 2, 2), AXES)
    in_specs = (P(IMG, None), P(TXT, None), P(IMG))
    out_specs = (P(IMG + TXT, None), P(TXT + IMG, None))
    return jax.shard_map(shards, mesh=fine, in_specs=in_specs, out_specs=out_specs, check_vma=False)
```

time: 98.3 us -> 95 us (0.966)
  the two profiles are of different devices: /device:TPU:2 before, /device:TPU:1 now
where the time goes in v2:
time: 95 us; the launch traced here: 94.6 us
  waiting for transfers between devices  40.5 us (43%)
  starting transfers between devices  31.1 us (33%)
  Pallas kernels  16.7 us (18%)
  other arithmetic  2.93 us (3%)
  local copies, waits for them, and re-layouts  1.72 us (2%)
  between operations  1.57 us (2%)
    ppermute x6, waiting for transfers between devices, swap(): return lax.ppermute(value, axis, [(i, i ^ bit) for i in range(n)])  18.4 us
    all_to_all x2, starting transfers between devices, spread(): return lax.all_to_all(copies, axes, 0, 0, tiled=True)  17.4 us
    all_to_all x1, waiting for transfers between devices, shards(): image_parts = lax.all_to_all(image_part, 'z', 0, 0, tiled=True)  11.5 us
    all_to_all x2, waiting for transfers between devices, spread(): return lax.all_to_all(copies, axes, 0, 0, tiled=True)  10.6 us
    ppermute x6, starting transfers between devices, swap(): return lax.ppermute(value, axis, [(i, i ^ bit) for i in range(n)])  7.23 us
    pallas_call x1, Pallas kernels, image_call(): pl.pallas_call(functools.partial(image_kernel, scale), in_specs=[SCALARS,...  6.93 us
    all_to_all x1, starting transfers between devices, shards(): image_parts = lax.all_to_all(image_part, 'z', 0, 0, tiled=True)  6.47 us
    pallas_call x1, Pallas kernels, first_call(): pl.pallas_call(functools.partial(first_kernel, scale, steps), grid=(steps...  5.05 us
  transfers between devices with their start and end apart: 9, of which 7 were waited for; matrix products, arithmetic and copies ran while one was open for 2% of the time, Pallas kernels for 12%

profile of v2, /device:TPU:1, one launch (start us, length us, event | category | flops | bytes accessed | tf_op | source)
XLA Modules:
  0.0 94.6 jit_solution(6197827290570626758)
XLA Ops:
  0.6 5.1 %logits.1 = (f32[384,1536]{1,0:T(8,128)S(1)}, f32[1,1536]{1,0:T(1,128)S(1)}, f32[1,384]{1,0:T(1,128)S(1)}, f32[1,128]{1,0:T(1,128)S(1)}) custom-call(bf16[384,1024]{1,0:T(8,128)(2,1)} %t0.1, bf16[1536,1024]{1,0:T(8,128)(2,1)} %image_ref.3), custom_call_target="tpu_custom_call" | custom-call | flops 1207959552 | bytes 6500000 | tf_op jit(solution)/shard_map/logits/pallas_call | solution.py:81
  5.7 0.7 broadcast_in_dim.14
  6.4 6.8 %all-to-all-start = ((f32[16,1,2048]{2,1,0:T(1,128)}), f32[16,1,2048]{2,1,0:T(1,128)S(1)}, u32[]{:S(2)}, u32[]{:S(2)}) async-start(f32[16,1,2048]{2,1,0:T(1,128)} %broadcast_in_dim.14), calls=%async_computation | async-start | bytes 262144 | tf_op jit(solution)/shard_map/all_to_all | solution.py:29
  13.3 6.1 %all-to-all-done = f32[16,1,2048]{2,1,0:T(1,128)S(1)} async-done(((f32[16,1,2048]{2,1,0:T(1,128)}), f32[16,1,2048]{2,1,0:T(1,128)S(1)}, u32[]{:S(2)}, u32[]{:S(2)}) %all-to-all-start) | async-done | bytes 131104 | tf_op jit(solution)/shard_map/all_to_all | solution.py:29
  19.4 0.3 reduce.1
  19.7 0.1 reshape.94
  20.0 0.7 broadcast_in_dim.32
  20.7 10.6 %all-to-all-start.1 = ((f32[16,1,2304]{2,1,0:T(1,128)}), f32[16,1,2304]{2,1,0:T(1,128)S(1)}, u32[]{:S(2)}, u32[]{:S(2)}) async-start(f32[16,1,2304]{2,1,0:T(1,128)} %broadcast_in_dim.32), calls=%async_computation.1 | async-start | bytes 294912 | tf_op jit(solution)/shard_map/all_to_all | solution.py:29
  31.3 2.9 %collective-permute-start.1 = (bf16[384,1024]{1,0:T(8,128)(2,1)}, bf16[384,1024]{1,0:T(8,128)(2,1)}, u32[]{:S(2)}, u32[]{:S(2)}) collective-permute-start(bf16[384,1024]{1,0:T(8,128)(2,1)} %t0.1), channel_id=1, source_target_pairs={{0,2},{2,0},{1,3},{3,1},{4,6},{6,4},{5,7},{7,5},{8,10},{10,8},{9,1... | collective-permute-start | bytes 2359304 | tf_op jit(solution)/shard_map/ppermute | solution.py:24
  34.2 1.3 %collective-permute-start = (bf16[384,1024]{1,0:T(8,128)(2,1)}, bf16[384,1024]{1,0:T(8,128)(2,1)}, u32[]{:S(2)}, u32[]{:S(2)}) collective-permute-start(bf16[384,1024]{1,0:T(8,128)(2,1)} %t0.1), channel_id=1, source_target_pairs={{0,1},{1,0},{2,3},{3,2},{4,5},{5,4},{6,7},{7,6},{8,9},{9,8},{10,11... | collective-permute-start | bytes 2359304 | tf_op jit(solution)/shard_map/ppermute | solution.py:24
  35.6 0.1 concatenate.12.at_ref
  35.6 0.1 pad_add_fusion.at_ref
  35.7 0.6 slice_reduce_fusion.2
  37.0 4.5 %all-to-all-done.1 = f32[16,1,2304]{2,1,0:T(1,128)S(1)} async-done(((f32[16,1,2304]{2,1,0:T(1,128)}), f32[16,1,2304]{2,1,0:T(1,128)S(1)}, u32[]{:S(2)}, u32[]{:S(2)}) %all-to-all-start.1) | async-done | bytes 147488 | tf_op jit(solution)/shard_map/all_to_all | solution.py:29
  41.7 4.7 %text_part.1 = (f32[4,48,1024]{2,1,0:T(8,128)S(1)}, f32[2,48,1024]{2,1,0:T(8,128)S(1)}, f32[48,1024]{1,0:T(8,128)S(1)}, f32[48,1024]{1,0:T(8,128)S(1)}) custom-call(s32[2]{0:T(128)S(1)} %pad_add_fusion.at_ref, f32[384,1536]{1,0:T(8,128)S(1)} %get-tuple-element.13.logits_ref, f32[1,1536]{1,0:T(1,128)S(1)} %add.98.row_ref, ...), custom_call_target="tpu_custom_call" | custom-call | flops 1207959552 | bytes 7000000 | tf_op jit(solution)/shard_map/text_part/pallas_call | solution.py:149
  46.4 6.7 %collective-permute-done.1.t2 = bf16[384,1024]{1,0:T(8,128)(2,1)} collective-permute-done((bf16[384,1024]{1,0:T(8,128)(2,1)}, bf16[384,1024]{1,0:T(8,128)(2,1)}, u32[]{:S(2)}, u32[]{:S(2)}) %collective-permute-start.1) | collective-permute-done | bytes 786464 | tf_op jit(solution)/shard_map/ppermute | solution.py:24
  53.2 1.5 %collective-permute-start.2 = (bf16[384,1024]{1,0:T(8,128)(2,1)}, bf16[384,1024]{1,0:T(8,128)(2,1)S(1)}, u32[]{:S(2)}, u32[]{:S(2)}) collective-permute-start(bf16[384,1024]{1,0:T(8,128)(2,1)} %collective-permute-done.1.t2), channel_id=1, source_target_pairs={{0,1},{1,0},{2,3},{3,2},{4,5},{5,4},{6,7},{7,6},{8,9},{9,8},{10,11... | collective-permute-start | bytes 2359304 | tf_op jit(solution)/shard_map/ppermute | solution.py:24
  54.7 0.1 multiply_convert_fusion
  54.8 0.1 collective-permute-start.3
  54.9 0.0 collective-permute-done.t1
  55.0 1.9 %collective-permute-done.2.t3 = bf16[384,1024]{1,0:T(8,128)(2,1)S(1)} collective-permute-done((bf16[384,1024]{1,0:T(8,128)(2,1)}, bf16[384,1024]{1,0:T(8,128)(2,1)S(1)}, u32[]{:S(2)}, u32[]{:S(2)}) %collective-permute-start.2) | collective-permute-done | bytes 786464 | tf_op jit(solution)/shard_map/ppermute | solution.py:24
  56.8 6.9 %image_part.1 = bf16[384,1024]{1,0:T(8,128)(2,1)} custom-call(s32[5]{0:T(128)S(1)} %concatenate.12.at_ref, f32[1,1536]{1,0:T(1,128)S(1)} %add.98.row_ref, f32[4,384]{1,0:T(4,128)S(1)} %pad_maximum_fusion.1.col_ref, s32[1,1536]{1,0:T(1,128)S(1)} %broadcast_in_dim.33.match_ref, bf16[8,4,48,1024]{3,2,1,0:T(8,128)(2,1)} %bitcast.36, bf16[384,1024]{1,0:T(8,128)(2,1)} %t0.1, ...), custom_call_target="tpu_custom_call" | custom-call | flops 2415919104 | bytes 5000000 | tf_op jit(solution)/shard_map/image_part/pallas_call | solution.py:206
  63.8 6.5 %all-to-all-start.2 = ((bf16[8,48,1024]{2,1,0:T(8,128)(2,1)}), bf16[8,48,1024]{2,1,0:T(8,128)(2,1)S(1)}, u32[]{:S(2)}, u32[]{:S(2)}) async-start(bf16[8,48,1024]{2,1,0:T(8,128)(2,1)} %bitcast.9), calls=%async_computation.2 | async-start | bytes 1572864 | tf_op jit(solution)/shard_map/all_to_all | solution.py:265
  70.2 0.0 collective-permute-done.3
  70.2 0.1 add_convert_fusion
  70.3 1.1 %collective-permute-start.4 = (f16[2,48,1024]{2,1,0:T(8,128)(2,1)S(1)}, f16[2,48,1024]{2,1,0:T(8,128)(2,1)S(1)}, u32[]{:S(2)}, u32[]{:S(2)}) collective-permute-start(f16[2,48,1024]{2,1,0:T(8,128)(2,1)S(1)} %add_convert_fusion), channel_id=1, source_target_pairs={{0,64},{32,96},{64,0},{96,32},{1,65},{33,97},{65,1},{97,33},{2,66}... | collective-permute-start | bytes 589832 | tf_op jit(solution)/shard_map/ppermute | solution.py:24
  71.4 6.3 %collective-permute-done.4 = f16[2,48,1024]{2,1,0:T(8,128)(2,1)S(1)} collective-permute-done((f16[2,48,1024]{2,1,0:T(8,128)(2,1)S(1)}, f16[2,48,1024]{2,1,0:T(8,128)(2,1)S(1)}, u32[]{:S(2)}, u32[]{:S(2)}) %collective-permute-start.4) | collective-permute-done | bytes 196640 | tf_op jit(solution)/shard_map/ppermute | solution.py:24
  77.7 0.4 collective-permute-start.5
  78.1 3.5 %collective-permute-done.5 = f16[48,1024]{1,0:T(8,128)(2,1)S(1)} collective-permute-done((f16[48,1024]{1,0:T(8,128)(2,1)S(1)}, f16[48,1024]{1,0:T(8,128)(2,1)S(1)}, u32[]{:S(2)}, u32[]{:S(2)}) %collective-permute-start.5) | collective-permute-done | bytes 98336 | tf_op jit(solution)/shard_map/ppermute | solution.py:24
  81.6 0.7 fusion.2
  82.3 11.5 %all-to-all-done.2 = bf16[8,48,1024]{2,1,0:T(8,128)(2,1)S(1)} async-done(((bf16[8,48,1024]{2,1,0:T(8,128)(2,1)}), bf16[8,48,1024]{2,1,0:T(8,128)(2,1)S(1)}, u32[]{:S(2)}, u32[]{:S(2)}) %all-to-all-start.2) | async-done | bytes 786464 | tf_op jit(solution)/shard_map/all_to_all | solution.py:265
  93.8 0.8 convert_reduce_fusion
  (24 shorter events, 0.4 us)
Async XLA Ops:
  0.6 34.9 %copy-start = (s32[1536]{0:T(1024)S(1)}, s32[1536]{0:T(1024)}, u32[]{:S(2)}) copy-start(s32[1536]{0:T(1024)} %param.5) | copy-start | bytes 18436
  6.4 12.9 %all-to-all-start = ((f32[16,1,2048]{2,1,0:T(1,128)}), f32[16,1,2048]{2,1,0:T(1,128)S(1)}, u32[]{:S(2)}, u32[]{:S(2)}) async-start(f32[16,1,2048]{2,1,0:T(1,128)} %broadcast_in_dim.14), calls=%async_computation | async-start | bytes 262144 | tf_op jit(solution)/shard_map/all_to_all | solution.py:29
  20.7 20.8 %all-to-all-start.1 = ((f32[16,1,2304]{2,1,0:T(1,128)}), f32[16,1,2304]{2,1,0:T(1,128)S(1)}, u32[]{:S(2)}, u32[]{:S(2)}) async-start(f32[16,1,2304]{2,1,0:T(1,128)} %broadcast_in_dim.32), calls=%async_computation.1 | async-start | bytes 294912 | tf_op jit(solution)/shard_map/all_to_all | solution.py:29
  31.3 21.8 %collective-permute-start.1 = (bf16[384,1024]{1,0:T(8,128)(2,1)}, bf16[384,1024]{1,0:T(8,128)(2,1)}, u32[]{:S(2)}, u32[]{:S(2)}) collective-permute-start(bf16[384,1024]{1,0:T(8,128)(2,1)} %t0.1), channel_id=1, source_target_pairs={{0,2},{2,0},{1,3},{3,1},{4,6},{6,4},{5,7},{7,5},{8,10},{10,8},{9,1... | collective-permute-start | bytes 2359304 | tf_op jit(solution)/shard_map/ppermute | solution.py:24
  34.2 20.7 %collective-permute-start = (bf16[384,1024]{1,0:T(8,128)(2,1)}, bf16[384,1024]{1,0:T(8,128)(2,1)}, u32[]{:S(2)}, u32[]{:S(2)}) collective-permute-start(bf16[384,1024]{1,0:T(8,128)(2,1)} %t0.1), channel_id=1, source_target_pairs={{0,1},{1,0},{2,3},{3,2},{4,5},{5,4},{6,7},{7,6},{8,9},{9,8},{10,11... | collective-permute-start | bytes 2359304 | tf_op jit(solution)/shard_map/ppermute | solution.py:24
  53.2 3.6 %collective-permute-start.2 = (bf16[384,1024]{1,0:T(8,128)(2,1)}, bf16[384,1024]{1,0:T(8,128)(2,1)S(1)}, u32[]{:S(2)}, u32[]{:S(2)}) collective-permute-start(bf16[384,1024]{1,0:T(8,128)(2,1)} %collective-permute-done.1.t2), channel_id=1, source_target_pairs={{0,1},{1,0},{2,3},{3,2},{4,5},{5,4},{6,7},{7,6},{8,9},{9,8},{10,11... | collective-permute-start | bytes 2359304 | tf_op jit(solution)/shard_map/ppermute | solution.py:24
  54.8 15.5 %collective-permute-start.3 = (f16[4,48,1024]{2,1,0:T(8,128)(2,1)S(1)}, f16[4,48,1024]{2,1,0:T(8,128)(2,1)S(1)}, u32[]{:S(2)}, u32[]{:S(2)}) collective-permute-start(f16[4,48,1024]{2,1,0:T(8,128)(2,1)S(1)} %multiply_convert_fusion), channel_id=1, source_target_pairs={{0,128},{128,0},{1,129},{129,1},{2,130},{130,2},{3,131},{131,3},{4... | collective-permute-start | bytes 1179656 | tf_op jit(solution)/shard_map/ppermute | solution.py:24
  63.8 30.0 %all-to-all-start.2 = ((bf16[8,48,1024]{2,1,0:T(8,128)(2,1)}), bf16[8,48,1024]{2,1,0:T(8,128)(2,1)S(1)}, u32[]{:S(2)}, u32[]{:S(2)}) async-start(bf16[8,48,1024]{2,1,0:T(8,128)(2,1)} %bitcast.9), calls=%async_computation.2 | async-start | bytes 1572864 | tf_op jit(solution)/shard_map/all_to_all | solution.py:265
  70.3 7.4 %collective-permute-start.4 = (f16[2,48,1024]{2,1,0:T(8,128)(2,1)S(1)}, f16[2,48,1024]{2,1,0:T(8,128)(2,1)S(1)}, u32[]{:S(2)}, u32[]{:S(2)}) collective-permute-start(f16[2,48,1024]{2,1,0:T(8,128)(2,1)S(1)} %add_convert_fusion), channel_id=1, source_target_pairs={{0,64},{32,96},{64,0},{96,32},{1,65},{33,97},{65,1},{97,33},{2,66}... | collective-permute-start | bytes 589832 | tf_op jit(solution)/shard_map/ppermute | solution.py:24
  77.7 3.8 %collective-permute-start.5 = (f16[48,1024]{1,0:T(8,128)(2,1)S(1)}, f16[48,1024]{1,0:T(8,128)(2,1)S(1)}, u32[]{:S(2)}, u32[]{:S(2)}) collective-permute-start(f16[48,1024]{1,0:T(8,128)(2,1)S(1)} %fusion), channel_id=1, source_target_pairs={{0,32},{32,0},{64,96},{96,64},{1,33},{33,1},{65,97},{97,65},{2,34}... | collective-permute-start | bytes 294920 | tf_op jit(solution)/shard_map/ppermute | solution.py:24

commit v3 on v2

v3 whole, which is shorter than its diff:
```python
import functools
import math

import jax
import jax.numpy as jnp
from jax import lax
from jax.experimental import pallas as pl
from jax.experimental.pallas import tpu as pltpu
from jax.sharding import Mesh, PartitionSpec as P

AXES = ("ylo", "x", "zhi", "zlo", "yhi", "core")
SIZES = (2, 4, 2, 4, 2, 2)
IMG = ("ylo", "x")
TXT = ("zhi", "zlo", "yhi", "core")
F32 = jnp.float32
BF16 = jnp.bfloat16
F16 = jnp.float16
LOG2E = 1.4426950408889634
VMEM_LIMIT = 48 * 1024 * 1024
HBM = pl.BlockSpec(memory_space=pl.ANY)
VMEM = pl.BlockSpec(memory_space=pltpu.VMEM)
SCALARS = pl.BlockSpec(memory_space=pltpu.SMEM)
FREE = pl.CostEstimate(flops=0, bytes_accessed=0, transcendentals=0)
LANES = 128


def swap(value, axis, bit=1):
    n = SIZES[AXES.index(axis)]
    return lax.ppermute(value, axis, [(i, i ^ bit) for i in range(n)])


def z_swap(value, bits):
    pairs = [(z * 2 + c, (z ^ bits[c]) * 2 + c) for z in range(8) for c in range(2)]
    return lax.ppermute(value, ("zhi", "zlo", "core"), pairs)


def img_swap(value, bits):
    pairs = [(i * 2 + c, (i ^ bits[c]) * 2 + c) for i in range(8) for c in range(2)]
    return lax.ppermute(value, ("ylo", "x", "core"), pairs)


def exchange(copies, axes):
    return lax.all_to_all(copies, axes, 0, 0, tiled=True)


def log2_sum(values, axis):
    top = jnp.max(values, axis=axis, keepdims=True)
    return top + jnp.log2(jnp.sum(jnp.exp2(values - top), axis=axis, keepdims=True))


def params():
    return pltpu.CompilerParams(vmem_limit_bytes=VMEM_LIMIT)


def nt_dot(a, b):
    return lax.dot_general(a, b, (((1,), (1,)), ((), ())), preferred_element_type=F32)


def largest(block):
    peak = jnp.max(jnp.abs(block).astype(F32), axis=0, keepdims=True)
    return jnp.max(peak, axis=1, keepdims=True)


def first_kernel(scale, steps, text_ref, image_ref, logits_ref, row_ref, col_ref, top_ref, sum_ref, peak_ref):
    step = pl.program_id(0)
    cols = text_ref.shape[0]
    size = image_ref.shape[0]
    rows = logits_ref.shape[1]
    block = image_ref[...]
    logits = nt_dot(text_ref[...], block) * scale
    where = pl.ds(pl.multiple_of(step * size, size), size)
    logits_ref[:, where] = logits
    row_ref[:, where] = log2_sum(logits, 0)
    peak = largest(block)
    top = jnp.max(logits, axis=1, keepdims=True)

    @pl.when(step == 0)
    def _():
        top_ref[...] = top
        sum_ref[...] = jnp.sum(jnp.exp2(logits - top), axis=1, keepdims=True)
        peak_ref[...] = jnp.broadcast_to(peak, peak_ref.shape)
        row_ref[:, rows:] = jnp.broadcast_to(largest(text_ref[...]), (1, LANES))

    @pl.when(step > 0)
    def _():
        old = top_ref[...]
        new = jnp.maximum(old, top)
        total = jnp.sum(jnp.exp2(logits - new), axis=1, keepdims=True)
        sum_ref[...] = sum_ref[...] * jnp.exp2(old - new) + total
        top_ref[...] = new
        peak_ref[...] = jnp.maximum(peak_ref[...], peak)

    @pl.when(step == steps - 1)
    def _():
        share = top_ref[...] + jnp.log2(sum_ref[...])
        share = jnp.transpose(jnp.broadcast_to(share, (cols, LANES)))[:1]
        for k in range(col_ref.shape[0]):
            col_ref[k, :, :cols] = share
            col_ref[k, :, cols:] = peak_ref[...]


def first_call(texts, images, scale):
    cols, width = texts.shape
    rows = images.shape[0]
    steps = 3
    size = rows // steps
    outs = [(cols, rows), (1, rows + LANES), (8, 1, cols + LANES)]
    return pl.pallas_call(
        functools.partial(first_kernel, scale, steps),
        grid=(steps,),
        in_specs=[
            pl.BlockSpec((cols, width), lambda i: (0, 0)),
            pl.BlockSpec((size, width), lambda i: (i, 0)),
        ],
        out_specs=[pl.BlockSpec(s, lambda i, n=len(s): (0,) * n) for s in outs],
        out_shape=[jax.ShapeDtypeStruct(s, F32) for s in outs],
        scratch_shapes=[
            pltpu.VMEM((cols, 1), F32),
            pltpu.VMEM((cols, 1), F32),
            pltpu.VMEM((1, LANES), F32),
        ],
        compiler_params=params(),
        cost_estimate=FREE,
        name="logits",
    )(texts, images)


def merge_kernel(got_ref, row_ref, cross_ref, out_ref, peak_ref):
    cols = got_ref.shape[2] - LANES
    rows = row_ref.shape[1] - LANES
    got = got_ref[:, 0, :]
    col = log2_sum(got[:, :cols], 0)
    peak_ref[...] = jnp.max(got[:, cols:], axis=0, keepdims=True)
    own, cross = row_ref[...], cross_ref[...]
    top = jnp.maximum(own, cross)
    both = top + jnp.log2(jnp.exp2(own - top) + jnp.exp2(cross - top))
    for k in range(out_ref.shape[0]):
        out_ref[k, :, :rows] = both[:, :rows]
        out_ref[k, :, rows : rows + LANES] = top[:, rows:]
        out_ref[k, :, rows + LANES :] = col


def merge_call(got, row, cross):
    cols = got.shape[2] - LANES
    return pl.pallas_call(
        merge_kernel,
        in_specs=[VMEM] * 3,
        out_specs=[VMEM] * 2,
        out_shape=[
            jax.ShapeDtypeStruct((16, 1, row.shape[1] + cols), F32),
            jax.ShapeDtypeStruct((1, LANES), F32),
        ],
        compiler_params=params(),
        cost_estimate=FREE,
        name="merge",
    )(got, row, cross)


def weigh(logits, row, col, paired):
    total = jnp.exp2(logits - row) + jnp.exp2(logits - col)
    return (0.5 * total - paired.astype(F32)).astype(BF16)


def up_scale(peak):
    return 8.0 / jnp.maximum(peak, 1e-30)


def down_scale(peak):
    return jnp.maximum(peak, 1e-30) * 0.125


def text_kernel(steps, at_ref, logits_ref, stat_ref, peak_ref, match_ref, image_ref, after_ref, out_ref, row_ref, col_ref, total_ref):
    step = pl.program_id(0)
    cols, size = logits_ref.shape
    rows = row_ref.shape[1]

    @pl.when(step == 0)
    def _():
        row_ref[...] = log2_sum(stat_ref[:, 0, :rows], 0)
        col = stat_ref[at_ref[2], :, rows + LANES :]
        col_ref[...] = jnp.transpose(jnp.broadcast_to(col, (LANES, cols)))

    ids = at_ref[0] + lax.broadcasted_iota(jnp.int32, logits_ref.shape, 0)
    row = row_ref[:, pl.ds(pl.multiple_of(step * size, size), size)]
    weights = weigh(logits_ref[...], row, col_ref[:, :1], match_ref[...] == ids)
    part = jnp.dot(weights, image_ref[...], preferred_element_type=F32).reshape(total_ref.shape)

    @pl.when(step == 0)
    def _():
        total_ref[...] = part

    @pl.when(step > 0)
    def _():
        total_ref[...] += part

    @pl.when(step == steps - 1)
    def _():
        out_ref[...] = total_ref[...].astype(BF16)


def put(total, me, core, up, a_ref, b_ref, c_ref, d_ref):
    one, two = 1 + core, 2 - core
    d_ref[...] = total[me] * up
    c_ref[...] = total[me ^ 7] * up
    b_ref[0] = total[me ^ two] * up
    b_ref[1] = total[me ^ two ^ 7] * up
    a_ref[0] = total[me ^ one] * up
    a_ref[1] = total[me ^ one ^ 7] * up
    a_ref[2] = total[me ^ 3] * up
    a_ref[3] = total[me ^ 4] * up


def text_call(at, logits, stats, peak, match, images, after):
    cols, rows = logits.shape
    width = images.shape[1]
    steps = 3
    size = rows // steps
    per = cols // 8
    whole = lambda *shape: pl.BlockSpec(shape, lambda i: (0,) * len(shape))
    outs = [(8, per, width)]
    return pl.pallas_call(
        functools.partial(text_kernel, steps),
        grid=(steps,),
        in_specs=[
            SCALARS,
            pl.BlockSpec((cols, size), lambda i: (0, i)),
            whole(*stats.shape),
            whole(*peak.shape),
            pl.BlockSpec((1, size), lambda i: (0, i)),
            pl.BlockSpec((size, width), lambda i: (i, 0)),
            HBM,
        ],
        out_specs=[whole(*s) for s in outs],
        out_shape=[jax.ShapeDtypeStruct(s, BF16) for s in outs],
        scratch_shapes=[
            pltpu.VMEM((1, rows), F32),
            pltpu.VMEM((cols, LANES), F32),
            pltpu.VMEM((8, per, width), F32),
        ],
        compiler_params=params(),
        cost_estimate=FREE,
        name="text_part",
    )(at, logits, stats, peak, match, images, after)[0]


def image_kernel(scale, at_ref, stat_ref, match_ref, image_ref, t0, t1, t2, t3, a_ref, b_ref, c_ref, d_ref, own, four, weights, total, sems):
    texts = (t0, t1, t2, t3)
    blocks, _, per, width = image_ref.shape
    cols = t0.shape[0]
    place, z, core = at_ref[0], at_ref[5], at_ref[6]
    copies = [pltpu.make_async_copy(image_ref.at[:, place], own, sems.at[4])]
    copies += [
        pltpu.make_async_copy(texts[k], four.at[pl.ds(k * cols, cols)], sems.at[k]) for k in range(4)
    ]
    for copy in copies:
        copy.start()
    rows = blocks * per
    every = match_ref.shape[1]
    lanes = lax.broadcasted_iota(jnp.int32, (rows, every), 1)
    places = lax.broadcasted_iota(jnp.int32, (rows, every), 0)
    wanted = lanes == places + (places // per) * (3 * per) + place * per
    row = log2_sum(stat_ref[:, 0, :every], 0)
    row = jnp.sum(jnp.where(wanted, row, 0.0), axis=1, keepdims=True)
    match = jnp.sum(jnp.where(wanted, match_ref[...], 0), axis=1, keepdims=True)
    copies[0].wait()
    mine = own[...].reshape(rows, width)
    first = (z % 4) * 4
    for k in range(4):
        copies[1 + k].wait()
        logits = nt_dot(mine, four[k * cols : (k + 1) * cols]) * scale
        ids = at_ref[1 + k] + lax.broadcasted_iota(jnp.int32, logits.shape, 1)
        col = stat_ref[first + (place ^ k), :, every + LANES :]
        weights[:, k * cols : (k + 1) * cols] = weigh(logits, row, col, match == ids)
    part = jnp.dot(weights[...], four[...], preferred_element_type=F32)
    peak = jnp.max(stat_ref[:, 0, every : every + LANES])
    total[...] = part.reshape(total.shape)
    put(total, z, core, up_scale(peak), a_ref, b_ref, c_ref, d_ref)


def image_call(at, stats, match, images, texts, scale):
    rows, width = images.shape
    cols = texts[0].shape[0]
    own = rows // 4
    per = rows // 32
    outs = [(4, per, width), (2, per, width), (per, width), (per, width)]
    return pl.pallas_call(
        functools.partial(image_kernel, scale),
        in_specs=[SCALARS, VMEM, VMEM] + [HBM] * 5,
        out_specs=[VMEM] * 4,
        out_shape=[jax.ShapeDtypeStruct(s, F32) for s in outs],
        scratch_shapes=[
            pltpu.VMEM((8, per, width), BF16),
            pltpu.VMEM((4 * cols, width), BF16),
            pltpu.VMEM((own, 4 * cols), BF16),
            pltpu.VMEM((8, per, width), F32),
            pltpu.SemaphoreType.DMA((5,)),
        ],
        compiler_params=params(),
        cost_estimate=FREE,
        name="image_part",
    )(at, stats, match, images.reshape(8, 4, per, width), *texts)


def halve(parts, swap_by):
    a, b, c, d = parts
    a = swap_by(a.astype(F16), (1, 2))
    b = swap_by((b + a[2:].astype(F32)).astype(F16), (2, 1))
    c = c + a[1].astype(F32)
    d = d + a[0].astype(F32)
    c = swap_by((c + b[1].astype(F32)).astype(F16), (7, 7))
    return d + b[0].astype(F32) + c.astype(F32)


def shards(images, texts, match):
    rows, width = images.shape
    cols = texts.shape[0]
    scale = 2.0 / math.sqrt(width) * LOG2E
    ylo, x, zhi, zlo, yhi, core = (lax.axis_index(a) for a in AXES)
    place = yhi * 2 + core
    z = zhi * 4 + zlo

    other_yhi = swap(texts, "yhi")
    other_core = swap(texts, "core")

    logits, row, col = first_call(texts, images, scale)
    cross = z_swap(row, (7, 7))
    got = exchange(col, IMG)
    sent, image_peak = merge_call(got, row, cross)
    other_yhi, sent = lax.optimization_barrier((other_yhi, sent))
    stats = exchange(sent, ("zlo", "yhi", "core"))
    other_both = swap(other_yhi, "core")

    bases = jnp.stack([(z * 4 + (place ^ k)) * cols for k in range(4)])
    match = match[None]
    image_parts = image_call(
        jnp.concatenate([place[None], bases, z[None], core[None]]), stats, match, images,
        (texts, other_core, other_yhi, other_both), scale,
    )
    text_parts = text_call(
        jnp.stack([bases[0], ylo * 4 + x, zlo * 4 + place, core]), logits, stats, image_peak, match, images,
        image_parts[3],
    )
    image_grad = halve(image_parts, z_swap)
    text_grad = jnp.sum(exchange(text_parts, IMG).astype(F32), axis=0)
    text_peak = jnp.max(stats[:, 0, rows : rows + 1])
    return image_grad * down_scale(text_peak), text_grad


def solution(mesh):
    fine = Mesh(mesh.devices.reshape(SIZES), AXES)
    in_specs = (P(IMG, None), P(TXT, None), P(IMG))
    out_specs = (P(IMG + TXT, None), P(TXT + IMG, None))
    return jax.shard_map(shards, mesh=fine, in_specs=in_specs, out_specs=out_specs, check_vma=False)
```

time: 95 us -> 77.7 us (0.82)
  the two profiles are of different devices: /device:TPU:1 before, /device:TPU:2 now
where the time goes in v3:
time: 77.7 us; the launch traced here: 77.2 us
  starting transfers between devices  28.7 us (37%)
  waiting for transfers between devices  22.4 us (29%)
  Pallas kernels  17.4 us (22%)
  other arithmetic  5.9 us (8%)
  between operations  1.38 us (2%)
  local copies, waits for them, and re-layouts  1.31 us (2%)
    all_to_all x3, starting transfers between devices, exchange(): return lax.all_to_all(copies, axes, 0, 0, tiled=True)  17 us
    ppermute x4, waiting for transfers between devices, z_swap(): return lax.ppermute(value, ('zhi', 'zlo', 'core'), pairs)  13.1 us
    all_to_all x3, waiting for transfers between devices, exchange(): return lax.all_to_all(copies, axes, 0, 0, tiled=True)  9.31 us
    ppermute x4, starting transfers between devices, z_swap(): return lax.ppermute(value, ('zhi', 'zlo', 'core'), pairs)  8.42 us
    pallas_call x1, Pallas kernels, image_call(): pl.pallas_call(functools.partial(image_kernel, scale), in_specs=[SCALARS,...  5.82 us
    pallas_call x1, Pallas kernels, first_call(): pl.pallas_call(functools.partial(first_kernel, scale, steps), grid=(steps...  5.55 us
    pallas_call x1, Pallas kernels, text_call(): pl.pallas_call(functools.partial(text_kernel, steps), grid=(steps,), in_s...  5.37 us
    ppermute x3, starting transfers between devices, swap(): return lax.ppermute(value, axis, [(i, i ^ bit) for i in range(n)])  3.29 us
  transfers between devices with their start and end apart: 10, of which 5 were waited for; matrix products, arithmetic and copies ran while one was open for 5% of the time, Pallas kernels for 15%

profile of v3, /device:TPU:2, one launch (start us, length us, event | category | flops | bytes accessed | tf_op | source)
XLA Modules:
  0.0 77.2 jit_solution(4992306105076992414)
XLA Ops:
  0.6 3.3 %collective-permute-start = (bf16[384,1024]{1,0:T(8,128)(2,1)}, bf16[384,1024]{1,0:T(8,128)(2,1)}, u32[]{:S(2)}, u32[]{:S(2)}) collective-permute-start(bf16[384,1024]{1,0:T(8,128)(2,1)} %t0.1), channel_id=1, source_target_pairs={{0,2},{2,0},{1,3},{3,1},{4,6},{6,4},{5,7},{7,5},{8,10},{10,8},{9,1... | collective-permute-start | bytes 2359304 | tf_op jit(solution)/shard_map/ppermute | solution.py:29
  3.9 1.2 %copy-done = bf16[384,1024]{1,0:T(8,128)(2,1)S(1)} copy-done((bf16[384,1024]{1,0:T(8,128)(2,1)S(1)}, bf16[384,1024]{1,0:T(8,128)(2,1)}, u32[]{:S(2)}) %copy-start) | copy-done | bytes 786456
  5.1 5.5 %logits.1 = (f32[384,1536]{1,0:T(8,128)S(1)}, f32[1,1664]{1,0:T(1,128)S(1)}, f32[8,1,512]{2,1,0:T(1,128)}) custom-call(bf16[384,1024]{1,0:T(8,128)(2,1)S(1)} %copy-done, bf16[1536,1024]{1,0:T(8,128)(2,1)} %image_ref.3), custom_call_target="tpu_custom_call" | custom-call | tf_op jit(solution)/shard_map/logits/pallas_call | solution.py:108
  10.6 4.9 %all-to-all-start = ((f32[8,1,512]{2,1,0:T(1,128)}), f32[8,1,512]{2,1,0:T(1,128)S(1)}, u32[]{:S(2)}, u32[]{:S(2)}) async-start(f32[8,1,512]{2,1,0:T(1,128)} %get-tuple-element.13), calls=%async_computation | async-start | bytes 32768 | tf_op jit(solution)/shard_map/all_to_all | solution.py:43
  15.6 5.9 %collective-permute-start.1 = (f32[1,1664]{1,0:T(1,128)S(1)}, f32[1,1664]{1,0:T(1,128)S(1)}, u32[]{:S(2)}, u32[]{:S(2)}) collective-permute-start(f32[1,1664]{1,0:T(1,128)S(1)} %get-tuple-element.14.row_ref), channel_id=1, source_target_pairs={{0,28},{1,29},{4,24},{5,25},{8,20},{9,21},{12,16},{13,17},{16,12},... | collective-permute-start | bytes 19976 | tf_op jit(solution)/shard_map/ppermute | solution.py:34
  21.4 1.6 %collective-permute-done.1.cross_ref = f32[1,1664]{1,0:T(1,128)S(1)} collective-permute-done((f32[1,1664]{1,0:T(1,128)S(1)}, f32[1,1664]{1,0:T(1,128)S(1)}, u32[]{:S(2)}, u32[]{:S(2)}) %collective-permute-start.1) | collective-permute-done | bytes 6688 | tf_op jit(solution)/shard_map/ppermute | solution.py:34
  23.0 0.0 all-to-all-done.got_ref
  23.0 0.7 merge.1
  23.7 0.0 collective-permute-done.t2
  23.7 0.0 collective-permute-start.3
  23.7 7.0 %all-to-all-start.1 = ((f32[16,1,2048]{2,1,0:T(1,128)}), f32[16,1,2048]{2,1,0:T(1,128)S(1)}, u32[]{:S(2)}, u32[]{:S(2)}) async-start(f32[16,1,2048]{2,1,0:T(1,128)} %get-tuple-element.16), calls=%async_computation.1 | async-start | bytes 262144 | tf_op jit(solution)/shard_map/all_to_all | solution.py:43
  30.8 0.1 concatenate.3.at_ref
  30.9 0.0 collective-permute-done.2.t1
  30.9 9.3 %all-to-all-done.1.stat_ref = f32[16,1,2048]{2,1,0:T(1,128)S(1)} async-done(((f32[16,1,2048]{2,1,0:T(1,128)}), f32[16,1,2048]{2,1,0:T(1,128)S(1)}, u32[]{:S(2)}, u32[]{:S(2)}) %all-to-all-start.1) | async-done | bytes 131104 | tf_op jit(solution)/shard_map/all_to_all | solution.py:43
  40.2 5.8 %image_part.1 = (f32[4,48,1024]{2,1,0:T(8,128)S(1)}, f32[2,48,1024]{2,1,0:T(8,128)S(1)}, f32[48,1024]{1,0:T(8,128)S(1)}, f32[48,1024]{1,0:T(8,128)S(1)}) custom-call(s32[7]{0:T(128)S(1)} %concatenate.3.at_ref, f32[16,1,2048]{2,1,0:T(1,128)S(1)} %all-to-all-done.1.stat_ref, s32[1,1536]{1,0:T(1,128)S(1)} %broadcast_in_dim.15.match_ref, ...), custom_call_target="tpu_custom_call" | custom-call | tf_op jit(solution)/shard_map/image_part/pallas_call | solution.py:286
  46.0 0.0 copy-start.4
  46.0 0.9 %convert_element_type.42 = f16[4,48,1024]{2,1,0:T(8,128)(2,1)} convert(f32[4,48,1024]{2,1,0:T(8,128)S(1)} %get-tuple-element.19) | non-fusion elementwise | flops 196608 | bytes 1179648 | tf_op jit(solution)/shard_map/convert_element_type | solution.py:306
  46.9 0.0 copy-done.4
  46.9 0.1 pad_add_fusion.at_ref
  47.0 5.4 %text_part.1 = bf16[8,48,1024]{2,1,0:T(8,128)(2,1)} custom-call(s32[4]{0:T(128)S(1)} %pad_add_fusion.at_ref, f32[384,1536]{1,0:T(8,128)S(1)} %get-tuple-element.22.logits_ref, f32[16,1,2048]{2,1,0:T(1,128)S(1)} %all-to-all-done.1.stat_ref, f32[1,128]{1,0:T(1,128)S(1)} %get-tuple-element.23.peak_ref, s32[1,1536]{1,0:T(1,128)S(1)} %broadcast_in_dim.15.match_ref, ...), custom_call_target="tpu_custom_call" | custom-call | tf_op jit(solution)/shard_map/text_part/pallas_call | solution.py:221
  52.4 5.1 %all-to-all-start.2 = ((bf16[8,48,1024]{2,1,0:T(8,128)(2,1)}), bf16[8,48,1024]{2,1,0:T(8,128)(2,1)S(1)}, u32[]{:S(2)}, u32[]{:S(2)}) async-start(bf16[8,48,1024]{2,1,0:T(8,128)(2,1)} %text_part.1), calls=%async_computation.2 | async-start | bytes 1572864 | tf_op jit(solution)/shard_map/all_to_all | solution.py:43
  57.5 1.5 %collective-permute-done.4 = f16[4,48,1024]{2,1,0:T(8,128)(2,1)} collective-permute-done((f16[4,48,1024]{2,1,0:T(8,128)(2,1)}, f16[4,48,1024]{2,1,0:T(8,128)(2,1)}, u32[]{:S(2)}, u32[]{:S(2)}) %collective-permute-start.4) | collective-permute-done | bytes 393248 | tf_op jit(solution)/shard_map/ppermute | solution.py:34
  59.0 1.0 %add_convert_fusion = f16[2,48,1024]{2,1,0:T(8,128)(2,1)S(1)} fusion(f32[2,48,1024]{2,1,0:T(8,128)S(1)} %copy-done.3, f16[4,48,1024]{2,1,0:T(8,128)(2,1)} %collective-permute-done.4), kind=kLoop, calls=%fused_computation.1 | loop fusion | flops 294912 | bytes 786432 | tf_op jit(solution)/shard_map/convert_element_type | solution.py:307
  60.0 0.3 collective-permute-start.5
  60.3 0.6 slice_reduce_fusion
  61.5 7.1 %collective-permute-done.5 = f16[2,48,1024]{2,1,0:T(8,128)(2,1)S(1)} collective-permute-done((f16[2,48,1024]{2,1,0:T(8,128)(2,1)S(1)}, f16[2,48,1024]{2,1,0:T(8,128)(2,1)S(1)}, u32[]{:S(2)}, u32[]{:S(2)}) %collective-permute-start.5) | collective-permute-done | bytes 196640 | tf_op jit(solution)/shard_map/ppermute | solution.py:34
  68.7 0.9 %fusion = f16[48,1024]{1,0:T(8,128)(2,1)S(1)} fusion(f32[48,1024]{1,0:T(8,128)S(1)} %copy-done.5, f16[2,48,1024]{2,1,0:T(8,128)(2,1)S(1)} %collective-permute-done.5, f16[4,48,1024]{2,1,0:T(8,128)(2,1)} %collective-permute-done.4), kind=kLoop, calls=%fused_computation.3 | loop fusion | flops 245760 | bytes 491520 | tf_op jit(solution)/shard_map/convert_element_type | solution.py:310
  69.6 2.3 %collective-permute-start.6 = (f16[48,1024]{1,0:T(8,128)(2,1)S(1)}, f16[48,1024]{1,0:T(8,128)(2,1)S(1)}, u32[]{:S(2)}, u32[]{:S(2)}) collective-permute-start(f16[48,1024]{1,0:T(8,128)(2,1)S(1)} %fusion), channel_id=1, source_target_pairs={{0,28},{1,29},{4,24},{5,25},{8,20},{9,21},{12,16},{13,17},{16,12},... | collective-permute-start | bytes 294920 | tf_op jit(solution)/shard_map/ppermute | solution.py:34
  71.9 0.0 all-to-all-done.2
  71.9 0.8 %convert_reduce_fusion = f32[48,1024]{1,0:T(8,128)} fusion(bf16[8,48,1024]{2,1,0:T(8,128)(2,1)S(1)} %all-to-all-done.2), kind=kLoop, calls=%fused_computation | loop fusion | flops 737280 | bytes 983040 | tf_op jit(solution)/shard_map/reduce_sum | solution.py:344
  72.7 2.9 %collective-permute-done.6 = f16[48,1024]{1,0:T(8,128)(2,1)S(1)} collective-permute-done((f16[48,1024]{1,0:T(8,128)(2,1)S(1)}, f16[48,1024]{1,0:T(8,128)(2,1)S(1)}, u32[]{:S(2)}, u32[]{:S(2)}) %collective-permute-start.6) | collective-permute-done | bytes 98336 | tf_op jit(solution)/shard_map/ppermute | solution.py:34
  75.5 1.6 %fusion.2 = f32[48,1024]{1,0:T(8,128)} fusion(f32[48,1024]{1,0:T(8,128)S(1)} %get-tuple-element.18.after_ref, f16[48,1024]{1,0:T(8,128)(2,1)S(1)} %collective-permute-done.6, f16[2,48,1024]{2,1,0:T(8,128)(2,1)S(1)} %collective-permute-done.5, f16[4,48,1024]{2,1,0:T(8,128)(2,1)} %collective-permute-done.4, f32[]{:T(128)S(6)} %mul.46), kind=kLoop, calls=%fused_computation.7 | loop fusion | flops 344064 | bytes 688132 | tf_op jit(solution)/shard_map/mul | solution.py:346
  (15 shorter events, 0.0 us)
Async XLA Ops:
  0.6 23.1 %collective-permute-start = (bf16[384,1024]{1,0:T(8,128)(2,1)}, bf16[384,1024]{1,0:T(8,128)(2,1)}, u32[]{:S(2)}, u32[]{:S(2)}) collective-permute-start(bf16[384,1024]{1,0:T(8,128)(2,1)} %t0.1), channel_id=1, source_target_pairs={{0,2},{2,0},{1,3},{3,1},{4,6},{6,4},{5,7},{7,5},{8,10},{10,8},{9,1... | collective-permute-start | bytes 2359304 | tf_op jit(solution)/shard_map/ppermute | solution.py:29
  3.9 1.2 %copy-start = (bf16[384,1024]{1,0:T(8,128)(2,1)S(1)}, bf16[384,1024]{1,0:T(8,128)(2,1)}, u32[]{:S(2)}) copy-start(bf16[384,1024]{1,0:T(8,128)(2,1)} %t0.1) | copy-start | bytes 2359300
  5.1 16.3 %copy-start.1 = (bf16[384,1024]{1,0:T(8,128)(2,1)S(1)}, bf16[384,1024]{1,0:T(8,128)(2,1)}, u32[]{:S(2)}) copy-start(bf16[384,1024]{1,0:T(8,128)(2,1)} %t0.1) | copy-start | bytes 2359300
  5.1 25.7 %copy-start.6 = (s32[1536]{0:T(1024)S(1)}, s32[1536]{0:T(1024)}, u32[]{:S(2)}) copy-start(s32[1536]{0:T(1024)} %param.5) | copy-start | bytes 18436
  10.6 12.4 %all-to-all-start = ((f32[8,1,512]{2,1,0:T(1,128)}), f32[8,1,512]{2,1,0:T(1,128)S(1)}, u32[]{:S(2)}, u32[]{:S(2)}) async-start(f32[8,1,512]{2,1,0:T(1,128)} %get-tuple-element.13), calls=%async_computation | async-start | bytes 32768 | tf_op jit(solution)/shard_map/all_to_all | solution.py:43
  15.6 7.5 %collective-permute-start.1 = (f32[1,1664]{1,0:T(1,128)S(1)}, f32[1,1664]{1,0:T(1,128)S(1)}, u32[]{:S(2)}, u32[]{:S(2)}) collective-permute-start(f32[1,1664]{1,0:T(1,128)S(1)} %get-tuple-element.14.row_ref), channel_id=1, source_target_pairs={{0,28},{1,29},{4,24},{5,25},{8,20},{9,21},{12,16},{13,17},{16,12},... | collective-permute-start | bytes 19976 | tf_op jit(solution)/shard_map/ppermute | solution.py:34
  21.4 9.4 %collective-permute-start.2 = (bf16[384,1024]{1,0:T(8,128)(2,1)S(1)}, bf16[384,1024]{1,0:T(8,128)(2,1)}, u32[]{:S(2)}, u32[]{:S(2)}) collective-permute-start(bf16[384,1024]{1,0:T(8,128)(2,1)S(1)} %copy-done.1), channel_id=1, source_target_pairs={{0,1},{1,0},{2,3},{3,2},{4,5},{5,4},{6,7},{7,6},{8,9},{9,8},{10,11... | collective-permute-start | bytes 2359304 | tf_op jit(solution)/shard_map/ppermute | solution.py:29
  23.7 16.4 %collective-permute-start.3 = (bf16[384,1024]{1,0:T(8,128)(2,1)}, bf16[384,1024]{1,0:T(8,128)(2,1)}, u32[]{:S(2)}, u32[]{:S(2)}) collective-permute-start(bf16[384,1024]{1,0:T(8,128)(2,1)} %collective-permute-done.t2), channel_id=1, source_target_pairs={{0,1},{1,0},{2,3},{3,2},{4,5},{5,4},{6,7},{7,6},{8,9},{9,8},{10,11... | collective-permute-start | bytes 2359304 | tf_op jit(solution)/shard_map/ppermute | solution.py:29
  23.7 16.4 %all-to-all-start.1 = ((f32[16,1,2048]{2,1,0:T(1,128)}), f32[16,1,2048]{2,1,0:T(1,128)S(1)}, u32[]{:S(2)}, u32[]{:S(2)}) async-start(f32[16,1,2048]{2,1,0:T(1,128)} %get-tuple-element.16), calls=%async_computation.1 | async-start | bytes 262144 | tf_op jit(solution)/shard_map/all_to_all | solution.py:43
  46.0 0.9 %copy-start.2 = (f32[2,48,1024]{2,1,0:T(8,128)}, f32[2,48,1024]{2,1,0:T(8,128)S(1)}, u32[]{:S(2)}) copy-start(f32[2,48,1024]{2,1,0:T(8,128)S(1)} %get-tuple-element.20) | copy-start | bytes 1179652
  46.0 0.9 %copy-start.4 = (f32[48,1024]{1,0:T(8,128)}, f32[48,1024]{1,0:T(8,128)S(1)}, u32[]{:S(2)}) copy-start(f32[48,1024]{1,0:T(8,128)S(1)} %get-tuple-element.21) | copy-start | bytes 589828
  46.9 12.1 %collective-permute-start.4 = (f16[4,48,1024]{2,1,0:T(8,128)(2,1)}, f16[4,48,1024]{2,1,0:T(8,128)(2,1)}, u32[]{:S(2)}, u32[]{:S(2)}) collective-permute-start(f16[4,48,1024]{2,1,0:T(8,128)(2,1)} %convert_element_type.42), channel_id=1, source_target_pairs={{0,4},{1,9},{4,0},{5,13},{8,12},{9,1},{12,8},{13,5},{16,20},{17,25... | collective-permute-start | bytes 1179656 | tf_op jit(solution)/shard_map/ppermute | solution.py:34
  47.0 12.0 %copy-start.3 = (f32[2,48,1024]{2,1,0:T(8,128)S(1)}, f32[2,48,1024]{2,1,0:T(8,128)}, u32[]{:S(2)}) copy-start(f32[2,48,1024]{2,1,0:T(8,128)} %copy-done.2) | copy-start | bytes 1179652
  52.4 16.3 %copy-start.5 = (f32[48,1024]{1,0:T(8,128)S(1)}, f32[48,1024]{1,0:T(8,128)}, u32[]{:S(2)}) copy-start(f32[48,1024]{1,0:T(8,128)} %copy-done.4) | copy-start | bytes 589828
  52.4 19.5 %all-to-all-start.2 = ((bf16[8,48,1024]{2,1,0:T(8,128)(2,1)}), bf16[8,48,1024]{2,1,0:T(8,128)(2,1)S(1)}, u32[]{:S(2)}, u32[]{:S(2)}) async-start(bf16[8,48,1024]{2,1,0:T(8,128)(2,1)} %text_part.1), calls=%async_computation.2 | async-start | bytes 1572864 | tf_op jit(solution)/shard_map/all_to_all | solution.py:43
  60.0 8.7 %collective-permute-start.5 = (f16[2,48,1024]{2,1,0:T(8,128)(2,1)S(1)}, f16[2,48,1024]{2,1,0:T(8,128)(2,1)S(1)}, u32[]{:S(2)}, u32[]{:S(2)}) collective-permute-start(f16[2,48,1024]{2,1,0:T(8,128)(2,1)S(1)} %add_convert_fusion), channel_id=1, source_target_pairs={{0,8},{1,5},{4,12},{5,1},{8,0},{9,13},{12,4},{13,9},{16,24},{17,21... | collective-permute-start | bytes 589832 | tf_op jit(solution)/shard_map/ppermute | solution.py:34
  69.6 5.9 %collective-permute-start.6 = (f16[48,1024]{1,0:T(8,128)(2,1)S(1)}, f16[48,1024]{1,0:T(8,128)(2,1)S(1)}, u32[]{:S(2)}, u32[]{:S(2)}) collective-permute-start(f16[48,1024]{1,0:T(8,128)(2,1)S(1)} %fusion), channel_id=1, source_target_pairs={{0,28},{1,29},{4,24},{5,25},{8,20},{9,21},{12,16},{13,17},{16,12},... | collective-permute-start | bytes 294920 | tf_op jit(solution)/shard_map/ppermute | solution.py:34

commit v4 on v1

v4 whole, which is shorter than its diff:
```python
import functools
import math

import jax
import jax.numpy as jnp
from jax import lax
from jax.experimental import pallas as pl
from jax.experimental.pallas import tpu as pltpu
from jax.sharding import Mesh, PartitionSpec as P

AXES = ("ylo", "x", "zhi", "zb", "za", "yhi", "core")
SIZES = (2, 4, 2, 2, 2, 2, 2)
IMG = ("ylo", "x")
TXT = ("zhi", "zb", "za", "yhi", "core")
F32 = jnp.float32
BF16 = jnp.bfloat16
F16 = jnp.float16
LOG2E = 1.4426950408889634
HBM = pl.BlockSpec(memory_space=pltpu.HBM)
VMEM = pl.BlockSpec(memory_space=pltpu.VMEM)
SCALARS = pl.BlockSpec(memory_space=pltpu.SMEM)
FREE = pl.CostEstimate(flops=0, bytes_accessed=0, transcendentals=0)
LANES = 128
MIB = 1024 * 1024


def swap(value, axis):
    return lax.ppermute(value, axis, [(0, 1), (1, 0)])


def z_swap(value, bits):
    pairs = [(z * 2 + c, (z ^ bits[c]) * 2 + c) for z in range(8) for c in range(2)]
    return lax.ppermute(value, ("zhi", "zb", "za", "core"), pairs)


def exchange(copies, axes):
    return lax.all_to_all(copies, axes, 0, 0, tiled=True)


def tie(*values):
    return lax.optimization_barrier(values)


def log2_sum(values, axis):
    top = jnp.max(values, axis=axis, keepdims=True)
    return top + jnp.log2(jnp.sum(jnp.exp2(values - top), axis=axis, keepdims=True))


def merge(own, got, n):
    top = jnp.maximum(own, got)
    total = top + jnp.log2(jnp.exp2(own - top) + jnp.exp2(got - top))
    lanes = lax.broadcasted_iota(jnp.int32, own.shape, 1)
    return jnp.where(lanes < n, total, top)


def params(mib):
    return pltpu.CompilerParams(vmem_limit_bytes=mib * MIB)


def nt_dot(a, b):
    return lax.dot_general(a, b, (((1,), (1,)), ((), ())), preferred_element_type=F32)


def largest(block):
    peak = jnp.max(jnp.abs(block).astype(F32), axis=0, keepdims=True)
    return jnp.max(peak, axis=1, keepdims=True)


def first_kernel(scale, text_in, image_in, logits_out, row_ref, col_ref, text_ref, image_ref, logits_ref, sems):
    cols = text_in.shape[0]
    rows = image_in.shape[0]
    size = rows // 3
    steps = range(0, rows, size)
    fetch = [pltpu.make_async_copy(text_in, text_ref, sems.at[0])]
    fetch += [
        pltpu.make_async_copy(image_in.at[pl.ds(j, size)], image_ref.at[pl.ds(j, size)], sems.at[1 + k])
        for k, j in enumerate(steps)
    ]
    for copy in fetch:
        copy.start()
    fetch[0].wait()
    text = text_ref[...]
    row_ref[:, rows:] = jnp.broadcast_to(largest(text), (1, LANES))
    high = total = None
    store = []
    for k, j in enumerate(steps):
        fetch[1 + k].wait()
        logits = nt_dot(text, image_ref[j : j + size]) * scale
        logits_ref[:, j : j + size] = logits
        where = pl.ds(j, size)
        store.append(pltpu.make_async_copy(logits_ref.at[:, where], logits_out.at[:, where], sems.at[4 + k]))
        store[k].start()
        deep = logits.reshape(cols // 8, 8, size)
        top = jnp.max(deep, axis=0)
        part = jnp.sum(jnp.exp2(deep - top[None]), axis=0)
        best = jnp.max(top, axis=0, keepdims=True)
        part = jnp.sum(part * jnp.exp2(top - best), axis=0, keepdims=True)
        row_ref[:, j : j + size] = best + jnp.log2(part)
        tiles = [logits[:, i : i + LANES] for i in range(0, size, LANES)]
        new = functools.reduce(jnp.maximum, tiles if high is None else [high, *tiles])
        sums = [jnp.exp2(tile - new) for tile in tiles]
        total = functools.reduce(jnp.add, sums if high is None else [total * jnp.exp2(high - new), *sums])
        high = new
    best = jnp.max(high, axis=1, keepdims=True)
    share = best + jnp.log2(jnp.sum(total * jnp.exp2(high - best), axis=1, keepdims=True))
    share = jnp.transpose(jnp.broadcast_to(share, (cols, LANES)))[:1]
    for k in range(col_ref.shape[0]):
        col_ref[k] = share
    for copy in store:
        copy.wait()


def first_call(texts, images, scale):
    cols = texts.shape[0]
    rows = images.shape[0]
    outs = [(cols, rows), (1, rows + LANES), (8, 1, cols)]
    return pl.pallas_call(
        functools.partial(first_kernel, scale),
        in_specs=[HBM] * 2,
        out_specs=[HBM, VMEM, VMEM],
        out_shape=[jax.ShapeDtypeStruct(s, F32) for s in outs],
        scratch_shapes=[
            pltpu.VMEM(texts.shape, BF16),
            pltpu.VMEM(images.shape, BF16),
            pltpu.VMEM((cols, rows), F32),
            pltpu.SemaphoreType.DMA((7,)),
        ],
        compiler_params=params(60),
        cost_estimate=FREE,
        name="logits",
    )(texts, images)


def merge_kernel(got_ref, row_ref, near_ref, out_ref):
    rows = row_ref.shape[1]
    col = log2_sum(got_ref[:, 0, :], 0)
    both = merge(row_ref[...], near_ref[...], rows - LANES)
    for k in range(out_ref.shape[0]):
        out_ref[k, :, :rows] = both
        out_ref[k, :, rows:] = col


def merge_call(got, row, near):
    cols = got.shape[2]
    return pl.pallas_call(
        merge_kernel,
        in_specs=[VMEM] * 3,
        out_specs=VMEM,
        out_shape=jax.ShapeDtypeStruct((8, 1, row.shape[1] + cols), F32),
        compiler_params=params(4),
        cost_estimate=FREE,
        name="merge",
    )(got, row, near)


def weigh(logits, row, col, paired):
    total = jnp.exp2(logits - row) + jnp.exp2(logits - col)
    return (0.5 * total - paired.astype(F32)).astype(BF16)


def up_scale(peak):
    return 8.0 / jnp.maximum(peak, 1e-30)


def down_scale(peak):
    return jnp.maximum(peak, 1e-30) * 0.125


def text_kernel(at_ref, logits_in, stat_ref, match_ref, image_in, after_ref, out_ref, logits_ref, image_ref, weights, sems):
    cols, rows = logits_in.shape
    size = rows // 4
    steps = range(0, rows, size)
    fetch = [
        pltpu.make_async_copy(logits_in.at[:, pl.ds(j, size)], logits_ref.at[:, pl.ds(j, size)], sems.at[k])
        for k, j in enumerate(steps)
    ]
    fetch.append(pltpu.make_async_copy(image_in, image_ref, sems.at[4]))
    for copy in fetch:
        copy.start()
    row = log2_sum(stat_ref[:, 0, :rows], 0)
    col = stat_ref[at_ref[7] + at_ref[0], :, rows + LANES :]
    col = jnp.transpose(jnp.broadcast_to(col, (LANES, cols)))[:, :1]
    ids = at_ref[1] + lax.broadcasted_iota(jnp.int32, (cols, size), 0)
    for k, j in enumerate(steps):
        fetch[k].wait()
        paired = match_ref[:, j : j + size] == ids
        weights[:, j : j + size] = weigh(logits_ref[:, j : j + size], row[:, j : j + size], col, paired)
    fetch[4].wait()
    part = jnp.dot(weights[...], image_ref[...], preferred_element_type=F32)
    out_ref[...] = part.astype(BF16).reshape(out_ref.shape)


def text_call(at, logits, stats, match, images, after):
    cols, rows = logits.shape
    width = images.shape[1]
    return pl.pallas_call(
        text_kernel,
        in_specs=[SCALARS, HBM, VMEM, VMEM, HBM, HBM],
        out_specs=VMEM,
        out_shape=jax.ShapeDtypeStruct((8, cols // 8, width), BF16),
        scratch_shapes=[
            pltpu.VMEM((cols, rows), F32),
            pltpu.VMEM(images.shape, BF16),
            pltpu.VMEM((cols, rows), BF16),
            pltpu.SemaphoreType.DMA((5,)),
        ],
        compiler_params=params(60),
        cost_estimate=FREE,
        name="text_part",
    )(at, logits, stats, match, images, after)


def image_kernel(scale, at_ref, stat_ref, match_ref, image_ref, t0, t1, t2, t3, a_ref, b_ref, c_ref, d_ref, down_ref, own, four, row_all, weights, sems):
    texts = (t0, t1, t2, t3)
    blocks, _, per, width = image_ref.shape
    cols = t0.shape[0]
    rows = blocks * per
    every = match_ref.shape[1]
    place, z, core, first = at_ref[0], at_ref[5], at_ref[6], at_ref[7]
    one, two = 1 + core, 2 - core
    order = [z ^ one, z ^ one ^ 7, z ^ 3, z ^ 4, z ^ two, z ^ two ^ 7, z ^ 7, z]
    fetch = [
        pltpu.make_async_copy(image_ref.at[block, place], own.at[k], sems.at[4]) for k, block in enumerate(order)
    ]
    fetch += [
        pltpu.make_async_copy(texts[k], four.at[pl.ds(k * cols, cols)], sems.at[k]) for k in range(4)
    ]
    for copy in fetch:
        copy.start()
    row_all[...] = log2_sum(stat_ref[:, 0, :every], 0)
    span = 2 * LANES
    lanes = lax.broadcasted_iota(jnp.int32, (per, span), 1) - lax.broadcasted_iota(jnp.int32, (per, span), 0)
    row, match = [], []
    for block in order:
        begin = block * (4 * per) + place * per
        start = jnp.minimum(begin // LANES * LANES, every - span)
        window = pl.ds(pl.multiple_of(start, LANES), span)
        wanted = lanes == begin - start
        row.append(jnp.sum(jnp.where(wanted, row_all[:, window], 0.0), axis=1, keepdims=True))
        match.append(jnp.sum(jnp.where(wanted, match_ref[:, window], 0), axis=1, keepdims=True))
    row = jnp.concatenate(row, axis=0)
    match = jnp.concatenate(match, axis=0)
    ids = lax.broadcasted_iota(jnp.int32, (rows, cols), 1)
    for copy in fetch[:8]:
        copy.wait()
    mine = own[...].reshape(rows, width)
    for k in range(4):
        fetch[8 + k].wait()
        where = slice(k * cols, (k + 1) * cols)
        logits = nt_dot(mine, four[where]) * scale
        col = stat_ref[first + (place ^ k), :, every + LANES :]
        weights[:, where] = weigh(logits, row, col, match - at_ref[1 + k] == ids)
    peak = jnp.max(stat_ref[:, 0, every : every + LANES], axis=0, keepdims=True)
    down_ref[...] = down_scale(peak)
    part = jnp.dot(weights[...], four[...], preferred_element_type=F32) * up_scale(peak[:, :1])
    a_ref[...] = part[: 4 * per].astype(a_ref.dtype).reshape(a_ref.shape)
    b_ref[...] = part[4 * per : 6 * per].reshape(b_ref.shape)
    c_ref[...] = part[6 * per : 7 * per]
    d_ref[...] = part[7 * per :]


def image_call(at, stats, match, images, texts, scale):
    rows, width = images.shape
    cols = texts[0].shape[0]
    own = rows // 4
    per = rows // 32
    outs = [(4, per, width), (2, per, width), (per, width), (per, width), (1, LANES)]
    kinds = [BF16, F32, F32, F32, F32]
    return pl.pallas_call(
        functools.partial(image_kernel, scale),
        in_specs=[SCALARS, VMEM, VMEM] + [HBM] * 5,
        out_specs=[VMEM] * 5,
        out_shape=[jax.ShapeDtypeStruct(s, t) for s, t in zip(outs, kinds)],
        scratch_shapes=[
            pltpu.VMEM((8, per, width), BF16),
            pltpu.VMEM((4 * cols, width), BF16),
            pltpu.VMEM((1, rows), F32),
            pltpu.VMEM((own, 4 * cols), BF16),
            pltpu.SemaphoreType.DMA((5,)),
        ],
        compiler_params=params(60),
        cost_estimate=FREE,
        name="image_part",
    )(at, stats, match, images.reshape(8, 4, per, width), *texts)


def shards(images, texts, match):
    rows, width = images.shape
    cols = texts.shape[0]
    scale = 2.0 / math.sqrt(width) * LOG2E
    zhi, zb, za, yhi, core = (lax.axis_index(a) for a in TXT)
    place = yhi * 2 + core
    z = zhi * 4 + zb * 2 + za

    other_yhi = swap(texts, "yhi")
    other_core = swap(texts, "core")

    logits, row, col = first_call(texts, images, scale)
    cross = z_swap(row, (7, 7))
    row = merge(row, cross, rows)
    near = z_swap(row, (1, 1))
    got = exchange(col, IMG)
    sent = merge_call(got, row, near)
    other_yhi, sent = tie(other_yhi, sent)
    stats = exchange(sent, ("zb", "yhi", "core"))
    other_both = swap(other_yhi, "core")

    bases = [(z * 4 + (place ^ k)) * cols for k in range(4)]
    at = jnp.stack([place, *bases, z, core, zb * 4])
    match = match[None]
    a, b, c, d, down = image_call(at, stats, match, images, (texts, other_core, other_yhi, other_both), scale)
    text_parts = text_call(at, logits, stats, match, images, d)

    a = z_swap(a, (1, 2))
    b = (b + a[2:].astype(F32)).astype(F16)
    b = z_swap(b, (2, 1))
    c = c + a[1].astype(F32)
    d = d + a[0].astype(F32)
    text_parts = exchange(text_parts, IMG)
    b, c, d = tie(b, c, d)
    c = z_swap((c + b[1].astype(F32)).astype(F16), (7, 7))
    d = d + b[0].astype(F32)
    text_grad = jnp.sum(text_parts.astype(F32), axis=0)
    c, d = tie(c, d)
    return (d + c.astype(F32)) * down[:, :1], text_grad


def solution(mesh):
    fine = Mesh(mesh.devices.reshape(SIZES), AXES)
    in_specs = (P(IMG, None), P(TXT, None), P(IMG))
    out_specs = (P(IMG + TXT, None), P(TXT + IMG, None))
    return jax.shard_map(shards, mesh=fine, in_specs=in_specs, out_specs=out_specs, check_vma=False)
```

time: 98.3 us -> 75.1 us (0.76)
  Pallas kernels: 0 us -> 19.3 us
  matrix products: 14.5 us -> 0 us
  waiting for transfers between devices: 33.4 us -> 21.8 us
  local copies, waits for them, and re-layouts: 12.4 us -> 2.16 us
  other arithmetic: 5.29 us -> 2.39 us
  starting transfers between devices: 31 us -> 28.3 us
    all_to_all x4 -> x3, waiting for transfers between devices: 31.8 us -> 9.11 us  [exchange(): return lax.all_to_all(copies, axes, 0, 0, tiled=True)]
    pallas_call x0 -> x4, Pallas kernels: none -> 19.3 us  [the longest x1 7.35 us: image_call(): pl.pallas_call(functools.partial(image_kernel, scale), in_specs=[SCALARS,...]
    dot_general x3 -> x0, matrix products: 14.5 us -> none  [the longest x1 7.06 us: shards(): jnp.dot(own_weights, four, preferred_element_type=F32).astype(jnp.bfloat16)]
    ppermute x0 -> x5, waiting for transfers between devices: none -> 12.7 us  [z_swap(): return lax.ppermute(value, ('zhi', 'zb', 'za', 'core'), pairs)]
    ppermute x0 -> x5, starting transfers between devices: none -> 9.64 us  [z_swap(): return lax.ppermute(value, ('zhi', 'zb', 'za', 'core'), pairs)]
    all_to_all x4 -> x3, starting transfers between devices: 23.8 us -> 15.3 us  [exchange(): return lax.all_to_all(copies, axes, 0, 0, tiled=True)]
    unnamed x9 -> x20, local copies, waits for them, and re-layouts: 7.68 us -> 0.92 us
    reduce_sum x6 -> x1, other arithmetic: 5.12 us -> 0.79 us  [shards(): text_grad = jnp.sum(text_parts.astype(F32), axis=0)]
  transfers between devices with their start and end apart: 10 -> 11, of which waited for: 4 -> 6; matrix products, arithmetic and copies ran while one was open for 30% -> 4% of each run, Pallas kernels for 0% -> 16%
where the time goes in v4:
time: 75.1 us; the launch traced here: 74.7 us
  starting transfers between devices  28.3 us (38%)
  waiting for transfers between devices  21.8 us (29%)
  Pallas kernels  19.3 us (26%)
  other arithmetic  2.39 us (3%)
  local copies, waits for them, and re-layouts  2.16 us (3%)
  between operations  0.77 us (1%)
    all_to_all x3, starting transfers between devices, exchange(): return lax.all_to_all(copies, axes, 0, 0, tiled=True)  15.3 us
    ppermute x5, waiting for transfers between devices, z_swap(): return lax.ppermute(value, ('zhi', 'zb', 'za', 'core'), pairs)  12.7 us
    ppermute x5, starting transfers between devices, z_swap(): return lax.ppermute(value, ('zhi', 'zb', 'za', 'core'), pairs)  9.64 us
    all_to_all x3, waiting for transfers between devices, exchange(): return lax.all_to_all(copies, axes, 0, 0, tiled=True)  9.11 us
    pallas_call x1, Pallas kernels, image_call(): pl.pallas_call(functools.partial(image_kernel, scale), in_specs=[SCALARS,...  7.35 us
    pallas_call x1, Pallas kernels, text_call(): pl.pallas_call(text_kernel, in_specs=[SCALARS, HBM, VMEM, VMEM, HBM, HBM]...  5.86 us
    pallas_call x1, Pallas kernels, first_call(): pl.pallas_call(functools.partial(first_kernel, scale), in_specs=[HBM] * 2...  5.42 us
    ppermute x3, starting transfers between devices, swap(): return lax.ppermute(value, axis, [(0, 1), (1, 0)])  3.29 us
  transfers between devices with their start and end apart: 11, of which 6 were waited for; matrix products, arithmetic and copies ran while one was open for 4% of the time, Pallas kernels for 16%

profile of v4, /device:TPU:2, one launch (start us, length us, event | category | flops | bytes accessed | tf_op | source)
XLA Modules:
  0.0 74.7 jit_solution(11316244401319232291)
XLA Ops:
  0.6 0.0 copy-start
  0.7 3.3 %collective-permute-start = (bf16[384,1024]{1,0:T(8,128)(2,1)}, bf16[384,1024]{1,0:T(8,128)(2,1)S(1)}, u32[]{:S(2)}, u32[]{:S(2)}) collective-permute-start(bf16[384,1024]{1,0:T(8,128)(2,1)} %t0.1), channel_id=1, source_target_pairs={{0,2},{2,0},{1,3},{3,1},{4,6},{6,4},{5,7},{7,5},{8,10},{10,8},{9,1... | collective-permute-start | bytes 2359304 | tf_op jit(solution)/shard_map/ppermute | solution.py:28
  3.9 5.4 %logits.1 = (f32[384,1536]{1,0:T(8,128)}, f32[1,1664]{1,0:T(1,128)}, f32[8,1,384]{2,1,0:T(1,128)}) custom-call(bf16[384,1024]{1,0:T(8,128)(2,1)} %t0.1, bf16[1536,1024]{1,0:T(8,128)(2,1)} %image_in.3), custom_call_target="tpu_custom_call" | custom-call | tf_op jit(solution)/shard_map/logits/pallas_call | solution.py:117
  9.4 5.9 %collective-permute-start.1 = (f32[1,1664]{1,0:T(1,128)}, f32[1,1664]{1,0:T(1,128)S(1)}, u32[]{:S(2)}, u32[]{:S(2)}) collective-permute-start(f32[1,1664]{1,0:T(1,128)} %get-tuple-element.18), channel_id=1, source_target_pairs={{0,28},{1,29},{4,24},{5,25},{8,20},{9,21},{12,16},{13,17},{16,12},... | collective-permute-start | bytes 19976 | tf_op jit(solution)/shard_map/ppermute | solution.py:33
  15.3 4.9 %all-to-all-start = ((f32[8,1,384]{2,1,0:T(1,128)}), f32[8,1,384]{2,1,0:T(1,128)S(1)}, u32[]{:S(2)}, u32[]{:S(2)}) async-start(f32[8,1,384]{2,1,0:T(1,128)} %get-tuple-element.17), calls=%async_computation | async-start | bytes 24576 | tf_op jit(solution)/shard_map/all_to_all | solution.py:37
  20.3 0.0 collective-permute-done.1
  20.3 0.7 compare_select_fusion.row_ref
  21.0 2.0 %collective-permute-start.2 = (f32[1,1664]{1,0:T(1,128)S(1)}, f32[1,1664]{1,0:T(1,128)S(1)}, u32[]{:S(2)}, u32[]{:S(2)}) collective-permute-start(f32[1,1664]{1,0:T(1,128)S(1)} %compare_select_fusion.row_ref), channel_id=1, source_target_pairs={{0,4},{1,5},{4,0},{5,1},{8,12},{9,13},{12,8},{13,9},{16,20},{17,21... | collective-permute-start | bytes 19976 | tf_op jit(solution)/shard_map/ppermute | solution.py:33
  23.0 0.0 collective-permute-start.3
  23.0 2.0 %all-to-all-done.got_ref = f32[8,1,384]{2,1,0:T(1,128)S(1)} async-done(((f32[8,1,384]{2,1,0:T(1,128)}), f32[8,1,384]{2,1,0:T(1,128)S(1)}, u32[]{:S(2)}, u32[]{:S(2)}) %all-to-all-start) | async-done | bytes 12320 | tf_op jit(solution)/shard_map/all_to_all | solution.py:37
  25.0 0.7 merge.1
  25.7 5.0 %all-to-all-start.1 = ((f32[8,1,2048]{2,1,0:T(1,128)}), f32[8,1,2048]{2,1,0:T(1,128)S(1)}, u32[]{:S(2)}, u32[]{:S(2)}) async-start(f32[8,1,2048]{2,1,0:T(1,128)} %merge.1), calls=%async_computation.1 | async-start | bytes 131072 | tf_op jit(solution)/shard_map/all_to_all | solution.py:37
  30.7 0.6 broadcast_in_dim.3.match_ref
  31.3 0.6 stack.35.at_ref
  32.0 6.3 %all-to-all-done.1.stat_ref = f32[8,1,2048]{2,1,0:T(1,128)S(1)} async-done(((f32[8,1,2048]{2,1,0:T(1,128)}), f32[8,1,2048]{2,1,0:T(1,128)S(1)}, u32[]{:S(2)}, u32[]{:S(2)}) %all-to-all-start.1) | async-done | bytes 65568 | tf_op jit(solution)/shard_map/all_to_all | solution.py:37
  38.3 0.6 copy-done.5
  38.9 0.3 copy-done.4
  39.2 7.4 %image_part.1 = (bf16[4,48,1024]{2,1,0:T(8,128)(2,1)}, f32[2,48,1024]{2,1,0:T(8,128)}, f32[48,1024]{1,0:T(8,128)}, f32[48,1024]{1,0:T(8,128)}, f32[1,128]{1,0:T(1,128)}) custom-call(s32[8]{0:T(128)} %stack.35.at_ref, f32[8,1,2048]{2,1,0:T(1,128)} %copy-done.5, s32[1,1536]{1,0:T(1,128)} %broadcast_in_dim.3.match_ref, bf16[8,4,48,1024]{3,2,1,0:T(8,128)(2,1)} %bitcast.27, ...), custom_call_target="tpu_custom_call" | custom-call | tf_op jit(solution)/shard_map/image_part/pallas_call | solution.py:269
  46.5 0.1 collective-permute-start.5
  46.7 5.9 %text_part.1 = bf16[8,48,1024]{2,1,0:T(8,128)(2,1)} custom-call(s32[8]{0:T(128)} %stack.35.at_ref, f32[384,1536]{1,0:T(8,128)} %get-tuple-element.31.logits_in, f32[8,1,2048]{2,1,0:T(1,128)} %copy-done.5, s32[1,1536]{1,0:T(1,128)} %broadcast_in_dim.3.match_ref, bf16[1536,1024]{1,0:T(8,128)(2,1)} %image_in.3, f32[48,1024]{1,0:T(8,128)} %get-tuple-element.24.after_ref), custom_call_target="tpu_custom_call" | custom-call | tf_op jit(solution)/shard_map/text_part/pallas_call | solution.py:196
  52.5 0.0 copy-start.1
  52.5 0.0 copy-start.7
  52.6 5.4 %all-to-all-start.2 = ((bf16[8,48,1024]{2,1,0:T(8,128)(2,1)}), bf16[8,48,1024]{2,1,0:T(8,128)(2,1)S(1)}, u32[]{:S(2)}, u32[]{:S(2)}) async-start(bf16[8,48,1024]{2,1,0:T(8,128)(2,1)} %text_part.1), calls=%async_computation.2 | async-start | bytes 1572864 | tf_op jit(solution)/shard_map/all_to_all | solution.py:37
  57.9 0.8 %collective-permute-done.5 = bf16[4,48,1024]{2,1,0:T(8,128)(2,1)S(1)} collective-permute-done((bf16[4,48,1024]{2,1,0:T(8,128)(2,1)}, bf16[4,48,1024]{2,1,0:T(8,128)(2,1)S(1)}, u32[]{:S(2)}, u32[]{:S(2)}) %collective-permute-start.5) | collective-permute-done | bytes 393248 | tf_op jit(solution)/shard_map/ppermute | solution.py:33
  58.7 0.1 add_convert_fusion
  58.8 0.1 collective-permute-start.6
  59.0 8.6 %collective-permute-done.6 = f16[2,48,1024]{2,1,0:T(8,128)(2,1)S(1)} collective-permute-done((f16[2,48,1024]{2,1,0:T(8,128)(2,1)S(1)}, f16[2,48,1024]{2,1,0:T(8,128)(2,1)S(1)}, u32[]{:S(2)}, u32[]{:S(2)}) %collective-permute-start.6) | collective-permute-done | bytes 196640 | tf_op jit(solution)/shard_map/ppermute | solution.py:33
  67.6 1.5 %collective-permute-start.7 = (f16[48,1024]{1,0:T(8,128)(2,1)S(1)}, f16[48,1024]{1,0:T(8,128)(2,1)S(1)}, u32[]{:S(2)}, u32[]{:S(2)}) collective-permute-start(f16[48,1024]{1,0:T(8,128)(2,1)S(1)} %get-tuple-element.35), channel_id=1, source_target_pairs={{0,28},{1,29},{4,24},{5,25},{8,20},{9,21},{12,16},{13,17},{16,12},... | collective-permute-start | bytes 294920 | tf_op jit(solution)/shard_map/ppermute | solution.py:33
  69.1 0.8 %all-to-all-done.2 = bf16[8,48,1024]{2,1,0:T(8,128)(2,1)S(1)} async-done(((bf16[8,48,1024]{2,1,0:T(8,128)(2,1)}), bf16[8,48,1024]{2,1,0:T(8,128)(2,1)S(1)}, u32[]{:S(2)}, u32[]{:S(2)}) %all-to-all-start.2) | async-done | bytes 786464 | tf_op jit(solution)/shard_map/all_to_all | solution.py:37
  69.9 0.8 %convert_reduce_fusion = f32[48,1024]{1,0:T(8,128)} fusion(bf16[8,48,1024]{2,1,0:T(8,128)(2,1)S(1)} %all-to-all-done.2), kind=kLoop, calls=%fused_computation | loop fusion | flops 737280 | bytes 983040 | tf_op jit(solution)/shard_map/reduce_sum | solution.py:323
  70.6 3.3 %collective-permute-done.7 = f16[48,1024]{1,0:T(8,128)(2,1)S(1)} collective-permute-done((f16[48,1024]{1,0:T(8,128)(2,1)S(1)}, f16[48,1024]{1,0:T(8,128)(2,1)S(1)}, u32[]{:S(2)}, u32[]{:S(2)}) %collective-permute-start.7) | collective-permute-done | bytes 98336 | tf_op jit(solution)/shard_map/ppermute | solution.py:33
  73.9 0.7 add_multiply_fusion
  (22 shorter events, 0.1 us)
Async XLA Ops:
  0.6 22.4 %copy-start = (bf16[384,1024]{1,0:T(8,128)(2,1)S(1)}, bf16[384,1024]{1,0:T(8,128)(2,1)}, u32[]{:S(2)}) copy-start(bf16[384,1024]{1,0:T(8,128)(2,1)} %t0.1) | copy-start | bytes 2359300
  0.6 30.1 %copy-start.8 = (s32[1536]{0:T(1024)S(1)}, s32[1536]{0:T(1024)}, u32[]{:S(2)}) copy-start(s32[1536]{0:T(1024)} %param.5) | copy-start | bytes 18436
  0.7 25.1 %collective-permute-start = (bf16[384,1024]{1,0:T(8,128)(2,1)}, bf16[384,1024]{1,0:T(8,128)(2,1)S(1)}, u32[]{:S(2)}, u32[]{:S(2)}) collective-permute-start(bf16[384,1024]{1,0:T(8,128)(2,1)} %t0.1), channel_id=1, source_target_pairs={{0,2},{2,0},{1,3},{3,1},{4,6},{6,4},{5,7},{7,5},{8,10},{10,8},{9,1... | collective-permute-start | bytes 2359304 | tf_op jit(solution)/shard_map/ppermute | solution.py:28
  9.4 10.9 %collective-permute-start.1 = (f32[1,1664]{1,0:T(1,128)}, f32[1,1664]{1,0:T(1,128)S(1)}, u32[]{:S(2)}, u32[]{:S(2)}) collective-permute-start(f32[1,1664]{1,0:T(1,128)} %get-tuple-element.18), channel_id=1, source_target_pairs={{0,28},{1,29},{4,24},{5,25},{8,20},{9,21},{12,16},{13,17},{16,12},... | collective-permute-start | bytes 19976 | tf_op jit(solution)/shard_map/ppermute | solution.py:33
  15.3 9.7 %all-to-all-start = ((f32[8,1,384]{2,1,0:T(1,128)}), f32[8,1,384]{2,1,0:T(1,128)S(1)}, u32[]{:S(2)}, u32[]{:S(2)}) async-start(f32[8,1,384]{2,1,0:T(1,128)} %get-tuple-element.17), calls=%async_computation | async-start | bytes 24576 | tf_op jit(solution)/shard_map/all_to_all | solution.py:37
  21.0 4.0 %collective-permute-start.2 = (f32[1,1664]{1,0:T(1,128)S(1)}, f32[1,1664]{1,0:T(1,128)S(1)}, u32[]{:S(2)}, u32[]{:S(2)}) collective-permute-start(f32[1,1664]{1,0:T(1,128)S(1)} %compare_select_fusion.row_ref), channel_id=1, source_target_pairs={{0,4},{1,5},{4,0},{5,1},{8,12},{9,13},{12,8},{13,9},{16,20},{17,21... | collective-permute-start | bytes 19976 | tf_op jit(solution)/shard_map/ppermute | solution.py:33
  23.0 9.0 %collective-permute-start.3 = (bf16[384,1024]{1,0:T(8,128)(2,1)S(1)}, bf16[384,1024]{1,0:T(8,128)(2,1)S(1)}, u32[]{:S(2)}, u32[]{:S(2)}) collective-permute-start(bf16[384,1024]{1,0:T(8,128)(2,1)S(1)} %copy-done), channel_id=1, source_target_pairs={{0,1},{1,0},{2,3},{3,2},{4,5},{5,4},{6,7},{7,6},{8,9},{9,8},{10,11... | collective-permute-start | bytes 2359304 | tf_op jit(solution)/shard_map/ppermute | solution.py:28
  25.7 12.6 %copy-start.2 = (bf16[384,1024]{1,0:T(8,128)(2,1)}, bf16[384,1024]{1,0:T(8,128)(2,1)S(1)}, u32[]{:S(2)}) copy-start(bf16[384,1024]{1,0:T(8,128)(2,1)S(1)} %collective-permute-done.t2) | copy-start | bytes 2359300
  25.7 12.6 %collective-permute-start.4 = (bf16[384,1024]{1,0:T(8,128)(2,1)S(1)}, bf16[384,1024]{1,0:T(8,128)(2,1)S(1)}, u32[]{:S(2)}, u32[]{:S(2)}) collective-permute-start(bf16[384,1024]{1,0:T(8,128)(2,1)S(1)} %collective-permute-done.t2), channel_id=1, source_target_pairs={{0,1},{1,0},{2,3},{3,2},{4,5},{5,4},{6,7},{7,6},{8,9},{9,8},{10,11... | collective-permute-start | bytes 2359304 | tf_op jit(solution)/shard_map/ppermute | solution.py:28
  25.7 12.5 %all-to-all-start.1 = ((f32[8,1,2048]{2,1,0:T(1,128)}), f32[8,1,2048]{2,1,0:T(1,128)S(1)}, u32[]{:S(2)}, u32[]{:S(2)}) async-start(f32[8,1,2048]{2,1,0:T(1,128)} %merge.1), calls=%async_computation.1 | async-start | bytes 131072 | tf_op jit(solution)/shard_map/all_to_all | solution.py:37
  32.0 6.3 %copy-start.3 = (bf16[384,1024]{1,0:T(8,128)(2,1)}, bf16[384,1024]{1,0:T(8,128)(2,1)S(1)}, u32[]{:S(2)}) copy-start(bf16[384,1024]{1,0:T(8,128)(2,1)S(1)} %collective-permute-done.3.t1) | copy-start | bytes 2359300
  38.3 0.6 copy-start.5
  38.3 0.9 %copy-start.4 = (bf16[384,1024]{1,0:T(8,128)(2,1)}, bf16[384,1024]{1,0:T(8,128)(2,1)S(1)}, u32[]{:S(2)}) copy-start(bf16[384,1024]{1,0:T(8,128)(2,1)S(1)} %collective-permute-done.4.t3) | copy-start | bytes 2359300
  46.5 12.2 %collective-permute-start.5 = (bf16[4,48,1024]{2,1,0:T(8,128)(2,1)}, bf16[4,48,1024]{2,1,0:T(8,128)(2,1)S(1)}, u32[]{:S(2)}, u32[]{:S(2)}) collective-permute-start(bf16[4,48,1024]{2,1,0:T(8,128)(2,1)} %get-tuple-element.22), channel_id=1, source_target_pairs={{0,4},{1,9},{4,0},{5,13},{8,12},{9,1},{12,8},{13,5},{16,20},{17,25... | collective-permute-start | bytes 1179656 | tf_op jit(solution)/shard_map/ppermute | solution.py:33
  46.7 12.1 %copy-start.6 = (f32[2,48,1024]{2,1,0:T(8,128)S(1)}, f32[2,48,1024]{2,1,0:T(8,128)}, u32[]{:S(2)}) copy-start(f32[2,48,1024]{2,1,0:T(8,128)} %get-tuple-element.21) | copy-start | bytes 1179652
  52.5 6.4 %copy-start.1 = (f32[48,1024]{1,0:T(8,128)S(1)}, f32[48,1024]{1,0:T(8,128)}, u32[]{:S(2)}) copy-start(f32[48,1024]{1,0:T(8,128)} %get-tuple-element.24.after_ref) | copy-start | bytes 589828
  52.5 6.4 %copy-start.7 = (f32[48,1024]{1,0:T(8,128)S(1)}, f32[48,1024]{1,0:T(8,128)}, u32[]{:S(2)}) copy-start(f32[48,1024]{1,0:T(8,128)} %get-tuple-element.23) | copy-start | bytes 589828
  52.6 21.4 %copy-start.9 = (f32[1,128]{1,0:T(1,128)S(1)}, f32[1,128]{1,0:T(1,128)}, u32[]{:S(2)}) copy-start(f32[1,128]{1,0:T(1,128)} %get-tuple-element.30) | copy-start | bytes 1540
  52.6 17.3 %all-to-all-start.2 = ((bf16[8,48,1024]{2,1,0:T(8,128)(2,1)}), bf16[8,48,1024]{2,1,0:T(8,128)(2,1)S(1)}, u32[]{:S(2)}, u32[]{:S(2)}) async-start(bf16[8,48,1024]{2,1,0:T(8,128)(2,1)} %text_part.1), calls=%async_computation.2 | async-start | bytes 1572864 | tf_op jit(solution)/shard_map/all_to_all | solution.py:37
  58.8 8.8 %collective-permute-start.6 = (f16[2,48,1024]{2,1,0:T(8,128)(2,1)S(1)}, f16[2,48,1024]{2,1,0:T(8,128)(2,1)S(1)}, u32[]{:S(2)}, u32[]{:S(2)}) collective-permute-start(f16[2,48,1024]{2,1,0:T(8,128)(2,1)S(1)} %add_convert_fusion), channel_id=1, source_target_pairs={{0,8},{1,5},{4,12},{5,1},{8,0},{9,13},{12,4},{13,9},{16,24},{17,21... | collective-permute-start | bytes 589832 | tf_op jit(solution)/shard_map/ppermute | solution.py:33
  67.6 6.3 %collective-permute-start.7 = (f16[48,1024]{1,0:T(8,128)(2,1)S(1)}, f16[48,1024]{1,0:T(8,128)(2,1)S(1)}, u32[]{:S(2)}, u32[]{:S(2)}) collective-permute-start(f16[48,1024]{1,0:T(8,128)(2,1)S(1)} %get-tuple-element.35), channel_id=1, source_target_pairs={{0,28},{1,29},{4,24},{5,25},{8,20},{9,21},{12,16},{13,17},{16,12},... | collective-permute-start | bytes 294920 | tf_op jit(solution)/shard_map/ppermute | solution.py:33

commit v5 on v4

--- a/solution.py
+++ b/solution.py
@@ -83,13 +83,17 @@
     row_ref[:, rows:] = jnp.broadcast_to(largest(text), (1, LANES))
     high = total = None
     store = []
-    for k, j in enumerate(steps):
-        fetch[1 + k].wait()
-        logits = nt_dot(text, image_ref[j : j + size]) * scale
-        logits_ref[:, j : j + size] = logits
-        where = pl.ds(j, size)
-        store.append(pltpu.make_async_copy(logits_ref.at[:, where], logits_out.at[:, where], sems.at[4 + k]))
-        store[k].start()
+    for k in range(len(steps) + 1):
+        if k < len(steps):
+            fetch[1 + k].wait()
+            where = pl.ds(steps[k], size)
+            logits_ref[:, where] = nt_dot(text, image_ref[where]) * scale
+            store.append(pltpu.make_async_copy(logits_ref.at[:, where], logits_out.at[:, where], sems.at[4 + k]))
+            store[k].start()
+        if k == 0:
+            continue
+        j = steps[k - 1]
+        logits = logits_ref[:, j : j + size]
         deep = logits.reshape(cols // 8, 8, size)
         top = jnp.max(deep, axis=0)
         part = jnp.sum(jnp.exp2(deep - top[None]), axis=0)
@@ -166,7 +170,7 @@
     return jnp.maximum(peak, 1e-30) * 0.125
 
 
-def text_kernel(at_ref, logits_in, stat_ref, match_ref, image_in, after_ref, out_ref, logits_ref, image_ref, weights, sems):
+def text_kernel(at_ref, logits_in, stat_in, match_in, image_in, after_ref, out_ref, stat_ref, match_ref, logits_ref, image_ref, weights, sems):
     cols, rows = logits_in.shape
     size = rows // 4
     steps = range(0, rows, size)
@@ -175,8 +179,11 @@
         for k, j in enumerate(steps)
     ]
     fetch.append(pltpu.make_async_copy(image_in, image_ref, sems.at[4]))
-    for copy in fetch:
+    facts = [pltpu.make_async_copy(stat_in, stat_ref, sems.at[5]), pltpu.make_async_copy(match_in, match_ref, sems.at[6])]
+    for copy in facts + fetch:
         copy.start()
+    for copy in facts:
+        copy.wait()
     row = log2_sum(stat_ref[:, 0, :rows], 0)
     col = stat_ref[at_ref[7] + at_ref[0], :, rows + LANES :]
     col = jnp.transpose(jnp.broadcast_to(col, (LANES, cols)))[:, :1]
@@ -195,14 +202,16 @@
     width = images.shape[1]
     return pl.pallas_call(
         text_kernel,
-        in_specs=[SCALARS, HBM, VMEM, VMEM, HBM, HBM],
+        in_specs=[SCALARS] + [HBM] * 5,
         out_specs=VMEM,
         out_shape=jax.ShapeDtypeStruct((8, cols // 8, width), BF16),
         scratch_shapes=[
+            pltpu.VMEM(stats.shape, F32),
+            pltpu.VMEM(match.shape, jnp.int32),
             pltpu.VMEM((cols, rows), F32),
             pltpu.VMEM(images.shape, BF16),
             pltpu.VMEM((cols, rows), BF16),
-            pltpu.SemaphoreType.DMA((5,)),
+            pltpu.SemaphoreType.DMA((7,)),
         ],
         compiler_params=params(60),
         cost_estimate=FREE,
@@ -210,16 +219,20 @@
     )(at, logits, stats, match, images, after)
 
 
-def image_kernel(scale, at_ref, stat_ref, match_ref, image_ref, t0, t1, t2, t3, a_ref, b_ref, c_ref, d_ref, down_ref, own, four, row_all, weights, sems):
+def image_kernel(scale, at_ref, stat_in, match_in, image_ref, t0, t1, t2, t3, a_ref, b_ref, c_ref, d_ref, down_ref, stat_ref, match_ref, own, four, row_by, match_by, weights, sems):
     texts = (t0, t1, t2, t3)
     blocks, _, per, width = image_ref.shape
     cols = t0.shape[0]
     rows = blocks * per
-    every = match_ref.shape[1]
+    every = match_in.shape[1]
     place, z, core, first = at_ref[0], at_ref[5], at_ref[6], at_ref[7]
     one, two = 1 + core, 2 - core
     order = [z ^ one, z ^ one ^ 7, z ^ 3, z ^ 4, z ^ two, z ^ two ^ 7, z ^ 7, z]
     fetch = [
+        pltpu.make_async_copy(stat_in, stat_ref, sems.at[5]),
+        pltpu.make_async_copy(match_in, match_ref, sems.at[6]),
+    ]
+    fetch += [
         pltpu.make_async_copy(image_ref.at[block, place], own.at[k], sems.at[4]) for k, block in enumerate(order)
     ]
     fetch += [
@@ -227,29 +240,32 @@
     ]
     for copy in fetch:
         copy.start()
-    row_all[...] = log2_sum(stat_ref[:, 0, :every], 0)
-    span = 2 * LANES
-    lanes = lax.broadcasted_iota(jnp.int32, (per, span), 1) - lax.broadcasted_iota(jnp.int32, (per, span), 0)
-    row, match = [], []
-    for block in order:
-        begin = block * (4 * per) + place * per
-        start = jnp.minimum(begin // LANES * LANES, every - span)
-        window = pl.ds(pl.multiple_of(start, LANES), span)
-        wanted = lanes == begin - start
-        row.append(jnp.sum(jnp.where(wanted, row_all[:, window], 0.0), axis=1, keepdims=True))
-        match.append(jnp.sum(jnp.where(wanted, match_ref[:, window], 0), axis=1, keepdims=True))
-    row = jnp.concatenate(row, axis=0)
-    match = jnp.concatenate(match, axis=0)
+    fetch[0].wait()
+    fetch[1].wait()
+    row_all = log2_sum(stat_ref[:, 0, :every], 0)
+    pair = lax.broadcasted_iota(jnp.int32, (2 * per, 1), 0)
+    lane = pair + jnp.where(pair < per, 0, 3 * per) + place * per
+    wanted = lax.broadcasted_iota(jnp.int32, (2 * per, 8 * per), 1) == lane
+    for k, j in enumerate(range(0, every, 8 * per)):
+        window = slice(j, j + 8 * per)
+        row = jnp.sum(jnp.where(wanted, row_all[:, window], 0.0), axis=1, keepdims=True)
+        match = jnp.sum(jnp.where(wanted, match_ref[:, window], 0), axis=1, keepdims=True)
+        row_by[2 * k : 2 * k + 2] = row.reshape(2, per, 1)
+        match_by[2 * k : 2 * k + 2] = match.reshape(2, per, 1)
+    row = jnp.concatenate([row_by[block] for block in order], axis=0)
+    match = jnp.concatenate([match_by[block] for block in order], axis=0)
     ids = lax.broadcasted_iota(jnp.int32, (rows, cols), 1)
-    for copy in fetch[:8]:
+    for copy in fetch[2:10]:
         copy.wait()
     mine = own[...].reshape(rows, width)
-    for k in range(4):
-        fetch[8 + k].wait()
-        where = slice(k * cols, (k + 1) * cols)
-        logits = nt_dot(mine, four[where]) * scale
-        col = stat_ref[first + (place ^ k), :, every + LANES :]
-        weights[:, where] = weigh(logits, row, col, match - at_ref[1 + k] == ids)
+    for group in ((0,), (1, 2, 3)):
+        for k in group:
+            fetch[10 + k].wait()
+        for k in group:
+            where = slice(k * cols, (k + 1) * cols)
+            logits = nt_dot(mine, four[where]) * scale
+            col = stat_ref[first + (place ^ k), :, every + LANES :]
+            weights[:, where] = weigh(logits, row, col, match - at_ref[1 + k] == ids)
     peak = jnp.max(stat_ref[:, 0, every : every + LANES], axis=0, keepdims=True)
     down_ref[...] = down_scale(peak)
     part = jnp.dot(weights[...], four[...], preferred_element_type=F32) * up_scale(peak[:, :1])
@@ -268,15 +284,18 @@
     kinds = [BF16, F32, F32, F32, F32]
     return pl.pallas_call(
         functools.partial(image_kernel, scale),
-        in_specs=[SCALARS, VMEM, VMEM] + [HBM] * 5,
+        in_specs=[SCALARS] + [HBM] * 7,
         out_specs=[VMEM] * 5,
         out_shape=[jax.ShapeDtypeStruct(s, t) for s, t in zip(outs, kinds)],
         scratch_shapes=[
+            pltpu.VMEM(stats.shape, F32),
+            pltpu.VMEM(match.shape, jnp.int32),
             pltpu.VMEM((8, per, width), BF16),
             pltpu.VMEM((4 * cols, width), BF16),
-            pltpu.VMEM((1, rows), F32),
+            pltpu.VMEM((8, per, 1), F32),
+            pltpu.VMEM((8, per, 1), jnp.int32),
             pltpu.VMEM((own, 4 * cols), BF16),
-            pltpu.SemaphoreType.DMA((5,)),
+            pltpu.SemaphoreType.DMA((7,)),
         ],
         compiler_params=params(60),
         cost_estimate=FREE,

time: 75.1 us -> 74 us (0.985)
  Pallas kernels: 19.3 us -> 18.2 us
where the time goes in v5:
time: 74 us; the launch traced here: 73.6 us
  starting transfers between devices  28.5 us (39%)
  waiting for transfers between devices  21.6 us (29%)
  Pallas kernels  18.2 us (25%)
  other arithmetic  2.39 us (3%)
  local copies, waits for them, and re-layouts  2.16 us (3%)
  between operations  0.75 us (1%)
    all_to_all x3, starting transfers between devices, exchange(): return lax.all_to_all(copies, axes, 0, 0, tiled=True)  15 us
    ppermute x5, waiting for transfers between devices, z_swap(): return lax.ppermute(value, ('zhi', 'zb', 'za', 'core'), pairs)  12.6 us
    ppermute x5, starting transfers between devices, z_swap(): return lax.ppermute(value, ('zhi', 'zb', 'za', 'core'), pairs)  10.1 us
    all_to_all x3, waiting for transfers between devices, exchange(): return lax.all_to_all(copies, axes, 0, 0, tiled=True)  8.97 us
    pallas_call x1, Pallas kernels, image_call(): pl.pallas_call(functools.partial(image_kernel, scale), in_specs=[SCALARS]...  6.73 us
    pallas_call x1, Pallas kernels, text_call(): pl.pallas_call(text_kernel, in_specs=[SCALARS] + [HBM] * 5, out_specs=VME...  5.81 us
    pallas_call x1, Pallas kernels, first_call(): pl.pallas_call(functools.partial(first_kernel, scale), in_specs=[HBM] * 2...  5.02 us
    ppermute x3, starting transfers between devices, swap(): return lax.ppermute(value, axis, [(0, 1), (1, 0)])  3.29 us
  transfers between devices with their start and end apart: 11, of which 6 were waited for; matrix products, arithmetic and copies ran while one was open for 4% of the time, Pallas kernels for 16%

profile of v5, /device:TPU:2, one launch (start us, length us, event | category | flops | bytes accessed | tf_op | source)
XLA Modules:
  0.0 73.6 jit_solution(10976878508218978455)
XLA Ops:
  0.6 0.0 copy-start
  0.7 3.3 %collective-permute-start = (bf16[384,1024]{1,0:T(8,128)(2,1)}, bf16[384,1024]{1,0:T(8,128)(2,1)S(1)}, u32[]{:S(2)}, u32[]{:S(2)}) collective-permute-start(bf16[384,1024]{1,0:T(8,128)(2,1)} %t0.1), channel_id=1, source_target_pairs={{0,2},{2,0},{1,3},{3,1},{4,6},{6,4},{5,7},{7,5},{8,10},{10,8},{9,1... | collective-permute-start | bytes 2359304 | tf_op jit(solution)/shard_map/ppermute | solution.py:28
  3.9 5.0 %logits.1 = (f32[384,1536]{1,0:T(8,128)}, f32[1,1664]{1,0:T(1,128)}, f32[8,1,384]{2,1,0:T(1,128)}) custom-call(bf16[384,1024]{1,0:T(8,128)(2,1)} %t0.1, bf16[1536,1024]{1,0:T(8,128)(2,1)} %image_in.3), custom_call_target="tpu_custom_call" | custom-call | tf_op jit(solution)/shard_map/logits/pallas_call | solution.py:121
  9.0 5.9 %collective-permute-start.1 = (f32[1,1664]{1,0:T(1,128)}, f32[1,1664]{1,0:T(1,128)S(1)}, u32[]{:S(2)}, u32[]{:S(2)}) collective-permute-start(f32[1,1664]{1,0:T(1,128)} %get-tuple-element.18), channel_id=1, source_target_pairs={{0,28},{1,29},{4,24},{5,25},{8,20},{9,21},{12,16},{13,17},{16,12},... | collective-permute-start | bytes 19976 | tf_op jit(solution)/shard_map/ppermute | solution.py:33
  14.9 4.9 %all-to-all-start = ((f32[8,1,384]{2,1,0:T(1,128)}), f32[8,1,384]{2,1,0:T(1,128)S(1)}, u32[]{:S(2)}, u32[]{:S(2)}) async-start(f32[8,1,384]{2,1,0:T(1,128)} %get-tuple-element.17), calls=%async_computation | async-start | bytes 24576 | tf_op jit(solution)/shard_map/all_to_all | solution.py:37
  19.9 0.7 compare_select_fusion.row_ref
  20.6 2.0 %collective-permute-start.2 = (f32[1,1664]{1,0:T(1,128)S(1)}, f32[1,1664]{1,0:T(1,128)S(1)}, u32[]{:S(2)}, u32[]{:S(2)}) collective-permute-start(f32[1,1664]{1,0:T(1,128)S(1)} %compare_select_fusion.row_ref), channel_id=1, source_target_pairs={{0,4},{1,5},{4,0},{5,1},{8,12},{9,13},{12,8},{13,9},{16,20},{17,21... | collective-permute-start | bytes 19976 | tf_op jit(solution)/shard_map/ppermute | solution.py:33
  22.6 2.0 %all-to-all-done.got_ref = f32[8,1,384]{2,1,0:T(1,128)S(1)} async-done(((f32[8,1,384]{2,1,0:T(1,128)}), f32[8,1,384]{2,1,0:T(1,128)S(1)}, u32[]{:S(2)}, u32[]{:S(2)}) %all-to-all-start) | async-done | bytes 12320 | tf_op jit(solution)/shard_map/all_to_all | solution.py:37
  24.6 0.7 merge.1
  25.3 0.0 collective-permute-done.t2
  25.3 5.0 %all-to-all-start.1 = ((f32[8,1,2048]{2,1,0:T(1,128)}), f32[8,1,2048]{2,1,0:T(1,128)S(1)}, u32[]{:S(2)}, u32[]{:S(2)}) async-start(f32[8,1,2048]{2,1,0:T(1,128)} %merge.1), calls=%async_computation.1 | async-start | bytes 131072 | tf_op jit(solution)/shard_map/all_to_all | solution.py:37
  30.3 0.6 broadcast_in_dim.3.match_in
  30.9 0.6 stack.35.at_ref
  31.6 0.0 collective-permute-done.3.t1
  31.6 6.5 %all-to-all-done.1.stat_in = f32[8,1,2048]{2,1,0:T(1,128)S(1)} async-done(((f32[8,1,2048]{2,1,0:T(1,128)}), f32[8,1,2048]{2,1,0:T(1,128)S(1)}, u32[]{:S(2)}, u32[]{:S(2)}) %all-to-all-start.1) | async-done | bytes 65568 | tf_op jit(solution)/shard_map/all_to_all | solution.py:37
  38.1 0.6 copy-done.5
  38.7 0.3 copy-done.4
  39.0 6.7 %image_part.1 = (bf16[4,48,1024]{2,1,0:T(8,128)(2,1)}, f32[2,48,1024]{2,1,0:T(8,128)}, f32[48,1024]{1,0:T(8,128)}, f32[48,1024]{1,0:T(8,128)}, f32[1,128]{1,0:T(1,128)}) custom-call(s32[8]{0:T(128)} %stack.35.at_ref, f32[8,1,2048]{2,1,0:T(1,128)} %copy-done.5, s32[1,1536]{1,0:T(1,128)} %broadcast_in_dim.3.match_in, bf16[8,4,48,1024]{3,2,1,0:T(8,128)(2,1)} %bitcast.27, ...), custom_call_target="tpu_custom_call" | custom-call | tf_op jit(solution)/shard_map/image_part/pallas_call | solution.py:285
  45.7 0.3 collective-permute-start.5
  46.0 5.8 %text_part.1 = bf16[8,48,1024]{2,1,0:T(8,128)(2,1)} custom-call(s32[8]{0:T(128)} %stack.35.at_ref, f32[384,1536]{1,0:T(8,128)} %get-tuple-element.31.logits_in, f32[8,1,2048]{2,1,0:T(1,128)} %copy-done.5, s32[1,1536]{1,0:T(1,128)} %broadcast_in_dim.3.match_in, bf16[1536,1024]{1,0:T(8,128)(2,1)} %image_in.3, f32[48,1024]{1,0:T(8,128)} %get-tuple-element.24.after_ref), custom_call_target="tpu_custom_call" | custom-call | tf_op jit(solution)/shard_map/text_part/pallas_call | solution.py:203
  51.9 0.0 copy-start.1
  51.9 0.0 copy-start.7
  51.9 5.1 %all-to-all-start.2 = ((bf16[8,48,1024]{2,1,0:T(8,128)(2,1)}), bf16[8,48,1024]{2,1,0:T(8,128)(2,1)S(1)}, u32[]{:S(2)}, u32[]{:S(2)}) async-start(bf16[8,48,1024]{2,1,0:T(8,128)(2,1)} %text_part.1), calls=%async_computation.2 | async-start | bytes 1572864 | tf_op jit(solution)/shard_map/all_to_all | solution.py:37
  57.0 0.8 %collective-permute-done.5 = bf16[4,48,1024]{2,1,0:T(8,128)(2,1)S(1)} collective-permute-done((bf16[4,48,1024]{2,1,0:T(8,128)(2,1)}, bf16[4,48,1024]{2,1,0:T(8,128)(2,1)S(1)}, u32[]{:S(2)}, u32[]{:S(2)}) %collective-permute-start.5) | collective-permute-done | bytes 393248 | tf_op jit(solution)/shard_map/ppermute | solution.py:33
  57.8 0.1 add_convert_fusion
  57.9 0.2 collective-permute-start.6
  58.1 8.5 %collective-permute-done.6 = f16[2,48,1024]{2,1,0:T(8,128)(2,1)S(1)} collective-permute-done((f16[2,48,1024]{2,1,0:T(8,128)(2,1)S(1)}, f16[2,48,1024]{2,1,0:T(8,128)(2,1)S(1)}, u32[]{:S(2)}, u32[]{:S(2)}) %collective-permute-start.6) | collective-permute-done | bytes 196640 | tf_op jit(solution)/shard_map/ppermute | solution.py:33
  66.7 1.7 %collective-permute-start.7 = (f16[48,1024]{1,0:T(8,128)(2,1)S(1)}, f16[48,1024]{1,0:T(8,128)(2,1)S(1)}, u32[]{:S(2)}, u32[]{:S(2)}) collective-permute-start(f16[48,1024]{1,0:T(8,128)(2,1)S(1)} %get-tuple-element.35), channel_id=1, source_target_pairs={{0,28},{1,29},{4,24},{5,25},{8,20},{9,21},{12,16},{13,17},{16,12},... | collective-permute-start | bytes 294920 | tf_op jit(solution)/shard_map/ppermute | solution.py:33
  68.4 0.4 all-to-all-done.2
  68.8 0.8 %convert_reduce_fusion = f32[48,1024]{1,0:T(8,128)} fusion(bf16[8,48,1024]{2,1,0:T(8,128)(2,1)S(1)} %all-to-all-done.2), kind=kLoop, calls=%fused_computation | loop fusion | flops 737280 | bytes 983040 | tf_op jit(solution)/shard_map/reduce_sum | solution.py:342
  69.6 3.3 %collective-permute-done.7 = f16[48,1024]{1,0:T(8,128)(2,1)S(1)} collective-permute-done((f16[48,1024]{1,0:T(8,128)(2,1)S(1)}, f16[48,1024]{1,0:T(8,128)(2,1)S(1)}, u32[]{:S(2)}, u32[]{:S(2)}) %collective-permute-start.7) | collective-permute-done | bytes 98336 | tf_op jit(solution)/shard_map/ppermute | solution.py:33
  72.9 0.7 %add_multiply_fusion = f32[48,1024]{1,0:T(8,128)} fusion(f32[48,1024]{1,0:T(8,128)S(1)} %get-tuple-element.28, f16[48,1024]{1,0:T(8,128)(2,1)S(1)} %collective-permute-done.7, f32[]{:T(128)S(1)} %bitcast.28), kind=kLoop, calls=%fused_computation.7 | loop fusion | flops 147456 | bytes 491524 | tf_op jit(solution)/shard_map/mul | solution.py:344
  (22 shorter events, 0.1 us)
Async XLA Ops:
  0.6 22.0 %copy-start = (bf16[384,1024]{1,0:T(8,128)(2,1)S(1)}, bf16[384,1024]{1,0:T(8,128)(2,1)}, u32[]{:S(2)}) copy-start(bf16[384,1024]{1,0:T(8,128)(2,1)} %t0.1) | copy-start | bytes 2359300
  0.6 29.7 %copy-start.8 = (s32[1536]{0:T(1024)S(1)}, s32[1536]{0:T(1024)}, u32[]{:S(2)}) copy-start(s32[1536]{0:T(1024)} %param.5) | copy-start | bytes 18436
  0.7 24.7 %collective-permute-start = (bf16[384,1024]{1,0:T(8,128)(2,1)}, bf16[384,1024]{1,0:T(8,128)(2,1)S(1)}, u32[]{:S(2)}, u32[]{:S(2)}) collective-permute-start(bf16[384,1024]{1,0:T(8,128)(2,1)} %t0.1), channel_id=1, source_target_pairs={{0,2},{2,0},{1,3},{3,1},{4,6},{6,4},{5,7},{7,5},{8,10},{10,8},{9,1... | collective-permute-start | bytes 2359304 | tf_op jit(solution)/shard_map/ppermute | solution.py:28
  9.0 10.9 %collective-permute-start.1 = (f32[1,1664]{1,0:T(1,128)}, f32[1,1664]{1,0:T(1,128)S(1)}, u32[]{:S(2)}, u32[]{:S(2)}) collective-permute-start(f32[1,1664]{1,0:T(1,128)} %get-tuple-element.18), channel_id=1, source_target_pairs={{0,28},{1,29},{4,24},{5,25},{8,20},{9,21},{12,16},{13,17},{16,12},... | collective-permute-start | bytes 19976 | tf_op jit(solution)/shard_map/ppermute | solution.py:33
  14.9 9.7 %all-to-all-start = ((f32[8,1,384]{2,1,0:T(1,128)}), f32[8,1,384]{2,1,0:T(1,128)S(1)}, u32[]{:S(2)}, u32[]{:S(2)}) async-start(f32[8,1,384]{2,1,0:T(1,128)} %get-tuple-element.17), calls=%async_computation | async-start | bytes 24576 | tf_op jit(solution)/shard_map/all_to_all | solution.py:37
  20.6 4.0 %collective-permute-start.2 = (f32[1,1664]{1,0:T(1,128)S(1)}, f32[1,1664]{1,0:T(1,128)S(1)}, u32[]{:S(2)}, u32[]{:S(2)}) collective-permute-start(f32[1,1664]{1,0:T(1,128)S(1)} %compare_select_fusion.row_ref), channel_id=1, source_target_pairs={{0,4},{1,5},{4,0},{5,1},{8,12},{9,13},{12,8},{13,9},{16,20},{17,21... | collective-permute-start | bytes 19976 | tf_op jit(solution)/shard_map/ppermute | solution.py:33
  22.6 9.0 %collective-permute-start.3 = (bf16[384,1024]{1,0:T(8,128)(2,1)S(1)}, bf16[384,1024]{1,0:T(8,128)(2,1)S(1)}, u32[]{:S(2)}, u32[]{:S(2)}) collective-permute-start(bf16[384,1024]{1,0:T(8,128)(2,1)S(1)} %copy-done), channel_id=1, source_target_pairs={{0,1},{1,0},{2,3},{3,2},{4,5},{5,4},{6,7},{7,6},{8,9},{9,8},{10,11... | collective-permute-start | bytes 2359304 | tf_op jit(solution)/shard_map/ppermute | solution.py:28
  25.3 12.8 %copy-start.2 = (bf16[384,1024]{1,0:T(8,128)(2,1)}, bf16[384,1024]{1,0:T(8,128)(2,1)S(1)}, u32[]{:S(2)}) copy-start(bf16[384,1024]{1,0:T(8,128)(2,1)S(1)} %collective-permute-done.t2) | copy-start | bytes 2359300
  25.3 12.8 %collective-permute-start.4 = (bf16[384,1024]{1,0:T(8,128)(2,1)S(1)}, bf16[384,1024]{1,0:T(8,128)(2,1)S(1)}, u32[]{:S(2)}, u32[]{:S(2)}) collective-permute-start(bf16[384,1024]{1,0:T(8,128)(2,1)S(1)} %collective-permute-done.t2), channel_id=1, source_target_pairs={{0,1},{1,0},{2,3},{3,2},{4,5},{5,4},{6,7},{7,6},{8,9},{9,8},{10,11... | collective-permute-start | bytes 2359304 | tf_op jit(solution)/shard_map/ppermute | solution.py:28
  25.3 12.8 %all-to-all-start.1 = ((f32[8,1,2048]{2,1,0:T(1,128)}), f32[8,1,2048]{2,1,0:T(1,128)S(1)}, u32[]{:S(2)}, u32[]{:S(2)}) async-start(f32[8,1,2048]{2,1,0:T(1,128)} %merge.1), calls=%async_computation.1 | async-start | bytes 131072 | tf_op jit(solution)/shard_map/all_to_all | solution.py:37
  31.6 6.5 %copy-start.3 = (bf16[384,1024]{1,0:T(8,128)(2,1)}, bf16[384,1024]{1,0:T(8,128)(2,1)S(1)}, u32[]{:S(2)}) copy-start(bf16[384,1024]{1,0:T(8,128)(2,1)S(1)} %collective-permute-done.3.t1) | copy-start | bytes 2359300
  38.1 0.6 copy-start.5
  38.1 0.9 %copy-start.4 = (bf16[384,1024]{1,0:T(8,128)(2,1)}, bf16[384,1024]{1,0:T(8,128)(2,1)S(1)}, u32[]{:S(2)}) copy-start(bf16[384,1024]{1,0:T(8,128)(2,1)S(1)} %collective-permute-done.4.t3) | copy-start | bytes 2359300
  45.7 12.1 %collective-permute-start.5 = (bf16[4,48,1024]{2,1,0:T(8,128)(2,1)}, bf16[4,48,1024]{2,1,0:T(8,128)(2,1)S(1)}, u32[]{:S(2)}, u32[]{:S(2)}) collective-permute-start(bf16[4,48,1024]{2,1,0:T(8,128)(2,1)} %get-tuple-element.22), channel_id=1, source_target_pairs={{0,4},{1,9},{4,0},{5,13},{8,12},{9,1},{12,8},{13,5},{16,20},{17,25... | collective-permute-start | bytes 1179656 | tf_op jit(solution)/shard_map/ppermute | solution.py:33
  46.0 11.8 %copy-start.6 = (f32[2,48,1024]{2,1,0:T(8,128)S(1)}, f32[2,48,1024]{2,1,0:T(8,128)}, u32[]{:S(2)}) copy-start(f32[2,48,1024]{2,1,0:T(8,128)} %get-tuple-element.21) | copy-start | bytes 1179652
  51.9 6.2 %copy-start.1 = (f32[48,1024]{1,0:T(8,128)S(1)}, f32[48,1024]{1,0:T(8,128)}, u32[]{:S(2)}) copy-start(f32[48,1024]{1,0:T(8,128)} %get-tuple-element.24.after_ref) | copy-start | bytes 589828
  51.9 6.2 %copy-start.7 = (f32[48,1024]{1,0:T(8,128)S(1)}, f32[48,1024]{1,0:T(8,128)}, u32[]{:S(2)}) copy-start(f32[48,1024]{1,0:T(8,128)} %get-tuple-element.23) | copy-start | bytes 589828
  51.9 21.0 %copy-start.9 = (f32[1,128]{1,0:T(1,128)S(1)}, f32[1,128]{1,0:T(1,128)}, u32[]{:S(2)}) copy-start(f32[1,128]{1,0:T(1,128)} %get-tuple-element.30) | copy-start | bytes 1540
  51.9 16.9 %all-to-all-start.2 = ((bf16[8,48,1024]{2,1,0:T(8,128)(2,1)}), bf16[8,48,1024]{2,1,0:T(8,128)(2,1)S(1)}, u32[]{:S(2)}, u32[]{:S(2)}) async-start(bf16[8,48,1024]{2,1,0:T(8,128)(2,1)} %text_part.1), calls=%async_computation.2 | async-start | bytes 1572864 | tf_op jit(solution)/shard_map/all_to_all | solution.py:37
  57.9 8.8 %collective-permute-start.6 = (f16[2,48,1024]{2,1,0:T(8,128)(2,1)S(1)}, f16[2,48,1024]{2,1,0:T(8,128)(2,1)S(1)}, u32[]{:S(2)}, u32[]{:S(2)}) collective-permute-start(f16[2,48,1024]{2,1,0:T(8,128)(2,1)S(1)} %add_convert_fusion), channel_id=1, source_target_pairs={{0,8},{1,5},{4,12},{5,1},{8,0},{9,13},{12,4},{13,9},{16,24},{17,21... | collective-permute-start | bytes 589832 | tf_op jit(solution)/shard_map/ppermute | solution.py:33
  66.7 6.2 %collective-permute-start.7 = (f16[48,1024]{1,0:T(8,128)(2,1)S(1)}, f16[48,1024]{1,0:T(8,128)(2,1)S(1)}, u32[]{:S(2)}, u32[]{:S(2)}) collective-permute-start(f16[48,1024]{1,0:T(8,128)(2,1)S(1)} %get-tuple-element.35), channel_id=1, source_target_pairs={{0,28},{1,29},{4,24},{5,25},{8,20},{9,21},{12,16},{13,17},{16,12},... | collective-permute-start | bytes 294920 | tf_op jit(solution)/shard_map/ppermute | solution.py:33

commit v6 on v5

--- a/solution.py
+++ b/solution.py
@@ -17,6 +17,7 @@
 F16 = jnp.float16
 LOG2E = 1.4426950408889634
 HBM = pl.BlockSpec(memory_space=pltpu.HBM)
+ANY = pl.BlockSpec(memory_space=pl.ANY)
 VMEM = pl.BlockSpec(memory_space=pltpu.VMEM)
 SCALARS = pl.BlockSpec(memory_space=pltpu.SMEM)
 FREE = pl.CostEstimate(flops=0, bytes_accessed=0, transcendentals=0)
@@ -202,7 +203,7 @@
     width = images.shape[1]
     return pl.pallas_call(
         text_kernel,
-        in_specs=[SCALARS] + [HBM] * 5,
+        in_specs=[SCALARS, HBM, ANY, ANY, HBM, ANY],
         out_specs=VMEM,
         out_shape=jax.ShapeDtypeStruct((8, cols // 8, width), BF16),
         scratch_shapes=[
@@ -213,7 +214,7 @@
             pltpu.VMEM((cols, rows), BF16),
             pltpu.SemaphoreType.DMA((7,)),
         ],
-        compiler_params=params(60),
+        compiler_params=params(50),
         cost_estimate=FREE,
         name="text_part",
     )(at, logits, stats, match, images, after)
@@ -284,7 +285,7 @@
     kinds = [BF16, F32, F32, F32, F32]
     return pl.pallas_call(
         functools.partial(image_kernel, scale),
-        in_specs=[SCALARS] + [HBM] * 7,
+        in_specs=[SCALARS, ANY, ANY] + [HBM] * 5,
         out_specs=[VMEM] * 5,
         out_shape=[jax.ShapeDtypeStruct(s, t) for s, t in zip(outs, kinds)],
         scratch_shapes=[
@@ -297,7 +298,7 @@
             pltpu.VMEM((own, 4 * cols), BF16),
             pltpu.SemaphoreType.DMA((7,)),
         ],
-        compiler_params=params(60),
+        compiler_params=params(50),
         cost_estimate=FREE,
         name="image_part",
     )(at, stats, match, images.reshape(8, 4, per, width), *texts)
@@ -328,7 +329,7 @@
     at = jnp.stack([place, *bases, z, core, zb * 4])
     match = match[None]
     a, b, c, d, down = image_call(at, stats, match, images, (texts, other_core, other_yhi, other_both), scale)
-    text_parts = text_call(at, logits, stats, match, images, d)
+    text_parts = text_call(at, logits, stats, match, images, down)
 
     a = z_swap(a, (1, 2))
     b = (b + a[2:].astype(F32)).astype(F16)

time: 74 us -> 72.7 us (0.982)
  waiting for transfers between devices: 21.6 us -> 24.5 us
  starting transfers between devices: 28.5 us -> 26.8 us
  Pallas kernels: 18.2 us -> 17 us
  local copies, waits for them, and re-layouts: 2.16 us -> 0.99 us
    all_to_all x3, waiting for transfers between devices: 8.97 us -> 11.2 us  [exchange(): return lax.all_to_all(copies, axes, 0, 0, tiled=True)]
    ppermute x5, starting transfers between devices: 10.1 us -> 8.57 us  [z_swap(): return lax.ppermute(value, ('zhi', 'zb', 'za', 'core'), pairs)]
    pallas_call x2, Pallas kernels: 12.5 us -> 11.3 us  [the longest x1 6.25 us: image_call(): pl.pallas_call(functools.partial(image_kernel, scale), in_specs=[SCALARS,...]
  transfers between devices with their start and end apart: 11 -> 11, of which waited for: 6 -> 6; matrix products, arithmetic and copies ran while one was open for 4% -> 2% of each run, Pallas kernels for 16% -> 15%
where the time goes in v6:
time: 72.7 us; the launch traced here: 72.4 us
  starting transfers between devices  26.8 us (37%)
  waiting for transfers between devices  24.5 us (34%)
  Pallas kernels  17 us (23%)
  other arithmetic  2.39 us (3%)
  local copies, waits for them, and re-layouts  0.99 us (1%)
    all_to_all x3, starting transfers between devices, exchange(): return lax.all_to_all(copies, axes, 0, 0, tiled=True)  14.9 us
    ppermute x5, waiting for transfers between devices, z_swap(): return lax.ppermute(value, ('zhi', 'zb', 'za', 'core'), pairs)  13.3 us
    all_to_all x3, waiting for transfers between devices, exchange(): return lax.all_to_all(copies, axes, 0, 0, tiled=True)  11.2 us
    ppermute x5, starting transfers between devices, z_swap(): return lax.ppermute(value, ('zhi', 'zb', 'za', 'core'), pairs)  8.57 us
    pallas_call x1, Pallas kernels, image_call(): pl.pallas_call(functools.partial(image_kernel, scale), in_specs=[SCALARS,...  6.25 us
    pallas_call x1, Pallas kernels, text_call(): pl.pallas_call(text_kernel, in_specs=[SCALARS, HBM, ANY, ANY, HBM, ANY],...  5.06 us
    pallas_call x1, Pallas kernels, first_call(): pl.pallas_call(functools.partial(first_kernel, scale), in_specs=[HBM] * 2...  5.03 us
    ppermute x3, starting transfers between devices, swap(): return lax.ppermute(value, axis, [(0, 1), (1, 0)])  3.29 us
  transfers between devices with their start and end apart: 11, of which 6 were waited for; matrix products, arithmetic and copies ran while one was open for 2% of the time, Pallas kernels for 15%

profile of v6, /device:TPU:2, one launch (start us, length us, event | category | flops | bytes accessed | tf_op | source)
XLA Modules:
  0.0 72.4 jit_solution(3656089054913999461)
XLA Ops:
  0.6 3.3 %collective-permute-start = (bf16[384,1024]{1,0:T(8,128)(2,1)}, bf16[384,1024]{1,0:T(8,128)(2,1)S(1)}, u32[]{:S(2)}, u32[]{:S(2)}) collective-permute-start(bf16[384,1024]{1,0:T(8,128)(2,1)} %t0.1), channel_id=1, source_target_pairs={{0,2},{2,0},{1,3},{3,1},{4,6},{6,4},{5,7},{7,5},{8,10},{10,8},{9,1... | collective-permute-start | bytes 2359304 | tf_op jit(solution)/shard_map/ppermute | solution.py:29
  3.9 5.0 %logits.1 = (f32[384,1536]{1,0:T(8,128)}, f32[1,1664]{1,0:T(1,128)}, f32[8,1,384]{2,1,0:T(1,128)}) custom-call(bf16[384,1024]{1,0:T(8,128)(2,1)} %t0.1, bf16[1536,1024]{1,0:T(8,128)(2,1)} %image_in.3), custom_call_target="tpu_custom_call" | custom-call | tf_op jit(solution)/shard_map/logits/pallas_call | solution.py:122
  9.0 5.9 %collective-permute-start.1 = (f32[1,1664]{1,0:T(1,128)}, f32[1,1664]{1,0:T(1,128)S(1)}, u32[]{:S(2)}, u32[]{:S(2)}) collective-permute-start(f32[1,1664]{1,0:T(1,128)} %get-tuple-element.18), channel_id=1, source_target_pairs={{0,28},{1,29},{4,24},{5,25},{8,20},{9,21},{12,16},{13,17},{16,12},... | collective-permute-start | bytes 19976 | tf_op jit(solution)/shard_map/ppermute | solution.py:34
  14.9 4.9 %all-to-all-start = ((f32[8,1,384]{2,1,0:T(1,128)}), f32[8,1,384]{2,1,0:T(1,128)S(1)}, u32[]{:S(2)}, u32[]{:S(2)}) async-start(f32[8,1,384]{2,1,0:T(1,128)} %get-tuple-element.17), calls=%async_computation | async-start | bytes 24576 | tf_op jit(solution)/shard_map/all_to_all | solution.py:38
  19.9 0.0 collective-permute-done.1
  19.9 0.7 %compare_select_fusion.row_ref = f32[1,1664]{1,0:T(1,128)S(1)} fusion(f32[1,1664]{1,0:T(1,128)S(1)} %collective-permute-done.1, f32[1,1664]{1,0:T(1,128)} %get-tuple-element.18), kind=kLoop, calls=%fused_computation.10 | loop fusion | flops 16640 | bytes 19968 | tf_op jit(solution)/shard_map/jit(_where)/select_n | solution.py:54
  20.6 2.0 %collective-permute-start.2 = (f32[1,1664]{1,0:T(1,128)S(1)}, f32[1,1664]{1,0:T(1,128)S(1)}, u32[]{:S(2)}, u32[]{:S(2)}) collective-permute-start(f32[1,1664]{1,0:T(1,128)S(1)} %compare_select_fusion.row_ref), channel_id=1, source_target_pairs={{0,4},{1,5},{4,0},{5,1},{8,12},{9,13},{12,8},{13,9},{16,20},{17,21... | collective-permute-start | bytes 19976 | tf_op jit(solution)/shard_map/ppermute | solution.py:34
  22.6 0.0 collective-permute-start.3
  22.6 2.0 %all-to-all-done.got_ref = f32[8,1,384]{2,1,0:T(1,128)S(1)} async-done(((f32[8,1,384]{2,1,0:T(1,128)}), f32[8,1,384]{2,1,0:T(1,128)S(1)}, u32[]{:S(2)}, u32[]{:S(2)}) %all-to-all-start) | async-done | bytes 12320 | tf_op jit(solution)/shard_map/all_to_all | solution.py:38
  24.6 0.0 collective-permute-done.2.near_ref
  24.6 0.7 merge.1
  25.3 0.0 collective-permute-done.t2
  25.3 0.0 collective-permute-start.4
  25.3 5.0 %all-to-all-start.1 = ((f32[8,1,2048]{2,1,0:T(1,128)}), f32[8,1,2048]{2,1,0:T(1,128)S(1)}, u32[]{:S(2)}, u32[]{:S(2)}) async-start(f32[8,1,2048]{2,1,0:T(1,128)} %merge.1), calls=%async_computation.1 | async-start | bytes 131072 | tf_op jit(solution)/shard_map/all_to_all | solution.py:38
  30.4 0.1 stack.35.at_ref
  30.4 0.0 collective-permute-done.3.t1
  30.5 7.6 %all-to-all-done.1.stat_in = f32[8,1,2048]{2,1,0:T(1,128)S(1)} async-done(((f32[8,1,2048]{2,1,0:T(1,128)}), f32[8,1,2048]{2,1,0:T(1,128)S(1)}, u32[]{:S(2)}, u32[]{:S(2)}) %all-to-all-start.1) | async-done | bytes 65568 | tf_op jit(solution)/shard_map/all_to_all | solution.py:38
  38.1 0.0 collective-permute-done.4.t3
  38.1 0.9 %copy-done.2 = bf16[384,1024]{1,0:T(8,128)(2,1)} copy-done((bf16[384,1024]{1,0:T(8,128)(2,1)}, bf16[384,1024]{1,0:T(8,128)(2,1)S(1)}, u32[]{:S(2)}) %copy-start.2) | copy-done | bytes 786456
  39.0 6.2 %image_part.1 = (bf16[4,48,1024]{2,1,0:T(8,128)(2,1)}, f32[2,48,1024]{2,1,0:T(8,128)S(1)}, f32[48,1024]{1,0:T(8,128)S(1)}, f32[48,1024]{1,0:T(8,128)S(1)}, f32[1,128]{1,0:T(1,128)S(1)}) custom-call(s32[8]{0:T(128)S(1)} %stack.35.at_ref, f32[8,1,2048]{2,1,0:T(1,128)S(1)} %all-to-all-done.1.stat_in, s32[1,1536]{1,0:T(1,128)S(1)} %broadcast_in_dim.3.match_in, ...), custom_call_target="tpu_custom_call" | custom-call | tf_op jit(solution)/shard_map/image_part/pallas_call | solution.py:286
  45.2 0.3 collective-permute-start.5
  45.5 5.1 %text_part.1 = bf16[8,48,1024]{2,1,0:T(8,128)(2,1)} custom-call(s32[8]{0:T(128)S(1)} %stack.35.at_ref, f32[384,1536]{1,0:T(8,128)S(1)} %copy-done.1, f32[8,1,2048]{2,1,0:T(1,128)S(1)} %all-to-all-done.1.stat_in, s32[1,1536]{1,0:T(1,128)S(1)} %broadcast_in_dim.3.match_in, bf16[1536,1024]{1,0:T(8,128)(2,1)} %image_in.3, f32[1,128]{1,0:T(1,128)S(1)} %get-tuple-element.30.after_ref), custom_call_target="tpu_custom_call" | custom-call | tf_op jit(solution)/shard_map/text_part/pallas_call | solution.py:204
  50.6 5.0 %all-to-all-start.2 = ((bf16[8,48,1024]{2,1,0:T(8,128)(2,1)}), bf16[8,48,1024]{2,1,0:T(8,128)(2,1)S(1)}, u32[]{:S(2)}, u32[]{:S(2)}) async-start(bf16[8,48,1024]{2,1,0:T(8,128)(2,1)} %text_part.1), calls=%async_computation.2 | async-start | bytes 1572864 | tf_op jit(solution)/shard_map/all_to_all | solution.py:38
  55.6 1.7 %collective-permute-done.5 = bf16[4,48,1024]{2,1,0:T(8,128)(2,1)S(1)} collective-permute-done((bf16[4,48,1024]{2,1,0:T(8,128)(2,1)}, bf16[4,48,1024]{2,1,0:T(8,128)(2,1)S(1)}, u32[]{:S(2)}, u32[]{:S(2)}) %collective-permute-start.5) | collective-permute-done | bytes 393248 | tf_op jit(solution)/shard_map/ppermute | solution.py:34
  57.3 0.1 add_convert_fusion
  57.4 0.2 collective-permute-start.6
  57.6 8.1 %collective-permute-done.6 = f16[2,48,1024]{2,1,0:T(8,128)(2,1)S(1)} collective-permute-done((f16[2,48,1024]{2,1,0:T(8,128)(2,1)S(1)}, f16[2,48,1024]{2,1,0:T(8,128)(2,1)S(1)}, u32[]{:S(2)}, u32[]{:S(2)}) %collective-permute-start.6) | collective-permute-done | bytes 196640 | tf_op jit(solution)/shard_map/ppermute | solution.py:34
  65.7 0.2 collective-permute-start.7
  65.9 1.5 %all-to-all-done.2 = bf16[8,48,1024]{2,1,0:T(8,128)(2,1)S(1)} async-done(((bf16[8,48,1024]{2,1,0:T(8,128)(2,1)}), bf16[8,48,1024]{2,1,0:T(8,128)(2,1)S(1)}, u32[]{:S(2)}, u32[]{:S(2)}) %all-to-all-start.2) | async-done | bytes 786464 | tf_op jit(solution)/shard_map/all_to_all | solution.py:38
  67.4 0.8 %convert_reduce_fusion = f32[48,1024]{1,0:T(8,128)} fusion(bf16[8,48,1024]{2,1,0:T(8,128)(2,1)S(1)} %all-to-all-done.2), kind=kLoop, calls=%fused_computation | loop fusion | flops 737280 | bytes 983040 | tf_op jit(solution)/shard_map/reduce_sum | solution.py:343
  68.2 3.5 %collective-permute-done.7 = f16[48,1024]{1,0:T(8,128)(2,1)S(1)} collective-permute-done((f16[48,1024]{1,0:T(8,128)(2,1)S(1)}, f16[48,1024]{1,0:T(8,128)(2,1)S(1)}, u32[]{:S(2)}, u32[]{:S(2)}) %collective-permute-start.7) | collective-permute-done | bytes 98336 | tf_op jit(solution)/shard_map/ppermute | solution.py:34
  71.6 0.7 %add_multiply_fusion = f32[48,1024]{1,0:T(8,128)} fusion(f32[48,1024]{1,0:T(8,128)S(1)} %get-tuple-element.28, f16[48,1024]{1,0:T(8,128)(2,1)S(1)} %collective-permute-done.7, f32[]{:T(128)S(1)} %bitcast.27), kind=kLoop, calls=%fused_computation.7 | loop fusion | flops 147456 | bytes 491524 | tf_op jit(solution)/shard_map/mul | solution.py:345
  (10 shorter events, 0.1 us)
Async XLA Ops:
  0.6 22.0 %copy-start = (bf16[384,1024]{1,0:T(8,128)(2,1)S(1)}, bf16[384,1024]{1,0:T(8,128)(2,1)}, u32[]{:S(2)}) copy-start(bf16[384,1024]{1,0:T(8,128)(2,1)} %t0.1) | copy-start | bytes 2359300
  0.6 29.7 %copy-start.3 = (s32[1536]{0:T(1024)S(1)}, s32[1536]{0:T(1024)}, u32[]{:S(2)}) copy-start(s32[1536]{0:T(1024)} %param.5) | copy-start | bytes 18436
  0.6 24.7 %collective-permute-start = (bf16[384,1024]{1,0:T(8,128)(2,1)}, bf16[384,1024]{1,0:T(8,128)(2,1)S(1)}, u32[]{:S(2)}, u32[]{:S(2)}) collective-permute-start(bf16[384,1024]{1,0:T(8,128)(2,1)} %t0.1), channel_id=1, source_target_pairs={{0,2},{2,0},{1,3},{3,1},{4,6},{6,4},{5,7},{7,5},{8,10},{10,8},{9,1... | collective-permute-start | bytes 2359304 | tf_op jit(solution)/shard_map/ppermute | solution.py:29
  9.0 10.9 %collective-permute-start.1 = (f32[1,1664]{1,0:T(1,128)}, f32[1,1664]{1,0:T(1,128)S(1)}, u32[]{:S(2)}, u32[]{:S(2)}) collective-permute-start(f32[1,1664]{1,0:T(1,128)} %get-tuple-element.18), channel_id=1, source_target_pairs={{0,28},{1,29},{4,24},{5,25},{8,20},{9,21},{12,16},{13,17},{16,12},... | collective-permute-start | bytes 19976 | tf_op jit(solution)/shard_map/ppermute | solution.py:34
  14.9 9.7 %all-to-all-start = ((f32[8,1,384]{2,1,0:T(1,128)}), f32[8,1,384]{2,1,0:T(1,128)S(1)}, u32[]{:S(2)}, u32[]{:S(2)}) async-start(f32[8,1,384]{2,1,0:T(1,128)} %get-tuple-element.17), calls=%async_computation | async-start | bytes 24576 | tf_op jit(solution)/shard_map/all_to_all | solution.py:38
  20.6 4.0 %collective-permute-start.2 = (f32[1,1664]{1,0:T(1,128)S(1)}, f32[1,1664]{1,0:T(1,128)S(1)}, u32[]{:S(2)}, u32[]{:S(2)}) collective-permute-start(f32[1,1664]{1,0:T(1,128)S(1)} %compare_select_fusion.row_ref), channel_id=1, source_target_pairs={{0,4},{1,5},{4,0},{5,1},{8,12},{9,13},{12,8},{13,9},{16,20},{17,21... | collective-permute-start | bytes 19976 | tf_op jit(solution)/shard_map/ppermute | solution.py:34
  22.6 7.9 %collective-permute-start.3 = (bf16[384,1024]{1,0:T(8,128)(2,1)S(1)}, bf16[384,1024]{1,0:T(8,128)(2,1)S(1)}, u32[]{:S(2)}, u32[]{:S(2)}) collective-permute-start(bf16[384,1024]{1,0:T(8,128)(2,1)S(1)} %copy-done), channel_id=1, source_target_pairs={{0,1},{1,0},{2,3},{3,2},{4,5},{5,4},{6,7},{7,6},{8,9},{9,8},{10,11... | collective-permute-start | bytes 2359304 | tf_op jit(solution)/shard_map/ppermute | solution.py:29
  25.3 12.8 %collective-permute-start.4 = (bf16[384,1024]{1,0:T(8,128)(2,1)S(1)}, bf16[384,1024]{1,0:T(8,128)(2,1)S(1)}, u32[]{:S(2)}, u32[]{:S(2)}) collective-permute-start(bf16[384,1024]{1,0:T(8,128)(2,1)S(1)} %collective-permute-done.t2), channel_id=1, source_target_pairs={{0,1},{1,0},{2,3},{3,2},{4,5},{5,4},{6,7},{7,6},{8,9},{9,8},{10,11... | collective-permute-start | bytes 2359304 | tf_op jit(solution)/shard_map/ppermute | solution.py:29
  25.3 12.8 %all-to-all-start.1 = ((f32[8,1,2048]{2,1,0:T(1,128)}), f32[8,1,2048]{2,1,0:T(1,128)S(1)}, u32[]{:S(2)}, u32[]{:S(2)}) async-start(f32[8,1,2048]{2,1,0:T(1,128)} %merge.1), calls=%async_computation.1 | async-start | bytes 131072 | tf_op jit(solution)/shard_map/all_to_all | solution.py:38
  38.1 0.9 %copy-start.2 = (bf16[384,1024]{1,0:T(8,128)(2,1)}, bf16[384,1024]{1,0:T(8,128)(2,1)S(1)}, u32[]{:S(2)}) copy-start(bf16[384,1024]{1,0:T(8,128)(2,1)S(1)} %collective-permute-done.4.t3) | copy-start | bytes 2359300
  39.0 6.6 %copy-start.1 = (f32[384,1536]{1,0:T(8,128)S(1)}, f32[384,1536]{1,0:T(8,128)}, u32[]{:S(2)}) copy-start(f32[384,1536]{1,0:T(8,128)} %get-tuple-element.31.logits_in) | copy-start | bytes 7077892
  45.2 12.1 %collective-permute-start.5 = (bf16[4,48,1024]{2,1,0:T(8,128)(2,1)}, bf16[4,48,1024]{2,1,0:T(8,128)(2,1)S(1)}, u32[]{:S(2)}, u32[]{:S(2)}) collective-permute-start(bf16[4,48,1024]{2,1,0:T(8,128)(2,1)} %get-tuple-element.22), channel_id=1, source_target_pairs={{0,4},{1,9},{4,0},{5,13},{8,12},{9,1},{12,8},{13,5},{16,20},{17,25... | collective-permute-start | bytes 1179656 | tf_op jit(solution)/shard_map/ppermute | solution.py:34
  50.6 16.8 %all-to-all-start.2 = ((bf16[8,48,1024]{2,1,0:T(8,128)(2,1)}), bf16[8,48,1024]{2,1,0:T(8,128)(2,1)S(1)}, u32[]{:S(2)}, u32[]{:S(2)}) async-start(bf16[8,48,1024]{2,1,0:T(8,128)(2,1)} %text_part.1), calls=%async_computation.2 | async-start | bytes 1572864 | tf_op jit(solution)/shard_map/all_to_all | solution.py:38
  57.4 8.3 %collective-permute-start.6 = (f16[2,48,1024]{2,1,0:T(8,128)(2,1)S(1)}, f16[2,48,1024]{2,1,0:T(8,128)(2,1)S(1)}, u32[]{:S(2)}, u32[]{:S(2)}) collective-permute-start(f16[2,48,1024]{2,1,0:T(8,128)(2,1)S(1)} %add_convert_fusion), channel_id=1, source_target_pairs={{0,8},{1,5},{4,12},{5,1},{8,0},{9,13},{12,4},{13,9},{16,24},{17,21... | collective-permute-start | bytes 589832 | tf_op jit(solution)/shard_map/ppermute | solution.py:34
  65.7 5.9 %collective-permute-start.7 = (f16[48,1024]{1,0:T(8,128)(2,1)S(1)}, f16[48,1024]{1,0:T(8,128)(2,1)S(1)}, u32[]{:S(2)}, u32[]{:S(2)}) collective-permute-start(f16[48,1024]{1,0:T(8,128)(2,1)S(1)} %get-tuple-element.35), channel_id=1, source_target_pairs={{0,28},{1,29},{4,24},{5,25},{8,20},{9,21},{12,16},{13,17},{16,12},... | collective-permute-start | bytes 294920 | tf_op jit(solution)/shard_map/ppermute | solution.py:34

commit v7 on v6

--- a/solution.py
+++ b/solution.py
@@ -220,7 +220,25 @@
     )(at, logits, stats, match, images, after)
 
 
-def image_kernel(scale, at_ref, stat_in, match_in, image_ref, t0, t1, t2, t3, a_ref, b_ref, c_ref, d_ref, down_ref, stat_ref, match_ref, own, four, row_by, match_by, weights, sems):
+def settle_kernel(in_ref, out_ref, sem):
+    copy = pltpu.make_async_copy(in_ref, out_ref, sem)
+    copy.start()
+    copy.wait()
+
+
+def settle(value):
+    return pl.pallas_call(
+        settle_kernel,
+        in_specs=[VMEM],
+        out_specs=HBM,
+        out_shape=jax.ShapeDtypeStruct(value.shape, value.dtype),
+        scratch_shapes=[pltpu.SemaphoreType.DMA],
+        cost_estimate=FREE,
+        name="settle",
+    )(value)
+
+
+def image_kernel(scale, at_ref, stat_in, match_in, image_ref, t0, t1, t2, t3, e_ref, a_ref, b_ref, c_ref, d_ref, down_ref, stat_ref, match_ref, own, four, row_by, match_by, weights, sems):
     texts = (t0, t1, t2, t3)
     blocks, _, per, width = image_ref.shape
     cols = t0.shape[0]
@@ -228,7 +246,7 @@
     every = match_in.shape[1]
     place, z, core, first = at_ref[0], at_ref[5], at_ref[6], at_ref[7]
     one, two = 1 + core, 2 - core
-    order = [z ^ one, z ^ one ^ 7, z ^ 3, z ^ 4, z ^ two, z ^ two ^ 7, z ^ 7, z]
+    order = [z ^ 3, z ^ 4, z ^ one, z ^ one ^ 7, z ^ two, z ^ two ^ 7, z ^ 7, z]
     fetch = [
         pltpu.make_async_copy(stat_in, stat_ref, sems.at[5]),
         pltpu.make_async_copy(match_in, match_ref, sems.at[6]),
@@ -270,7 +288,8 @@
     peak = jnp.max(stat_ref[:, 0, every : every + LANES], axis=0, keepdims=True)
     down_ref[...] = down_scale(peak)
     part = jnp.dot(weights[...], four[...], preferred_element_type=F32) * up_scale(peak[:, :1])
-    a_ref[...] = part[: 4 * per].astype(a_ref.dtype).reshape(a_ref.shape)
+    e_ref[...] = part[: 2 * per].astype(e_ref.dtype).reshape(e_ref.shape)
+    a_ref[...] = part[2 * per : 4 * per].astype(a_ref.dtype).reshape(a_ref.shape)
     b_ref[...] = part[4 * per : 6 * per].reshape(b_ref.shape)
     c_ref[...] = part[6 * per : 7 * per]
     d_ref[...] = part[7 * per :]
@@ -281,12 +300,12 @@
     cols = texts[0].shape[0]
     own = rows // 4
     per = rows // 32
-    outs = [(4, per, width), (2, per, width), (per, width), (per, width), (1, LANES)]
-    kinds = [BF16, F32, F32, F32, F32]
+    outs = [(2, per, width), (2, per, width), (2, per, width), (per, width), (per, width), (1, LANES)]
+    kinds = [BF16, BF16, F32, F32, F32, F32]
     return pl.pallas_call(
         functools.partial(image_kernel, scale),
         in_specs=[SCALARS, ANY, ANY] + [HBM] * 5,
-        out_specs=[VMEM] * 5,
+        out_specs=[VMEM] * 6,
         out_shape=[jax.ShapeDtypeStruct(s, t) for s, t in zip(outs, kinds)],
         scratch_shapes=[
             pltpu.VMEM(stats.shape, F32),
@@ -323,17 +342,22 @@
     sent = merge_call(got, row, near)
     other_yhi, sent = tie(other_yhi, sent)
     stats = exchange(sent, ("zb", "yhi", "core"))
-    other_both = swap(other_yhi, "core")
+    other_both = settle(swap(other_yhi, "core"))
 
     bases = [(z * 4 + (place ^ k)) * cols for k in range(4)]
     at = jnp.stack([place, *bases, z, core, zb * 4])
     match = match[None]
-    a, b, c, d, down = image_call(at, stats, match, images, (texts, other_core, other_yhi, other_both), scale)
+    e, a, b, c, d, down = image_call(at, stats, match, images, (texts, other_core, other_yhi, other_both), scale)
     text_parts = text_call(at, logits, stats, match, images, down)
 
+    e = z_swap(e, (1, 2))
     a = z_swap(a, (1, 2))
-    b = (b + a[2:].astype(F32)).astype(F16)
+    e, text_parts = tie(e, text_parts)
+    b = (b + e.astype(F32)).astype(F16)
+    b, down = tie(b, down)
     b = z_swap(b, (2, 1))
+    down = swap(down, "core")
+    down, text_parts = tie(down, text_parts)
     c = c + a[1].astype(F32)
     d = d + a[0].astype(F32)
     text_parts = exchange(text_parts, IMG)

time: 72.7 us -> 72.8 us (level)
  the two profiles are of different devices: /device:TPU:2 before, /device:TPU:1 now
where the time goes in v7:
time: 72.8 us; the launch traced here: 72.4 us
  starting transfers between devices  31.1 us (43%)
  waiting for transfers between devices  19.7 us (27%)
  Pallas kernels  18.3 us (25%)
  other arithmetic  2.42 us (3%)
  between operations  0.74 us (1%)
    all_to_all x3, starting transfers between devices, exchange(): return lax.all_to_all(copies, axes, 0, 0, tiled=True)  13 us
    ppermute x6, starting transfers between devices, z_swap(): return lax.ppermute(value, ('zhi', 'zb', 'za', 'core'), pairs)  10.7 us
    all_to_all x3, waiting for transfers between devices, exchange(): return lax.all_to_all(copies, axes, 0, 0, tiled=True)  9.89 us
    ppermute x6, waiting for transfers between devices, z_swap(): return lax.ppermute(value, ('zhi', 'zb', 'za', 'core'), pairs)  8.96 us
    ppermute x4, starting transfers between devices, swap(): return lax.ppermute(value, axis, [(0, 1), (1, 0)])  7.48 us
    pallas_call x1, Pallas kernels, image_call(): pl.pallas_call(functools.partial(image_kernel, scale), in_specs=[SCALARS,...  5.54 us
    pallas_call x1, Pallas kernels, text_call(): pl.pallas_call(text_kernel, in_specs=[SCALARS, HBM, ANY, ANY, HBM, ANY],...  5.06 us
    pallas_call x1, Pallas kernels, first_call(): pl.pallas_call(functools.partial(first_kernel, scale), in_specs=[HBM] * 2...  5.04 us
  transfers between devices with their start and end apart: 13, of which 7 were waited for; matrix products, arithmetic and copies ran while one was open for 2% of the time, Pallas kernels for 18%

profile of v7, /device:TPU:1, one launch (start us, length us, event | category | flops | bytes accessed | tf_op | source)
XLA Modules:
  0.0 72.4 jit_solution(4954903784499249858)
XLA Ops:
  0.6 3.8 %collective-permute-start = (bf16[384,1024]{1,0:T(8,128)(2,1)}, bf16[384,1024]{1,0:T(8,128)(2,1)S(1)}, u32[]{:S(2)}, u32[]{:S(2)}) collective-permute-start(bf16[384,1024]{1,0:T(8,128)(2,1)} %t0.1), channel_id=1, source_target_pairs={{0,2},{2,0},{1,3},{3,1},{4,6},{6,4},{5,7},{7,5},{8,10},{10,8},{9,1... | collective-permute-start | bytes 2359304 | tf_op jit(solution)/shard_map/ppermute | solution.py:29
  4.5 5.0 %logits.1 = (f32[384,1536]{1,0:T(8,128)}, f32[1,1664]{1,0:T(1,128)}, f32[8,1,384]{2,1,0:T(1,128)}) custom-call(bf16[384,1024]{1,0:T(8,128)(2,1)} %t0.1, bf16[1536,1024]{1,0:T(8,128)(2,1)} %image_in.3), custom_call_target="tpu_custom_call" | custom-call | tf_op jit(solution)/shard_map/logits/pallas_call | solution.py:122
  9.5 5.7 %collective-permute-start.1 = (f32[1,1664]{1,0:T(1,128)}, f32[1,1664]{1,0:T(1,128)S(1)}, u32[]{:S(2)}, u32[]{:S(2)}) collective-permute-start(f32[1,1664]{1,0:T(1,128)} %get-tuple-element.25), channel_id=1, source_target_pairs={{0,28},{1,29},{4,24},{5,25},{8,20},{9,21},{12,16},{13,17},{16,12},... | collective-permute-start | bytes 19976 | tf_op jit(solution)/shard_map/ppermute | solution.py:34
  15.2 4.1 %all-to-all-start = ((f32[8,1,384]{2,1,0:T(1,128)}), f32[8,1,384]{2,1,0:T(1,128)S(1)}, u32[]{:S(2)}, u32[]{:S(2)}) async-start(f32[8,1,384]{2,1,0:T(1,128)} %get-tuple-element.24), calls=%async_computation | async-start | bytes 24576 | tf_op jit(solution)/shard_map/all_to_all | solution.py:38
  19.3 0.0 collective-permute-done.1
  19.3 0.7 %compare_select_fusion.row_ref = f32[1,1664]{1,0:T(1,128)S(1)} fusion(f32[1,1664]{1,0:T(1,128)S(1)} %collective-permute-done.1, f32[1,1664]{1,0:T(1,128)} %get-tuple-element.25), kind=kLoop, calls=%fused_computation.10 | loop fusion | flops 16640 | bytes 19968 | tf_op jit(solution)/shard_map/jit(_where)/select_n | solution.py:54
  20.1 1.7 %collective-permute-start.2 = (f32[1,1664]{1,0:T(1,128)S(1)}, f32[1,1664]{1,0:T(1,128)S(1)}, u32[]{:S(2)}, u32[]{:S(2)}) collective-permute-start(f32[1,1664]{1,0:T(1,128)S(1)} %compare_select_fusion.row_ref), channel_id=1, source_target_pairs={{0,4},{1,5},{4,0},{5,1},{8,12},{9,13},{12,8},{13,9},{16,20},{17,21... | collective-permute-start | bytes 19976 | tf_op jit(solution)/shard_map/ppermute | solution.py:34
  21.8 2.6 %all-to-all-done.got_ref = f32[8,1,384]{2,1,0:T(1,128)S(1)} async-done(((f32[8,1,384]{2,1,0:T(1,128)}), f32[8,1,384]{2,1,0:T(1,128)S(1)}, u32[]{:S(2)}, u32[]{:S(2)}) %all-to-all-start) | async-done | bytes 12320 | tf_op jit(solution)/shard_map/all_to_all | solution.py:38
  24.4 0.7 merge.1
  25.1 0.0 collective-permute-done.t2
  25.1 2.7 %collective-permute-start.4 = (bf16[384,1024]{1,0:T(8,128)(2,1)S(1)}, bf16[384,1024]{1,0:T(8,128)(2,1)}, u32[]{:S(2)}, u32[]{:S(2)}) collective-permute-start(bf16[384,1024]{1,0:T(8,128)(2,1)S(1)} %collective-permute-done.t2), channel_id=1, source_target_pairs={{0,1},{1,0},{2,3},{3,2},{4,5},{5,4},{6,7},{7,6},{8,9},{9,8},{10,11... | collective-permute-start | bytes 2359304 | tf_op jit(solution)/shard_map/ppermute | solution.py:29
  27.7 0.1 collective-permute-start.3
  27.8 5.3 %all-to-all-start.1 = ((f32[8,1,2048]{2,1,0:T(1,128)}), f32[8,1,2048]{2,1,0:T(1,128)S(1)}, u32[]{:S(2)}, u32[]{:S(2)}) async-start(f32[8,1,2048]{2,1,0:T(1,128)} %merge.1), calls=%async_computation.1 | async-start | bytes 131072 | tf_op jit(solution)/shard_map/all_to_all | solution.py:38
  33.1 0.1 stack.35.at_ref
  33.2 2.0 %settle.1.t3 = bf16[384,1024]{1,0:T(8,128)(2,1)} custom-call(bf16[384,1024]{1,0:T(8,128)(2,1)} %collective-permute-done.4.in_ref), custom_call_target="tpu_custom_call" | custom-call | tf_op jit(solution)/shard_map/settle/pallas_call | solution.py:230
  35.3 4.7 %all-to-all-done.1.stat_in = f32[8,1,2048]{2,1,0:T(1,128)S(1)} async-done(((f32[8,1,2048]{2,1,0:T(1,128)}), f32[8,1,2048]{2,1,0:T(1,128)S(1)}, u32[]{:S(2)}, u32[]{:S(2)}) %all-to-all-start.1) | async-done | bytes 65568 | tf_op jit(solution)/shard_map/all_to_all | solution.py:38
  40.1 5.5 %image_part.1 = (bf16[2,48,1024]{2,1,0:T(8,128)(2,1)S(1)}, bf16[2,48,1024]{2,1,0:T(8,128)(2,1)S(1)}, f32[2,48,1024]{2,1,0:T(8,128)S(1)}, f32[48,1024]{1,0:T(8,12...) custom-call(s32[8]{0:T(128)S(1)} %stack.35.at_ref, f32[8,1,2048]{2,1,0:T(1,128)S(1)} %all-to-all-done.1.stat_in, ...), custom_call_target="tpu_custom_call" | custom-call | tf_op jit(solution)/shard_map/image_part/pallas_call | solution.py:305
  45.6 0.3 collective-permute-start.5
  45.9 2.1 %collective-permute-start.7 = (bf16[2,48,1024]{2,1,0:T(8,128)(2,1)S(1)}, bf16[2,48,1024]{2,1,0:T(8,128)(2,1)S(1)}, u32[]{:S(2)}, u32[]{:S(2)}) collective-permute-start(bf16[2,48,1024]{2,1,0:T(8,128)(2,1)S(1)} %get-tuple-element.35), channel_id=1, source_target_pairs={{0,4},{1,9},{4,0},{5,13},{8,12},{9,1},{12,8},{13,5},{16,20},{17,25... | collective-permute-start | bytes 589832 | tf_op jit(solution)/shard_map/ppermute | solution.py:34
  48.1 5.1 %text_part.1 = bf16[8,48,1024]{2,1,0:T(8,128)(2,1)} custom-call(s32[8]{0:T(128)S(1)} %stack.35.at_ref, f32[384,1536]{1,0:T(8,128)S(1)} %copy-done.1, f32[8,1,2048]{2,1,0:T(1,128)S(1)} %all-to-all-done.1.stat_in, s32[1,1536]{1,0:T(1,128)S(1)} %broadcast_in_dim.3.match_in, bf16[1536,1024]{1,0:T(8,128)(2,1)} %image_in.3, f32[1,128]{1,0:T(1,128)S(1)} %get-tuple-element.42.after_ref), custom_call_target="tpu_custom_call" | custom-call | tf_op jit(solution)/shard_map/text_part/pallas_call | solution.py:204
  53.1 0.1 collective-permute-done.5
  53.3 0.1 add_convert_fusion
  53.3 0.9 %collective-permute-start.9 = (f32[1,128]{1,0:T(1,128)S(1)}, f32[1,128]{1,0:T(1,128)S(1)}, u32[]{:S(2)}, u32[]{:S(2)}) collective-permute-start(f32[1,128]{1,0:T(1,128)S(1)} %get-tuple-element.42.after_ref), channel_id=1, source_target_pairs={{0,1},{1,0},{2,3},{3,2},{4,5},{5,4},{6,7},{7,6},{8,9},{9,8},{10,11... | collective-permute-start | bytes 1544 | tf_op jit(solution)/shard_map/ppermute | solution.py:29
  54.2 0.8 %collective-permute-done.9 = f32[1,128]{1,0:T(1,128)S(1)} collective-permute-done((f32[1,128]{1,0:T(1,128)S(1)}, f32[1,128]{1,0:T(1,128)S(1)}, u32[]{:S(2)}, u32[]{:S(2)}) %collective-permute-start.9) | collective-permute-done | bytes 544 | tf_op jit(solution)/shard_map/ppermute | solution.py:29
  55.0 3.5 %all-to-all-start.2 = ((bf16[8,48,1024]{2,1,0:T(8,128)(2,1)}), bf16[8,48,1024]{2,1,0:T(8,128)(2,1)S(1)}, u32[]{:S(2)}, u32[]{:S(2)}) async-start(bf16[8,48,1024]{2,1,0:T(8,128)(2,1)} %text_part.1), calls=%async_computation.2 | async-start | bytes 1572864 | tf_op jit(solution)/shard_map/all_to_all | solution.py:38
  58.6 0.1 convert_add_fusion.2
  58.6 2.4 %collective-permute-done.6 = f16[2,48,1024]{2,1,0:T(8,128)(2,1)S(1)} collective-permute-done((f16[2,48,1024]{2,1,0:T(8,128)(2,1)S(1)}, f16[2,48,1024]{2,1,0:T(8,128)(2,1)S(1)}, u32[]{:S(2)}, u32[]{:S(2)}) %collective-permute-start.6) | collective-permute-done | bytes 196640 | tf_op jit(solution)/shard_map/ppermute | solution.py:34
  61.1 0.8 %collective-permute-start.8 = (f16[48,1024]{1,0:T(8,128)(2,1)S(1)}, f16[48,1024]{1,0:T(8,128)(2,1)S(1)}, u32[]{:S(2)}, u32[]{:S(2)}) collective-permute-start(f16[48,1024]{1,0:T(8,128)(2,1)S(1)} %get-tuple-element.47), channel_id=1, source_target_pairs={{0,28},{1,29},{4,24},{5,25},{8,20},{9,21},{12,16},{13,17},{16,12},... | collective-permute-start | bytes 294920 | tf_op jit(solution)/shard_map/ppermute | solution.py:34
  61.9 6.4 %collective-permute-done.8 = f16[48,1024]{1,0:T(8,128)(2,1)S(1)} collective-permute-done((f16[48,1024]{1,0:T(8,128)(2,1)S(1)}, f16[48,1024]{1,0:T(8,128)(2,1)S(1)}, u32[]{:S(2)}, u32[]{:S(2)}) %collective-permute-start.8) | collective-permute-done | bytes 98336 | tf_op jit(solution)/shard_map/ppermute | solution.py:34
  68.3 0.7 %add_multiply_fusion = f32[48,1024]{1,0:T(8,128)} fusion(f32[48,1024]{1,0:T(8,128)S(1)} %get-tuple-element.40, f16[48,1024]{1,0:T(8,128)(2,1)S(1)} %collective-permute-done.8, f32[]{:T(128)S(1)} %bitcast.28), kind=kLoop, calls=%fused_computation.7 | loop fusion | flops 147456 | bytes 491524 | tf_op jit(solution)/shard_map/mul | solution.py:369
  69.0 2.6 %all-to-all-done.2 = bf16[8,48,1024]{2,1,0:T(8,128)(2,1)S(1)} async-done(((bf16[8,48,1024]{2,1,0:T(8,128)(2,1)}), bf16[8,48,1024]{2,1,0:T(8,128)(2,1)S(1)}, u32[]{:S(2)}, u32[]{:S(2)}) %all-to-all-start.2) | async-done | bytes 786464 | tf_op jit(solution)/shard_map/all_to_all | solution.py:38
  71.6 0.8 %convert_reduce_fusion = f32[48,1024]{1,0:T(8,128)} fusion(bf16[8,48,1024]{2,1,0:T(8,128)(2,1)S(1)} %all-to-all-done.2), kind=kLoop, calls=%fused_computation | loop fusion | flops 737280 | bytes 983040 | tf_op jit(solution)/shard_map/reduce_sum | solution.py:367
  (13 shorter events, 0.1 us)
Async XLA Ops:
  0.6 27.1 %copy-start = (bf16[384,1024]{1,0:T(8,128)(2,1)S(1)}, bf16[384,1024]{1,0:T(8,128)(2,1)}, u32[]{:S(2)}) copy-start(bf16[384,1024]{1,0:T(8,128)(2,1)} %t0.1) | copy-start | bytes 2359300
  0.6 32.5 %copy-start.2 = (s32[1536]{0:T(1024)S(1)}, s32[1536]{0:T(1024)}, u32[]{:S(2)}) copy-start(s32[1536]{0:T(1024)} %param.5) | copy-start | bytes 18436
  0.6 24.4 %collective-permute-start = (bf16[384,1024]{1,0:T(8,128)(2,1)}, bf16[384,1024]{1,0:T(8,128)(2,1)S(1)}, u32[]{:S(2)}, u32[]{:S(2)}) collective-permute-start(bf16[384,1024]{1,0:T(8,128)(2,1)} %t0.1), channel_id=1, source_target_pairs={{0,2},{2,0},{1,3},{3,1},{4,6},{6,4},{5,7},{7,5},{8,10},{10,8},{9,1... | collective-permute-start | bytes 2359304 | tf_op jit(solution)/shard_map/ppermute | solution.py:29
  9.5 9.8 %collective-permute-start.1 = (f32[1,1664]{1,0:T(1,128)}, f32[1,1664]{1,0:T(1,128)S(1)}, u32[]{:S(2)}, u32[]{:S(2)}) collective-permute-start(f32[1,1664]{1,0:T(1,128)} %get-tuple-element.25), channel_id=1, source_target_pairs={{0,28},{1,29},{4,24},{5,25},{8,20},{9,21},{12,16},{13,17},{16,12},... | collective-permute-start | bytes 19976 | tf_op jit(solution)/shard_map/ppermute | solution.py:34
  15.2 9.2 %all-to-all-start = ((f32[8,1,384]{2,1,0:T(1,128)}), f32[8,1,384]{2,1,0:T(1,128)S(1)}, u32[]{:S(2)}, u32[]{:S(2)}) async-start(f32[8,1,384]{2,1,0:T(1,128)} %get-tuple-element.24), calls=%async_computation | async-start | bytes 24576 | tf_op jit(solution)/shard_map/all_to_all | solution.py:38
  20.1 4.3 %collective-permute-start.2 = (f32[1,1664]{1,0:T(1,128)S(1)}, f32[1,1664]{1,0:T(1,128)S(1)}, u32[]{:S(2)}, u32[]{:S(2)}) collective-permute-start(f32[1,1664]{1,0:T(1,128)S(1)} %compare_select_fusion.row_ref), channel_id=1, source_target_pairs={{0,4},{1,5},{4,0},{5,1},{8,12},{9,13},{12,8},{13,9},{16,20},{17,21... | collective-permute-start | bytes 19976 | tf_op jit(solution)/shard_map/ppermute | solution.py:34
  25.1 8.2 %collective-permute-start.4 = (bf16[384,1024]{1,0:T(8,128)(2,1)S(1)}, bf16[384,1024]{1,0:T(8,128)(2,1)}, u32[]{:S(2)}, u32[]{:S(2)}) collective-permute-start(bf16[384,1024]{1,0:T(8,128)(2,1)S(1)} %collective-permute-done.t2), channel_id=1, source_target_pairs={{0,1},{1,0},{2,3},{3,2},{4,5},{5,4},{6,7},{7,6},{8,9},{9,8},{10,11... | collective-permute-start | bytes 2359304 | tf_op jit(solution)/shard_map/ppermute | solution.py:29
  27.7 7.6 %collective-permute-start.3 = (bf16[384,1024]{1,0:T(8,128)(2,1)S(1)}, bf16[384,1024]{1,0:T(8,128)(2,1)S(1)}, u32[]{:S(2)}, u32[]{:S(2)}) collective-permute-start(bf16[384,1024]{1,0:T(8,128)(2,1)S(1)} %copy-done), channel_id=1, source_target_pairs={{0,1},{1,0},{2,3},{3,2},{4,5},{5,4},{6,7},{7,6},{8,9},{9,8},{10,11... | collective-permute-start | bytes 2359304 | tf_op jit(solution)/shard_map/ppermute | solution.py:29
  27.8 12.2 %all-to-all-start.1 = ((f32[8,1,2048]{2,1,0:T(1,128)}), f32[8,1,2048]{2,1,0:T(1,128)S(1)}, u32[]{:S(2)}, u32[]{:S(2)}) async-start(f32[8,1,2048]{2,1,0:T(1,128)} %merge.1), calls=%async_computation.1 | async-start | bytes 131072 | tf_op jit(solution)/shard_map/all_to_all | solution.py:38
  40.0 8.0 %copy-start.1 = (f32[384,1536]{1,0:T(8,128)S(1)}, f32[384,1536]{1,0:T(8,128)}, u32[]{:S(2)}) copy-start(f32[384,1536]{1,0:T(8,128)} %get-tuple-element.30.logits_in) | copy-start | bytes 7077892
  45.6 7.7 %collective-permute-start.5 = (bf16[2,48,1024]{2,1,0:T(8,128)(2,1)S(1)}, bf16[2,48,1024]{2,1,0:T(8,128)(2,1)S(1)}, u32[]{:S(2)}, u32[]{:S(2)}) collective-permute-start(bf16[2,48,1024]{2,1,0:T(8,128)(2,1)S(1)} %get-tuple-element.29), channel_id=1, source_target_pairs={{0,4},{1,9},{4,0},{5,13},{8,12},{9,1},{12,8},{13,5},{16,20},{17,25... | collective-permute-start | bytes 589832 | tf_op jit(solution)/shard_map/ppermute | solution.py:34
  45.9 12.7 %collective-permute-start.7 = (bf16[2,48,1024]{2,1,0:T(8,128)(2,1)S(1)}, bf16[2,48,1024]{2,1,0:T(8,128)(2,1)S(1)}, u32[]{:S(2)}, u32[]{:S(2)}) collective-permute-start(bf16[2,48,1024]{2,1,0:T(8,128)(2,1)S(1)} %get-tuple-element.35), channel_id=1, source_target_pairs={{0,4},{1,9},{4,0},{5,13},{8,12},{9,1},{12,8},{13,5},{16,20},{17,25... | collective-permute-start | bytes 589832 | tf_op jit(solution)/shard_map/ppermute | solution.py:34
  53.3 1.7 %collective-permute-start.9 = (f32[1,128]{1,0:T(1,128)S(1)}, f32[1,128]{1,0:T(1,128)S(1)}, u32[]{:S(2)}, u32[]{:S(2)}) collective-permute-start(f32[1,128]{1,0:T(1,128)S(1)} %get-tuple-element.42.after_ref), channel_id=1, source_target_pairs={{0,1},{1,0},{2,3},{3,2},{4,5},{5,4},{6,7},{7,6},{8,9},{9,8},{10,11... | collective-permute-start | bytes 1544 | tf_op jit(solution)/shard_map/ppermute | solution.py:29
  54.2 6.9 %collective-permute-start.6 = (f16[2,48,1024]{2,1,0:T(8,128)(2,1)S(1)}, f16[2,48,1024]{2,1,0:T(8,128)(2,1)S(1)}, u32[]{:S(2)}, u32[]{:S(2)}) collective-permute-start(f16[2,48,1024]{2,1,0:T(8,128)(2,1)S(1)} %add_convert_fusion), channel_id=1, source_target_pairs={{0,8},{1,5},{4,12},{5,1},{8,0},{9,13},{12,4},{13,9},{16,24},{17,21... | collective-permute-start | bytes 589832 | tf_op jit(solution)/shard_map/ppermute | solution.py:34
  55.0 16.6 %all-to-all-start.2 = ((bf16[8,48,1024]{2,1,0:T(8,128)(2,1)}), bf16[8,48,1024]{2,1,0:T(8,128)(2,1)S(1)}, u32[]{:S(2)}, u32[]{:S(2)}) async-start(bf16[8,48,1024]{2,1,0:T(8,128)(2,1)} %text_part.1), calls=%async_computation.2 | async-start | bytes 1572864 | tf_op jit(solution)/shard_map/all_to_all | solution.py:38
  61.1 7.2 %collective-permute-start.8 = (f16[48,1024]{1,0:T(8,128)(2,1)S(1)}, f16[48,1024]{1,0:T(8,128)(2,1)S(1)}, u32[]{:S(2)}, u32[]{:S(2)}) collective-permute-start(f16[48,1024]{1,0:T(8,128)(2,1)S(1)} %get-tuple-element.47), channel_id=1, source_target_pairs={{0,28},{1,29},{4,24},{5,25},{8,20},{9,21},{12,16},{13,17},{16,12},... | collective-permute-start | bytes 294920 | tf_op jit(solution)/shard_map/ppermute | solution.py:34

commit v8 on v7

--- a/solution.py
+++ b/solution.py
@@ -220,24 +220,6 @@
     )(at, logits, stats, match, images, after)
 
 
-def settle_kernel(in_ref, out_ref, sem):
-    copy = pltpu.make_async_copy(in_ref, out_ref, sem)
-    copy.start()
-    copy.wait()
-
-
-def settle(value):
-    return pl.pallas_call(
-        settle_kernel,
-        in_specs=[VMEM],
-        out_specs=HBM,
-        out_shape=jax.ShapeDtypeStruct(value.shape, value.dtype),
-        scratch_shapes=[pltpu.SemaphoreType.DMA],
-        cost_estimate=FREE,
-        name="settle",
-    )(value)
-
-
 def image_kernel(scale, at_ref, stat_in, match_in, image_ref, t0, t1, t2, t3, e_ref, a_ref, b_ref, c_ref, d_ref, down_ref, stat_ref, match_ref, own, four, row_by, match_by, weights, sems):
     texts = (t0, t1, t2, t3)
     blocks, _, per, width = image_ref.shape
@@ -342,7 +324,7 @@
     sent = merge_call(got, row, near)
     other_yhi, sent = tie(other_yhi, sent)
     stats = exchange(sent, ("zb", "yhi", "core"))
-    other_both = settle(swap(other_yhi, "core"))
+    other_both = swap(other_yhi, "core")
 
     bases = [(z * 4 + (place ^ k)) * cols for k in range(4)]
     at = jnp.stack([place, *bases, z, core, zb * 4])

time: 72.8 us -> 72.2 us (level)
  Pallas kernels: 18.3 us -> 16.3 us
  starting transfers between devices: 31.1 us -> 32.4 us
    pallas_call x1 -> x0, Pallas kernels: 2.05 us -> none  [settle(): pl.pallas_call(settle_kernel, in_specs=[VMEM], out_specs=HBM, out_shape=j...]
    ppermute x4, starting transfers between devices: 7.48 us -> 9.04 us  [swap(): return lax.ppermute(value, axis, [(0, 1), (1, 0)])]
  transfers between devices with their start and end apart: 13 -> 13, of which waited for: 7 -> 7; matrix products, arithmetic and copies ran while one was open for 2% -> 2% of each run, Pallas kernels for 18% -> 15%
where the time goes in v8:
time: 72.2 us; the launch traced here: 71.8 us
  starting transfers between devices  32.4 us (45%)
  waiting for transfers between devices  19.9 us (28%)
  Pallas kernels  16.3 us (23%)
  other arithmetic  2.42 us (3%)
    all_to_all x3, starting transfers between devices, exchange(): return lax.all_to_all(copies, axes, 0, 0, tiled=True)  12.7 us
    ppermute x6, starting transfers between devices, z_swap(): return lax.ppermute(value, ('zhi', 'zb', 'za', 'core'), pairs)  10.7 us
    all_to_all x3, waiting for transfers between devices, exchange(): return lax.all_to_all(copies, axes, 0, 0, tiled=True)  9.69 us
    ppermute x6, waiting for transfers between devices, z_swap(): return lax.ppermute(value, ('zhi', 'zb', 'za', 'core'), pairs)  9.34 us
    ppermute x4, starting transfers between devices, swap(): return lax.ppermute(value, axis, [(0, 1), (1, 0)])  9.04 us
    pallas_call x1, Pallas kernels, image_call(): pl.pallas_call(functools.partial(image_kernel, scale), in_specs=[SCALARS,...  5.55 us
    pallas_call x1, Pallas kernels, text_call(): pl.pallas_call(text_kernel, in_specs=[SCALARS, HBM, ANY, ANY, HBM, ANY],...  5.06 us
    pallas_call x1, Pallas kernels, first_call(): pl.pallas_call(functools.partial(first_kernel, scale), in_specs=[HBM] * 2...  5.04 us
  transfers between devices with their start and end apart: 13, of which 7 were waited for; matrix products, arithmetic and copies ran while one was open for 2% of the time, Pallas kernels for 15%

profile of v8, /device:TPU:1, one launch (start us, length us, event | category | flops | bytes accessed | tf_op | source)
XLA Modules:
  0.0 71.8 jit_solution(9660237018248241140)
XLA Ops:
  0.6 3.8 %collective-permute-start = (bf16[384,1024]{1,0:T(8,128)(2,1)}, bf16[384,1024]{1,0:T(8,128)(2,1)S(1)}, u32[]{:S(2)}, u32[]{:S(2)}) collective-permute-start(bf16[384,1024]{1,0:T(8,128)(2,1)} %t0.1), channel_id=1, source_target_pairs={{0,2},{2,0},{1,3},{3,1},{4,6},{6,4},{5,7},{7,5},{8,10},{10,8},{9,1... | collective-permute-start | bytes 2359304 | tf_op jit(solution)/shard_map/ppermute | solution.py:29
  4.5 5.0 %logits.1 = (f32[384,1536]{1,0:T(8,128)}, f32[1,1664]{1,0:T(1,128)}, f32[8,1,384]{2,1,0:T(1,128)}) custom-call(bf16[384,1024]{1,0:T(8,128)(2,1)} %t0.1, bf16[1536,1024]{1,0:T(8,128)(2,1)} %image_in.3), custom_call_target="tpu_custom_call" | custom-call | tf_op jit(solution)/shard_map/logits/pallas_call | solution.py:122
  9.5 5.7 %collective-permute-start.1 = (f32[1,1664]{1,0:T(1,128)}, f32[1,1664]{1,0:T(1,128)S(1)}, u32[]{:S(2)}, u32[]{:S(2)}) collective-permute-start(f32[1,1664]{1,0:T(1,128)} %get-tuple-element.25), channel_id=1, source_target_pairs={{0,28},{1,29},{4,24},{5,25},{8,20},{9,21},{12,16},{13,17},{16,12},... | collective-permute-start | bytes 19976 | tf_op jit(solution)/shard_map/ppermute | solution.py:34
  15.2 4.1 %all-to-all-start = ((f32[8,1,384]{2,1,0:T(1,128)}), f32[8,1,384]{2,1,0:T(1,128)S(1)}, u32[]{:S(2)}, u32[]{:S(2)}) async-start(f32[8,1,384]{2,1,0:T(1,128)} %get-tuple-element.24), calls=%async_computation | async-start | bytes 24576 | tf_op jit(solution)/shard_map/all_to_all | solution.py:38
  19.3 0.0 collective-permute-done.1
  19.3 0.7 %compare_select_fusion.row_ref = f32[1,1664]{1,0:T(1,128)S(1)} fusion(f32[1,1664]{1,0:T(1,128)S(1)} %collective-permute-done.1, f32[1,1664]{1,0:T(1,128)} %get-tuple-element.25), kind=kLoop, calls=%fused_computation.10 | loop fusion | flops 16640 | bytes 19968 | tf_op jit(solution)/shard_map/jit(_where)/select_n | solution.py:54
  20.1 1.7 %collective-permute-start.2 = (f32[1,1664]{1,0:T(1,128)S(1)}, f32[1,1664]{1,0:T(1,128)S(1)}, u32[]{:S(2)}, u32[]{:S(2)}) collective-permute-start(f32[1,1664]{1,0:T(1,128)S(1)} %compare_select_fusion.row_ref), channel_id=1, source_target_pairs={{0,4},{1,5},{4,0},{5,1},{8,12},{9,13},{12,8},{13,9},{16,20},{17,21... | collective-permute-start | bytes 19976 | tf_op jit(solution)/shard_map/ppermute | solution.py:34
  21.8 1.8 %collective-permute-start.3 = (bf16[384,1024]{1,0:T(8,128)(2,1)S(1)}, bf16[384,1024]{1,0:T(8,128)(2,1)S(1)}, u32[]{:S(2)}, u32[]{:S(2)}) collective-permute-start(bf16[384,1024]{1,0:T(8,128)(2,1)S(1)} %copy-done), channel_id=1, source_target_pairs={{0,1},{1,0},{2,3},{3,2},{4,5},{5,4},{6,7},{7,6},{8,9},{9,8},{10,11... | collective-permute-start | bytes 2359304 | tf_op jit(solution)/shard_map/ppermute | solution.py:29
  23.6 0.8 %all-to-all-done.got_ref = f32[8,1,384]{2,1,0:T(1,128)S(1)} async-done(((f32[8,1,384]{2,1,0:T(1,128)}), f32[8,1,384]{2,1,0:T(1,128)S(1)}, u32[]{:S(2)}, u32[]{:S(2)}) %all-to-all-start) | async-done | bytes 12320 | tf_op jit(solution)/shard_map/all_to_all | solution.py:38
  24.4 0.0 collective-permute-done.2.near_ref
  24.4 0.7 merge.1
  25.1 2.7 %collective-permute-start.4 = (bf16[384,1024]{1,0:T(8,128)(2,1)S(1)}, bf16[384,1024]{1,0:T(8,128)(2,1)}, u32[]{:S(2)}, u32[]{:S(2)}) collective-permute-start(bf16[384,1024]{1,0:T(8,128)(2,1)S(1)} %collective-permute-done.t2), channel_id=1, source_target_pairs={{0,1},{1,0},{2,3},{3,2},{4,5},{5,4},{6,7},{7,6},{8,9},{9,8},{10,11... | collective-permute-start | bytes 2359304 | tf_op jit(solution)/shard_map/ppermute | solution.py:29
  27.7 5.0 %all-to-all-start.1 = ((f32[8,1,2048]{2,1,0:T(1,128)}), f32[8,1,2048]{2,1,0:T(1,128)S(1)}, u32[]{:S(2)}, u32[]{:S(2)}) async-start(f32[8,1,2048]{2,1,0:T(1,128)} %merge.1), calls=%async_computation.1 | async-start | bytes 131072 | tf_op jit(solution)/shard_map/all_to_all | solution.py:38
  32.7 0.1 stack.35.at_ref
  32.8 6.5 %all-to-all-done.1.stat_in = f32[8,1,2048]{2,1,0:T(1,128)S(1)} async-done(((f32[8,1,2048]{2,1,0:T(1,128)}), f32[8,1,2048]{2,1,0:T(1,128)S(1)}, u32[]{:S(2)}, u32[]{:S(2)}) %all-to-all-start.1) | async-done | bytes 65568 | tf_op jit(solution)/shard_map/all_to_all | solution.py:38
  39.4 0.0 collective-permute-done.4.t3
  39.4 5.5 %image_part.1 = (bf16[2,48,1024]{2,1,0:T(8,128)(2,1)S(1)}, bf16[2,48,1024]{2,1,0:T(8,128)(2,1)S(1)}, f32[2,48,1024]{2,1,0:T(8,128)S(1)}, f32[48,1024]{1,0:T(8,12...) custom-call(s32[8]{0:T(128)S(1)} %stack.35.at_ref, f32[8,1,2048]{2,1,0:T(1,128)S(1)} %all-to-all-done.1.stat_in, ...), custom_call_target="tpu_custom_call" | custom-call | tf_op jit(solution)/shard_map/image_part/pallas_call | solution.py:287
  44.9 0.6 collective-permute-start.5
  45.5 1.9 %collective-permute-start.7 = (bf16[2,48,1024]{2,1,0:T(8,128)(2,1)S(1)}, bf16[2,48,1024]{2,1,0:T(8,128)(2,1)S(1)}, u32[]{:S(2)}, u32[]{:S(2)}) collective-permute-start(bf16[2,48,1024]{2,1,0:T(8,128)(2,1)S(1)} %get-tuple-element.35), channel_id=1, source_target_pairs={{0,4},{1,9},{4,0},{5,13},{8,12},{9,1},{12,8},{13,5},{16,20},{17,25... | collective-permute-start | bytes 589832 | tf_op jit(solution)/shard_map/ppermute | solution.py:34
  47.4 5.1 %text_part.1 = bf16[8,48,1024]{2,1,0:T(8,128)(2,1)} custom-call(s32[8]{0:T(128)S(1)} %stack.35.at_ref, f32[384,1536]{1,0:T(8,128)S(1)} %copy-done.1, f32[8,1,2048]{2,1,0:T(1,128)S(1)} %all-to-all-done.1.stat_in, s32[1,1536]{1,0:T(1,128)S(1)} %broadcast_in_dim.3.match_in, bf16[1536,1024]{1,0:T(8,128)(2,1)} %image_in.3, f32[1,128]{1,0:T(1,128)S(1)} %get-tuple-element.42.after_ref), custom_call_target="tpu_custom_call" | custom-call | tf_op jit(solution)/shard_map/text_part/pallas_call | solution.py:204
  52.5 0.4 collective-permute-done.5
  52.9 0.1 add_convert_fusion
  52.9 0.7 %collective-permute-start.9 = (f32[1,128]{1,0:T(1,128)S(1)}, f32[1,128]{1,0:T(1,128)S(1)}, u32[]{:S(2)}, u32[]{:S(2)}) collective-permute-start(f32[1,128]{1,0:T(1,128)S(1)} %get-tuple-element.42.after_ref), channel_id=1, source_target_pairs={{0,1},{1,0},{2,3},{3,2},{4,5},{5,4},{6,7},{7,6},{8,9},{9,8},{10,11... | collective-permute-start | bytes 1544 | tf_op jit(solution)/shard_map/ppermute | solution.py:29
  53.7 0.8 %collective-permute-done.9 = f32[1,128]{1,0:T(1,128)S(1)} collective-permute-done((f32[1,128]{1,0:T(1,128)S(1)}, f32[1,128]{1,0:T(1,128)S(1)}, u32[]{:S(2)}, u32[]{:S(2)}) %collective-permute-start.9) | collective-permute-done | bytes 544 | tf_op jit(solution)/shard_map/ppermute | solution.py:29
  54.5 3.5 %all-to-all-start.2 = ((bf16[8,48,1024]{2,1,0:T(8,128)(2,1)}), bf16[8,48,1024]{2,1,0:T(8,128)(2,1)S(1)}, u32[]{:S(2)}, u32[]{:S(2)}) async-start(bf16[8,48,1024]{2,1,0:T(8,128)(2,1)} %text_part.1), calls=%async_computation.2 | async-start | bytes 1572864 | tf_op jit(solution)/shard_map/all_to_all | solution.py:38
  58.0 0.1 convert_add_fusion.2
  58.1 2.6 %collective-permute-done.6 = f16[2,48,1024]{2,1,0:T(8,128)(2,1)S(1)} collective-permute-done((f16[2,48,1024]{2,1,0:T(8,128)(2,1)S(1)}, f16[2,48,1024]{2,1,0:T(8,128)(2,1)S(1)}, u32[]{:S(2)}, u32[]{:S(2)}) %collective-permute-start.6) | collective-permute-done | bytes 196640 | tf_op jit(solution)/shard_map/ppermute | solution.py:34
  60.7 0.8 %collective-permute-start.8 = (f16[48,1024]{1,0:T(8,128)(2,1)S(1)}, f16[48,1024]{1,0:T(8,128)(2,1)S(1)}, u32[]{:S(2)}, u32[]{:S(2)}) collective-permute-start(f16[48,1024]{1,0:T(8,128)(2,1)S(1)} %get-tuple-element.47), channel_id=1, source_target_pairs={{0,28},{1,29},{4,24},{5,25},{8,20},{9,21},{12,16},{13,17},{16,12},... | collective-permute-start | bytes 294920 | tf_op jit(solution)/shard_map/ppermute | solution.py:34
  61.6 6.4 %collective-permute-done.8 = f16[48,1024]{1,0:T(8,128)(2,1)S(1)} collective-permute-done((f16[48,1024]{1,0:T(8,128)(2,1)S(1)}, f16[48,1024]{1,0:T(8,128)(2,1)S(1)}, u32[]{:S(2)}, u32[]{:S(2)}) %collective-permute-start.8) | collective-permute-done | bytes 98336 | tf_op jit(solution)/shard_map/ppermute | solution.py:34
  67.9 0.7 %add_multiply_fusion = f32[48,1024]{1,0:T(8,128)} fusion(f32[48,1024]{1,0:T(8,128)S(1)} %get-tuple-element.40, f16[48,1024]{1,0:T(8,128)(2,1)S(1)} %collective-permute-done.8, f32[]{:T(128)S(1)} %bitcast.28), kind=kLoop, calls=%fused_computation.7 | loop fusion | flops 147456 | bytes 491524 | tf_op jit(solution)/shard_map/mul | solution.py:351
  68.7 2.4 %all-to-all-done.2 = bf16[8,48,1024]{2,1,0:T(8,128)(2,1)S(1)} async-done(((bf16[8,48,1024]{2,1,0:T(8,128)(2,1)}), bf16[8,48,1024]{2,1,0:T(8,128)(2,1)S(1)}, u32[]{:S(2)}, u32[]{:S(2)}) %all-to-all-start.2) | async-done | bytes 786464 | tf_op jit(solution)/shard_map/all_to_all | solution.py:38
  71.0 0.8 %convert_reduce_fusion = f32[48,1024]{1,0:T(8,128)} fusion(bf16[8,48,1024]{2,1,0:T(8,128)(2,1)S(1)} %all-to-all-done.2), kind=kLoop, calls=%fused_computation | loop fusion | flops 737280 | bytes 983040 | tf_op jit(solution)/shard_map/reduce_sum | solution.py:349
  (12 shorter events, 0.1 us)
Async XLA Ops:
  0.6 21.2 %copy-start = (bf16[384,1024]{1,0:T(8,128)(2,1)S(1)}, bf16[384,1024]{1,0:T(8,128)(2,1)}, u32[]{:S(2)}) copy-start(bf16[384,1024]{1,0:T(8,128)(2,1)} %t0.1) | copy-start | bytes 2359300
  0.6 32.1 %copy-start.2 = (s32[1536]{0:T(1024)S(1)}, s32[1536]{0:T(1024)}, u32[]{:S(2)}) copy-start(s32[1536]{0:T(1024)} %param.5) | copy-start | bytes 18436
  0.6 24.4 %collective-permute-start = (bf16[384,1024]{1,0:T(8,128)(2,1)}, bf16[384,1024]{1,0:T(8,128)(2,1)S(1)}, u32[]{:S(2)}, u32[]{:S(2)}) collective-permute-start(bf16[384,1024]{1,0:T(8,128)(2,1)} %t0.1), channel_id=1, source_target_pairs={{0,2},{2,0},{1,3},{3,1},{4,6},{6,4},{5,7},{7,5},{8,10},{10,8},{9,1... | collective-permute-start | bytes 2359304 | tf_op jit(solution)/shard_map/ppermute | solution.py:29
  9.5 9.8 %collective-permute-start.1 = (f32[1,1664]{1,0:T(1,128)}, f32[1,1664]{1,0:T(1,128)S(1)}, u32[]{:S(2)}, u32[]{:S(2)}) collective-permute-start(f32[1,1664]{1,0:T(1,128)} %get-tuple-element.25), channel_id=1, source_target_pairs={{0,28},{1,29},{4,24},{5,25},{8,20},{9,21},{12,16},{13,17},{16,12},... | collective-permute-start | bytes 19976 | tf_op jit(solution)/shard_map/ppermute | solution.py:34
  15.2 9.2 %all-to-all-start = ((f32[8,1,384]{2,1,0:T(1,128)}), f32[8,1,384]{2,1,0:T(1,128)S(1)}, u32[]{:S(2)}, u32[]{:S(2)}) async-start(f32[8,1,384]{2,1,0:T(1,128)} %get-tuple-element.24), calls=%async_computation | async-start | bytes 24576 | tf_op jit(solution)/shard_map/all_to_all | solution.py:38
  20.1 4.3 %collective-permute-start.2 = (f32[1,1664]{1,0:T(1,128)S(1)}, f32[1,1664]{1,0:T(1,128)S(1)}, u32[]{:S(2)}, u32[]{:S(2)}) collective-permute-start(f32[1,1664]{1,0:T(1,128)S(1)} %compare_select_fusion.row_ref), channel_id=1, source_target_pairs={{0,4},{1,5},{4,0},{5,1},{8,12},{9,13},{12,8},{13,9},{16,20},{17,21... | collective-permute-start | bytes 19976 | tf_op jit(solution)/shard_map/ppermute | solution.py:34
  21.8 11.0 %collective-permute-start.3 = (bf16[384,1024]{1,0:T(8,128)(2,1)S(1)}, bf16[384,1024]{1,0:T(8,128)(2,1)S(1)}, u32[]{:S(2)}, u32[]{:S(2)}) collective-permute-start(bf16[384,1024]{1,0:T(8,128)(2,1)S(1)} %copy-done), channel_id=1, source_target_pairs={{0,1},{1,0},{2,3},{3,2},{4,5},{5,4},{6,7},{7,6},{8,9},{9,8},{10,11... | collective-permute-start | bytes 2359304 | tf_op jit(solution)/shard_map/ppermute | solution.py:29
  25.1 14.3 %collective-permute-start.4 = (bf16[384,1024]{1,0:T(8,128)(2,1)S(1)}, bf16[384,1024]{1,0:T(8,128)(2,1)}, u32[]{:S(2)}, u32[]{:S(2)}) collective-permute-start(bf16[384,1024]{1,0:T(8,128)(2,1)S(1)} %collective-permute-done.t2), channel_id=1, source_target_pairs={{0,1},{1,0},{2,3},{3,2},{4,5},{5,4},{6,7},{7,6},{8,9},{9,8},{10,11... | collective-permute-start | bytes 2359304 | tf_op jit(solution)/shard_map/ppermute | solution.py:29
  27.7 11.6 %all-to-all-start.1 = ((f32[8,1,2048]{2,1,0:T(1,128)}), f32[8,1,2048]{2,1,0:T(1,128)S(1)}, u32[]{:S(2)}, u32[]{:S(2)}) async-start(f32[8,1,2048]{2,1,0:T(1,128)} %merge.1), calls=%async_computation.1 | async-start | bytes 131072 | tf_op jit(solution)/shard_map/all_to_all | solution.py:38
  39.4 8.0 %copy-start.1 = (f32[384,1536]{1,0:T(8,128)S(1)}, f32[384,1536]{1,0:T(8,128)}, u32[]{:S(2)}) copy-start(f32[384,1536]{1,0:T(8,128)} %get-tuple-element.30.logits_in) | copy-start | bytes 7077892
  44.9 7.9 %collective-permute-start.5 = (bf16[2,48,1024]{2,1,0:T(8,128)(2,1)S(1)}, bf16[2,48,1024]{2,1,0:T(8,128)(2,1)S(1)}, u32[]{:S(2)}, u32[]{:S(2)}) collective-permute-start(bf16[2,48,1024]{2,1,0:T(8,128)(2,1)S(1)} %get-tuple-element.29), channel_id=1, source_target_pairs={{0,4},{1,9},{4,0},{5,13},{8,12},{9,1},{12,8},{13,5},{16,20},{17,25... | collective-permute-start | bytes 589832 | tf_op jit(solution)/shard_map/ppermute | solution.py:34
  45.5 12.5 %collective-permute-start.7 = (bf16[2,48,1024]{2,1,0:T(8,128)(2,1)S(1)}, bf16[2,48,1024]{2,1,0:T(8,128)(2,1)S(1)}, u32[]{:S(2)}, u32[]{:S(2)}) collective-permute-start(bf16[2,48,1024]{2,1,0:T(8,128)(2,1)S(1)} %get-tuple-element.35), channel_id=1, source_target_pairs={{0,4},{1,9},{4,0},{5,13},{8,12},{9,1},{12,8},{13,5},{16,20},{17,25... | collective-permute-start | bytes 589832 | tf_op jit(solution)/shard_map/ppermute | solution.py:34
  52.9 1.6 %collective-permute-start.9 = (f32[1,128]{1,0:T(1,128)S(1)}, f32[1,128]{1,0:T(1,128)S(1)}, u32[]{:S(2)}, u32[]{:S(2)}) collective-permute-start(f32[1,128]{1,0:T(1,128)S(1)} %get-tuple-element.42.after_ref), channel_id=1, source_target_pairs={{0,1},{1,0},{2,3},{3,2},{4,5},{5,4},{6,7},{7,6},{8,9},{9,8},{10,11... | collective-permute-start | bytes 1544 | tf_op jit(solution)/shard_map/ppermute | solution.py:29
  53.7 7.0 %collective-permute-start.6 = (f16[2,48,1024]{2,1,0:T(8,128)(2,1)S(1)}, f16[2,48,1024]{2,1,0:T(8,128)(2,1)S(1)}, u32[]{:S(2)}, u32[]{:S(2)}) collective-permute-start(f16[2,48,1024]{2,1,0:T(8,128)(2,1)S(1)} %add_convert_fusion), channel_id=1, source_target_pairs={{0,8},{1,5},{4,12},{5,1},{8,0},{9,13},{12,4},{13,9},{16,24},{17,21... | collective-permute-start | bytes 589832 | tf_op jit(solution)/shard_map/ppermute | solution.py:34
  54.5 16.6 %all-to-all-start.2 = ((bf16[8,48,1024]{2,1,0:T(8,128)(2,1)}), bf16[8,48,1024]{2,1,0:T(8,128)(2,1)S(1)}, u32[]{:S(2)}, u32[]{:S(2)}) async-start(bf16[8,48,1024]{2,1,0:T(8,128)(2,1)} %text_part.1), calls=%async_computation.2 | async-start | bytes 1572864 | tf_op jit(solution)/shard_map/all_to_all | solution.py:38
  60.7 7.2 %collective-permute-start.8 = (f16[48,1024]{1,0:T(8,128)(2,1)S(1)}, f16[48,1024]{1,0:T(8,128)(2,1)S(1)}, u32[]{:S(2)}, u32[]{:S(2)}) collective-permute-start(f16[48,1024]{1,0:T(8,128)(2,1)S(1)} %get-tuple-element.47), channel_id=1, source_target_pairs={{0,28},{1,29},{4,24},{5,25},{8,20},{9,21},{12,16},{13,17},{16,12},... | collective-permute-start | bytes 294920 | tf_op jit(solution)/shard_map/ppermute | solution.py:34

commit v9 on v8

--- a/solution.py
+++ b/solution.py
@@ -228,7 +228,7 @@
     every = match_in.shape[1]
     place, z, core, first = at_ref[0], at_ref[5], at_ref[6], at_ref[7]
     one, two = 1 + core, 2 - core
-    order = [z ^ 3, z ^ 4, z ^ one, z ^ one ^ 7, z ^ two, z ^ two ^ 7, z ^ 7, z]
+    order = [z ^ 3, z ^ 5, z ^ one, z ^ one ^ 6, z ^ two, z ^ two ^ 6, z ^ 6, z]
     fetch = [
         pltpu.make_async_copy(stat_in, stat_ref, sems.at[5]),
         pltpu.make_async_copy(match_in, match_ref, sems.at[6]),
@@ -317,7 +317,7 @@
     other_core = swap(texts, "core")
 
     logits, row, col = first_call(texts, images, scale)
-    cross = z_swap(row, (7, 7))
+    cross = z_swap(row, (6, 6))
     row = merge(row, cross, rows)
     near = z_swap(row, (1, 1))
     got = exchange(col, IMG)
@@ -344,7 +344,7 @@
     d = d + a[0].astype(F32)
     text_parts = exchange(text_parts, IMG)
     b, c, d = tie(b, c, d)
-    c = z_swap((c + b[1].astype(F32)).astype(F16), (7, 7))
+    c = z_swap((c + b[1].astype(F32)).astype(F16), (6, 6))
     d = d + b[0].astype(F32)
     text_grad = jnp.sum(text_parts.astype(F32), axis=0)
     c, d = tie(c, d)

time: 72.2 us -> 71.8 us (level)
    all_to_all x3, waiting for transfers between devices: 9.69 us -> 11.7 us  [exchange(): return lax.all_to_all(copies, axes, 0, 0, tiled=True)]
    ppermute x6, waiting for transfers between devices: 9.34 us -> 7.41 us  [z_swap(): return lax.ppermute(value, ('zhi', 'zb', 'za', 'core'), pairs)]
    all_to_all x3, starting transfers between devices: 12.7 us -> 11.8 us  [exchange(): return lax.all_to_all(copies, axes, 0, 0, tiled=True)]
  transfers between devices with their start and end apart: 13 -> 13, of which waited for: 7 -> 6; matrix products, arithmetic and copies ran while one was open for 2% -> 2% of each run, Pallas kernels for 15% -> 15%
where the time goes in v9:
time: 71.8 us; the launch traced here: 71.4 us
  starting transfers between devices  32.6 us (45%)
  waiting for transfers between devices  19.3 us (27%)
  Pallas kernels  16.3 us (23%)
  other arithmetic  2.42 us (3%)
  between operations  0.73 us (1%)
    all_to_all x3, starting transfers between devices, exchange(): return lax.all_to_all(copies, axes, 0, 0, tiled=True)  11.8 us
    all_to_all x3, waiting for transfers between devices, exchange(): return lax.all_to_all(copies, axes, 0, 0, tiled=True)  11.7 us
    ppermute x6, starting transfers between devices, z_swap(): return lax.ppermute(value, ('zhi', 'zb', 'za', 'core'), pairs)  11.4 us
    ppermute x4, starting transfers between devices, swap(): return lax.ppermute(value, axis, [(0, 1), (1, 0)])  9.38 us
    ppermute x6, waiting for transfers between devices, z_swap(): return lax.ppermute(value, ('zhi', 'zb', 'za', 'core'), pairs)  7.41 us
    pallas_call x1, Pallas kernels, image_call(): pl.pallas_call(functools.partial(image_kernel, scale), in_specs=[SCALARS,...  5.54 us
    pallas_call x1, Pallas kernels, text_call(): pl.pallas_call(text_kernel, in_specs=[SCALARS, HBM, ANY, ANY, HBM, ANY],...  5.06 us
    pallas_call x1, Pallas kernels, first_call(): pl.pallas_call(functools.partial(first_kernel, scale), in_specs=[HBM] * 2...  5.04 us
  transfers between devices with their start and end apart: 13, of which 6 were waited for; matrix products, arithmetic and copies ran while one was open for 2% of the time, Pallas kernels for 15%

profile of v9, /device:TPU:1, one launch (start us, length us, event | category | flops | bytes accessed | tf_op | source)
XLA Modules:
  0.0 71.4 jit_solution(7692025706445905441)
XLA Ops:
  0.6 3.8 %collective-permute-start = (bf16[384,1024]{1,0:T(8,128)(2,1)}, bf16[384,1024]{1,0:T(8,128)(2,1)S(1)}, u32[]{:S(2)}, u32[]{:S(2)}) collective-permute-start(bf16[384,1024]{1,0:T(8,128)(2,1)} %t0.1), channel_id=1, source_target_pairs={{0,2},{2,0},{1,3},{3,1},{4,6},{6,4},{5,7},{7,5},{8,10},{10,8},{9,1... | collective-permute-start | bytes 2359304 | tf_op jit(solution)/shard_map/ppermute | solution.py:29
  4.5 5.0 %logits.1 = (f32[384,1536]{1,0:T(8,128)}, f32[1,1664]{1,0:T(1,128)}, f32[8,1,384]{2,1,0:T(1,128)}) custom-call(bf16[384,1024]{1,0:T(8,128)(2,1)} %t0.1, bf16[1536,1024]{1,0:T(8,128)(2,1)} %image_in.3), custom_call_target="tpu_custom_call" | custom-call | tf_op jit(solution)/shard_map/logits/pallas_call | solution.py:122
  9.5 6.1 %collective-permute-start.1 = (f32[1,1664]{1,0:T(1,128)}, f32[1,1664]{1,0:T(1,128)S(1)}, u32[]{:S(2)}, u32[]{:S(2)}) collective-permute-start(f32[1,1664]{1,0:T(1,128)} %get-tuple-element.25), channel_id=1, source_target_pairs={{0,24},{1,25},{4,28},{5,29},{8,16},{9,17},{12,20},{13,21},{16,8},{... | collective-permute-start | bytes 19976 | tf_op jit(solution)/shard_map/ppermute | solution.py:34
  15.6 4.1 %all-to-all-start = ((f32[8,1,384]{2,1,0:T(1,128)}), f32[8,1,384]{2,1,0:T(1,128)S(1)}, u32[]{:S(2)}, u32[]{:S(2)}) async-start(f32[8,1,384]{2,1,0:T(1,128)} %get-tuple-element.24), calls=%async_computation | async-start | bytes 24576 | tf_op jit(solution)/shard_map/all_to_all | solution.py:38
  19.8 0.7 %compare_select_fusion.row_ref = f32[1,1664]{1,0:T(1,128)S(1)} fusion(f32[1,1664]{1,0:T(1,128)S(1)} %collective-permute-done.1, f32[1,1664]{1,0:T(1,128)} %get-tuple-element.25), kind=kLoop, calls=%fused_computation.10 | loop fusion | flops 16640 | bytes 19968 | tf_op jit(solution)/shard_map/jit(_where)/select_n | solution.py:54
  20.5 0.8 %collective-permute-start.2 = (f32[1,1664]{1,0:T(1,128)S(1)}, f32[1,1664]{1,0:T(1,128)S(1)}, u32[]{:S(2)}, u32[]{:S(2)}) collective-permute-start(f32[1,1664]{1,0:T(1,128)S(1)} %compare_select_fusion.row_ref), channel_id=1, source_target_pairs={{0,4},{1,5},{4,0},{5,1},{8,12},{9,13},{12,8},{13,9},{16,20},{17,21... | collective-permute-start | bytes 19976 | tf_op jit(solution)/shard_map/ppermute | solution.py:34
  21.3 1.8 %collective-permute-start.3 = (bf16[384,1024]{1,0:T(8,128)(2,1)S(1)}, bf16[384,1024]{1,0:T(8,128)(2,1)S(1)}, u32[]{:S(2)}, u32[]{:S(2)}) collective-permute-start(bf16[384,1024]{1,0:T(8,128)(2,1)S(1)} %copy-done), channel_id=1, source_target_pairs={{0,1},{1,0},{2,3},{3,2},{4,5},{5,4},{6,7},{7,6},{8,9},{9,8},{10,11... | collective-permute-start | bytes 2359304 | tf_op jit(solution)/shard_map/ppermute | solution.py:29
  23.1 1.7 %all-to-all-done.got_ref = f32[8,1,384]{2,1,0:T(1,128)S(1)} async-done(((f32[8,1,384]{2,1,0:T(1,128)}), f32[8,1,384]{2,1,0:T(1,128)S(1)}, u32[]{:S(2)}, u32[]{:S(2)}) %all-to-all-start) | async-done | bytes 12320 | tf_op jit(solution)/shard_map/all_to_all | solution.py:38
  24.8 0.0 collective-permute-done.2.near_ref
  24.8 0.7 merge.1
  25.5 2.7 %collective-permute-start.4 = (bf16[384,1024]{1,0:T(8,128)(2,1)S(1)}, bf16[384,1024]{1,0:T(8,128)(2,1)}, u32[]{:S(2)}, u32[]{:S(2)}) collective-permute-start(bf16[384,1024]{1,0:T(8,128)(2,1)S(1)} %collective-permute-done.t2), channel_id=1, source_target_pairs={{0,1},{1,0},{2,3},{3,2},{4,5},{5,4},{6,7},{7,6},{8,9},{9,8},{10,11... | collective-permute-start | bytes 2359304 | tf_op jit(solution)/shard_map/ppermute | solution.py:29
  28.2 4.1 %all-to-all-start.1 = ((f32[8,1,2048]{2,1,0:T(1,128)}), f32[8,1,2048]{2,1,0:T(1,128)S(1)}, u32[]{:S(2)}, u32[]{:S(2)}) async-start(f32[8,1,2048]{2,1,0:T(1,128)} %merge.1), calls=%async_computation.1 | async-start | bytes 131072 | tf_op jit(solution)/shard_map/all_to_all | solution.py:38
  32.3 0.1 stack.35.at_ref
  32.4 0.0 collective-permute-done.3.t1
  32.4 6.6 %all-to-all-done.1.stat_in = f32[8,1,2048]{2,1,0:T(1,128)S(1)} async-done(((f32[8,1,2048]{2,1,0:T(1,128)}), f32[8,1,2048]{2,1,0:T(1,128)S(1)}, u32[]{:S(2)}, u32[]{:S(2)}) %all-to-all-start.1) | async-done | bytes 65568 | tf_op jit(solution)/shard_map/all_to_all | solution.py:38
  39.0 5.5 %image_part.1 = (bf16[2,48,1024]{2,1,0:T(8,128)(2,1)S(1)}, bf16[2,48,1024]{2,1,0:T(8,128)(2,1)S(1)}, f32[2,48,1024]{2,1,0:T(8,128)S(1)}, f32[48,1024]{1,0:T(8,12...) custom-call(s32[8]{0:T(128)S(1)} %stack.35.at_ref, f32[8,1,2048]{2,1,0:T(1,128)S(1)} %all-to-all-done.1.stat_in, ...), custom_call_target="tpu_custom_call" | custom-call | tf_op jit(solution)/shard_map/image_part/pallas_call | solution.py:287
  44.6 0.5 collective-permute-start.5
  45.1 2.0 %collective-permute-start.7 = (bf16[2,48,1024]{2,1,0:T(8,128)(2,1)S(1)}, bf16[2,48,1024]{2,1,0:T(8,128)(2,1)S(1)}, u32[]{:S(2)}, u32[]{:S(2)}) collective-permute-start(bf16[2,48,1024]{2,1,0:T(8,128)(2,1)S(1)} %get-tuple-element.35), channel_id=1, source_target_pairs={{0,4},{1,9},{4,0},{5,13},{8,12},{9,1},{12,8},{13,5},{16,20},{17,25... | collective-permute-start | bytes 589832 | tf_op jit(solution)/shard_map/ppermute | solution.py:34
  47.0 5.1 %text_part.1 = bf16[8,48,1024]{2,1,0:T(8,128)(2,1)} custom-call(s32[8]{0:T(128)S(1)} %stack.35.at_ref, f32[384,1536]{1,0:T(8,128)S(1)} %copy-done.1, f32[8,1,2048]{2,1,0:T(1,128)S(1)} %all-to-all-done.1.stat_in, s32[1,1536]{1,0:T(1,128)S(1)} %broadcast_in_dim.3.match_in, bf16[1536,1024]{1,0:T(8,128)(2,1)} %image_in.3, f32[1,128]{1,0:T(1,128)S(1)} %get-tuple-element.42.after_ref), custom_call_target="tpu_custom_call" | custom-call | tf_op jit(solution)/shard_map/text_part/pallas_call | solution.py:204
  52.1 0.0 collective-permute-done.5
  52.1 0.1 add_convert_fusion
  52.2 1.1 %collective-permute-start.9 = (f32[1,128]{1,0:T(1,128)S(1)}, f32[1,128]{1,0:T(1,128)S(1)}, u32[]{:S(2)}, u32[]{:S(2)}) collective-permute-start(f32[1,128]{1,0:T(1,128)S(1)} %get-tuple-element.42.after_ref), channel_id=1, source_target_pairs={{0,1},{1,0},{2,3},{3,2},{4,5},{5,4},{6,7},{7,6},{8,9},{9,8},{10,11... | collective-permute-start | bytes 1544 | tf_op jit(solution)/shard_map/ppermute | solution.py:29
  53.2 0.6 collective-permute-start.6
  53.9 0.2 collective-permute-done.9
  54.1 3.5 %all-to-all-start.2 = ((bf16[8,48,1024]{2,1,0:T(8,128)(2,1)}), bf16[8,48,1024]{2,1,0:T(8,128)(2,1)S(1)}, u32[]{:S(2)}, u32[]{:S(2)}) async-start(bf16[8,48,1024]{2,1,0:T(8,128)(2,1)} %text_part.1), calls=%async_computation.2 | async-start | bytes 1572864 | tf_op jit(solution)/shard_map/all_to_all | solution.py:38
  57.6 0.1 convert_add_fusion.2
  57.7 2.8 %collective-permute-done.6 = f16[2,48,1024]{2,1,0:T(8,128)(2,1)S(1)} collective-permute-done((f16[2,48,1024]{2,1,0:T(8,128)(2,1)S(1)}, f16[2,48,1024]{2,1,0:T(8,128)(2,1)S(1)}, u32[]{:S(2)}, u32[]{:S(2)}) %collective-permute-start.6) | collective-permute-done | bytes 196640 | tf_op jit(solution)/shard_map/ppermute | solution.py:34
  60.6 1.4 %collective-permute-start.8 = (f16[48,1024]{1,0:T(8,128)(2,1)S(1)}, f16[48,1024]{1,0:T(8,128)(2,1)S(1)}, u32[]{:S(2)}, u32[]{:S(2)}) collective-permute-start(f16[48,1024]{1,0:T(8,128)(2,1)S(1)} %get-tuple-element.47), channel_id=1, source_target_pairs={{0,24},{1,25},{4,28},{5,29},{8,16},{9,17},{12,20},{13,21},{16,8},{... | collective-permute-start | bytes 294920 | tf_op jit(solution)/shard_map/ppermute | solution.py:34
  62.0 4.6 %collective-permute-done.8 = f16[48,1024]{1,0:T(8,128)(2,1)S(1)} collective-permute-done((f16[48,1024]{1,0:T(8,128)(2,1)S(1)}, f16[48,1024]{1,0:T(8,128)(2,1)S(1)}, u32[]{:S(2)}, u32[]{:S(2)}) %collective-permute-start.8) | collective-permute-done | bytes 98336 | tf_op jit(solution)/shard_map/ppermute | solution.py:34
  66.5 0.7 %add_multiply_fusion = f32[48,1024]{1,0:T(8,128)} fusion(f32[48,1024]{1,0:T(8,128)S(1)} %get-tuple-element.40, f16[48,1024]{1,0:T(8,128)(2,1)S(1)} %collective-permute-done.8, f32[]{:T(128)S(1)} %bitcast.28), kind=kLoop, calls=%fused_computation.7 | loop fusion | flops 147456 | bytes 491524 | tf_op jit(solution)/shard_map/mul | solution.py:351
  67.3 3.4 %all-to-all-done.2 = bf16[8,48,1024]{2,1,0:T(8,128)(2,1)S(1)} async-done(((bf16[8,48,1024]{2,1,0:T(8,128)(2,1)}), bf16[8,48,1024]{2,1,0:T(8,128)(2,1)S(1)}, u32[]{:S(2)}, u32[]{:S(2)}) %all-to-all-start.2) | async-done | bytes 786464 | tf_op jit(solution)/shard_map/all_to_all | solution.py:38
  70.6 0.8 %convert_reduce_fusion = f32[48,1024]{1,0:T(8,128)} fusion(bf16[8,48,1024]{2,1,0:T(8,128)(2,1)S(1)} %all-to-all-done.2), kind=kLoop, calls=%fused_computation | loop fusion | flops 737280 | bytes 983040 | tf_op jit(solution)/shard_map/reduce_sum | solution.py:349
  (12 shorter events, 0.1 us)
Async XLA Ops:
  0.6 20.7 %copy-start = (bf16[384,1024]{1,0:T(8,128)(2,1)S(1)}, bf16[384,1024]{1,0:T(8,128)(2,1)}, u32[]{:S(2)}) copy-start(bf16[384,1024]{1,0:T(8,128)(2,1)} %t0.1) | copy-start | bytes 2359300
  0.6 31.6 %copy-start.2 = (s32[1536]{0:T(1024)S(1)}, s32[1536]{0:T(1024)}, u32[]{:S(2)}) copy-start(s32[1536]{0:T(1024)} %param.5) | copy-start | bytes 18436
  0.6 24.9 %collective-permute-start = (bf16[384,1024]{1,0:T(8,128)(2,1)}, bf16[384,1024]{1,0:T(8,128)(2,1)S(1)}, u32[]{:S(2)}, u32[]{:S(2)}) collective-permute-start(bf16[384,1024]{1,0:T(8,128)(2,1)} %t0.1), channel_id=1, source_target_pairs={{0,2},{2,0},{1,3},{3,1},{4,6},{6,4},{5,7},{7,5},{8,10},{10,8},{9,1... | collective-permute-start | bytes 2359304 | tf_op jit(solution)/shard_map/ppermute | solution.py:29
  9.5 10.3 %collective-permute-start.1 = (f32[1,1664]{1,0:T(1,128)}, f32[1,1664]{1,0:T(1,128)S(1)}, u32[]{:S(2)}, u32[]{:S(2)}) collective-permute-start(f32[1,1664]{1,0:T(1,128)} %get-tuple-element.25), channel_id=1, source_target_pairs={{0,24},{1,25},{4,28},{5,29},{8,16},{9,17},{12,20},{13,21},{16,8},{... | collective-permute-start | bytes 19976 | tf_op jit(solution)/shard_map/ppermute | solution.py:34
  15.6 9.2 %all-to-all-start = ((f32[8,1,384]{2,1,0:T(1,128)}), f32[8,1,384]{2,1,0:T(1,128)S(1)}, u32[]{:S(2)}, u32[]{:S(2)}) async-start(f32[8,1,384]{2,1,0:T(1,128)} %get-tuple-element.24), calls=%async_computation | async-start | bytes 24576 | tf_op jit(solution)/shard_map/all_to_all | solution.py:38
  20.5 4.3 %collective-permute-start.2 = (f32[1,1664]{1,0:T(1,128)S(1)}, f32[1,1664]{1,0:T(1,128)S(1)}, u32[]{:S(2)}, u32[]{:S(2)}) collective-permute-start(f32[1,1664]{1,0:T(1,128)S(1)} %compare_select_fusion.row_ref), channel_id=1, source_target_pairs={{0,4},{1,5},{4,0},{5,1},{8,12},{9,13},{12,8},{13,9},{16,20},{17,21... | collective-permute-start | bytes 19976 | tf_op jit(solution)/shard_map/ppermute | solution.py:34
  21.3 11.1 %collective-permute-start.3 = (bf16[384,1024]{1,0:T(8,128)(2,1)S(1)}, bf16[384,1024]{1,0:T(8,128)(2,1)S(1)}, u32[]{:S(2)}, u32[]{:S(2)}) collective-permute-start(bf16[384,1024]{1,0:T(8,128)(2,1)S(1)} %copy-done), channel_id=1, source_target_pairs={{0,1},{1,0},{2,3},{3,2},{4,5},{5,4},{6,7},{7,6},{8,9},{9,8},{10,11... | collective-permute-start | bytes 2359304 | tf_op jit(solution)/shard_map/ppermute | solution.py:29
  25.5 13.5 %collective-permute-start.4 = (bf16[384,1024]{1,0:T(8,128)(2,1)S(1)}, bf16[384,1024]{1,0:T(8,128)(2,1)}, u32[]{:S(2)}, u32[]{:S(2)}) collective-permute-start(bf16[384,1024]{1,0:T(8,128)(2,1)S(1)} %collective-permute-done.t2), channel_id=1, source_target_pairs={{0,1},{1,0},{2,3},{3,2},{4,5},{5,4},{6,7},{7,6},{8,9},{9,8},{10,11... | collective-permute-start | bytes 2359304 | tf_op jit(solution)/shard_map/ppermute | solution.py:29
  28.2 10.8 %all-to-all-start.1 = ((f32[8,1,2048]{2,1,0:T(1,128)}), f32[8,1,2048]{2,1,0:T(1,128)S(1)}, u32[]{:S(2)}, u32[]{:S(2)}) async-start(f32[8,1,2048]{2,1,0:T(1,128)} %merge.1), calls=%async_computation.1 | async-start | bytes 131072 | tf_op jit(solution)/shard_map/all_to_all | solution.py:38
  39.0 8.0 %copy-start.1 = (f32[384,1536]{1,0:T(8,128)S(1)}, f32[384,1536]{1,0:T(8,128)}, u32[]{:S(2)}) copy-start(f32[384,1536]{1,0:T(8,128)} %get-tuple-element.30.logits_in) | copy-start | bytes 7077892
  44.6 7.5 %collective-permute-start.5 = (bf16[2,48,1024]{2,1,0:T(8,128)(2,1)S(1)}, bf16[2,48,1024]{2,1,0:T(8,128)(2,1)S(1)}, u32[]{:S(2)}, u32[]{:S(2)}) collective-permute-start(bf16[2,48,1024]{2,1,0:T(8,128)(2,1)S(1)} %get-tuple-element.29), channel_id=1, source_target_pairs={{0,4},{1,9},{4,0},{5,13},{8,12},{9,1},{12,8},{13,5},{16,20},{17,25... | collective-permute-start | bytes 589832 | tf_op jit(solution)/shard_map/ppermute | solution.py:34
  45.1 12.6 %collective-permute-start.7 = (bf16[2,48,1024]{2,1,0:T(8,128)(2,1)S(1)}, bf16[2,48,1024]{2,1,0:T(8,128)(2,1)S(1)}, u32[]{:S(2)}, u32[]{:S(2)}) collective-permute-start(bf16[2,48,1024]{2,1,0:T(8,128)(2,1)S(1)} %get-tuple-element.35), channel_id=1, source_target_pairs={{0,4},{1,9},{4,0},{5,13},{8,12},{9,1},{12,8},{13,5},{16,20},{17,25... | collective-permute-start | bytes 589832 | tf_op jit(solution)/shard_map/ppermute | solution.py:34
  52.2 1.9 %collective-permute-start.9 = (f32[1,128]{1,0:T(1,128)S(1)}, f32[1,128]{1,0:T(1,128)S(1)}, u32[]{:S(2)}, u32[]{:S(2)}) collective-permute-start(f32[1,128]{1,0:T(1,128)S(1)} %get-tuple-element.42.after_ref), channel_id=1, source_target_pairs={{0,1},{1,0},{2,3},{3,2},{4,5},{5,4},{6,7},{7,6},{8,9},{9,8},{10,11... | collective-permute-start | bytes 1544 | tf_op jit(solution)/shard_map/ppermute | solution.py:29
  53.2 7.3 %collective-permute-start.6 = (f16[2,48,1024]{2,1,0:T(8,128)(2,1)S(1)}, f16[2,48,1024]{2,1,0:T(8,128)(2,1)S(1)}, u32[]{:S(2)}, u32[]{:S(2)}) collective-permute-start(f16[2,48,1024]{2,1,0:T(8,128)(2,1)S(1)} %add_convert_fusion), channel_id=1, source_target_pairs={{0,8},{1,5},{4,12},{5,1},{8,0},{9,13},{12,4},{13,9},{16,24},{17,21... | collective-permute-start | bytes 589832 | tf_op jit(solution)/shard_map/ppermute | solution.py:34
  54.1 16.6 %all-to-all-start.2 = ((bf16[8,48,1024]{2,1,0:T(8,128)(2,1)}), bf16[8,48,1024]{2,1,0:T(8,128)(2,1)S(1)}, u32[]{:S(2)}, u32[]{:S(2)}) async-start(bf16[8,48,1024]{2,1,0:T(8,128)(2,1)} %text_part.1), calls=%async_computation.2 | async-start | bytes 1572864 | tf_op jit(solution)/shard_map/all_to_all | solution.py:38
  60.6 6.0 %collective-permute-start.8 = (f16[48,1024]{1,0:T(8,128)(2,1)S(1)}, f16[48,1024]{1,0:T(8,128)(2,1)S(1)}, u32[]{:S(2)}, u32[]{:S(2)}) collective-permute-start(f16[48,1024]{1,0:T(8,128)(2,1)S(1)} %get-tuple-element.47), channel_id=1, source_target_pairs={{0,24},{1,25},{4,28},{5,29},{8,16},{9,17},{12,20},{13,21},{16,8},{... | collective-permute-start | bytes 294920 | tf_op jit(solution)/shard_map/ppermute | solution.py:34
